TPU v7x, 32 devices: a whole 2x2x4 slice. The times are simulated.
32 devices in a mesh: pack: 2 (over x), seq: 16 (over z, y, core).
Axes of the slice: x: 2, y: 2, z: 4, core: 2. Of those that a mesh axis runs over, the one named last changes fastest.
Arguments:
- queries: bfloat16 [4096, 2048], P(('pack', 'seq')), parts along dimension 0, may hold values from -48 to 48
- token_key_heads: bfloat16 [4096, 256], P(('pack', 'seq')), parts along dimension 0, may hold values from -6 to 6
- token_value_heads: bfloat16 [4096, 256], P(('pack', 'seq')), parts along dimension 0, may hold values from -6 to 6
- residual: bfloat16 [4096, 1024], P(('pack', 'seq')), parts along dimension 0, may hold values from -40 to 40
- out_weight: bfloat16 [2048, 1024], P('seq'), may hold values from -0.125 to 0.125
- norm_gain: bfloat16 [1024], replicated, may hold values from 0.5 to 1.5
- w_gate: bfloat16 [16, 1024, 384], P('seq'), may hold values from -0.1875 to 0.1875
- w_up: bfloat16 [16, 1024, 384], P('seq'), may hold values from -0.1875 to 0.1875
- w_down: bfloat16 [16, 384, 1024], P('seq'), may hold values from -0.3125 to 0.3125
- expert_ids: int32 [4096, 8], P(('pack', 'seq')), parts along dimension 0, may hold values from 0 to 15, all different within a row; in each aligned block of 128 rows (0 to 127, 128 to 255, ...) at most 96 rows name the same one
- gate_weights: float32 [4096, 8], P(('pack', 'seq')), parts along dimension 0, may hold values from 0.05 to 0.3
- doc_of_block: int32 [32], P('pack'), parts along dimension 0, may hold values from 0 to 3, never falling along the last dimension, each value on 1 to 8 neighbouring positions
Outputs:
- attention: bfloat16 [4096, 2048], P(('pack', 'seq')), parts along dimension 0
- hidden_out: bfloat16 [4096, 1024], P(('pack', 'seq')), parts along dimension 0
- expert_mix: bfloat16 [4096, 1024], P(('pack', 'seq')), parts along dimension 0
There are 2 independent parts, one for each index of `pack`. A program takes and returns all parts, laid end to end along the dimension named above; an argument that names none is the same for every part. Nothing has to cross between parts.
Inputs may be any that keep to these rules, and one draw needn't show every extreme that they name: `expert_ids`: each row names 8 different experts; within the rows of one block no expert is named more than 96 times, and in every draw some expert is named exactly 96 times by the rows of some block. `doc_of_block`: never falls from block to block; each document covers 1 to 8 blocks, one exactly 8.
All inputs are finite; a program needn't handle non-finite values.
Results may differ from a plain program's by a relative error of at most 0.015.
Values may be sent and summed in bfloat16 or wider, within the bound.
No kernel may reach another device: no remote copies, remote signals or barrier semaphores. Data moves between devices by JAX's collectives and lax.ppermute only.
A program may use at most 64 MiB of HBM per device.

v0:
```python
import math

import jax
import jax.numpy as jnp
from jax import lax
from jax.sharding import PartitionSpec as P

QUERY_HEADS = 16
KEY_VALUE_HEADS = 2
HEAD_SIZE = 128
TOP = 8


def attend(queries, key_token_rows, value_token_rows, query_pos, key_pos, allowed):
    token_rows = queries.shape[0]
    heads_per_group = QUERY_HEADS // KEY_VALUE_HEADS
    token_query_heads = queries.reshape(token_rows, KEY_VALUE_HEADS, heads_per_group, HEAD_SIZE)
    key_count = key_token_rows.shape[0]
    tile_length = math.gcd(key_count, 512)
    number_of_tiles = key_count // tile_length
    key_tile_list = key_token_rows.reshape(number_of_tiles, tile_length, KEY_VALUE_HEADS, HEAD_SIZE)
    value_tile_list = value_token_rows.reshape(
        number_of_tiles, tile_length, KEY_VALUE_HEADS, HEAD_SIZE
    )
    pos_tiles = key_pos.reshape(number_of_tiles, tile_length)
    allowed_tiles = allowed.reshape(number_of_tiles, tile_length)
    factor = 1.0 / HEAD_SIZE**0.5

    def tile_step(running, tile):
        key_tile, value_tile, pos_tile, allowed_tile = tile
        visible = allowed_tile[None, :] & (pos_tile[None, :] <= query_pos[:, None])

        def compute(current):
            run_max, run_sum, accum = current
            scores = (
                jnp.einsum(
                    "tkgd,skd->kgts",
                    token_query_heads,
                    key_tile,
                    preferred_element_type=jnp.float32,
                )
                * factor
            )
            scores = jnp.where(visible, scores, -1e30)
            new_max = jnp.maximum(run_max, jnp.max(scores, axis=-1))
            terms = jnp.where(visible, jnp.exp(scores - new_max[..., None]), 0.0)
            rescale = jnp.exp(run_max - new_max)
            new_sum = run_sum * rescale + jnp.sum(terms, axis=-1)
            product = jnp.einsum(
                "kgts,skd->kgtd",
                terms.astype(jnp.bfloat16),
                value_tile,
                preferred_element_type=jnp.float32,
            )
            return (new_max, new_sum, accum * rescale[..., None] + product)

        return (lax.cond(jnp.any(visible), compute, lambda current: current, running), None)

    start_state = (
        jnp.full((KEY_VALUE_HEADS, heads_per_group, token_rows), -1e30, jnp.float32),
        jnp.zeros((KEY_VALUE_HEADS, heads_per_group, token_rows), jnp.float32),
        jnp.zeros((KEY_VALUE_HEADS, heads_per_group, token_rows, HEAD_SIZE), jnp.float32),
    )
    final_state, _ = lax.scan(
        tile_step, start_state, (key_tile_list, value_tile_list, pos_tiles, allowed_tiles)
    )
    run_max, run_sum, accum = final_state
    result = accum / run_sum[..., None]
    return (
        jnp.transpose(result, (2, 0, 1, 3))
        .reshape(token_rows, QUERY_HEADS * HEAD_SIZE)
        .astype(jnp.bfloat16)
    )


def expert_rows(arrived, gate_proj, up_proj, down_proj):
    sources, slot_count, width = arrived.shape
    flat_rows = arrived.reshape(sources * slot_count, width)
    gate_part = jnp.dot(flat_rows, gate_proj, preferred_element_type=jnp.float32)
    up_part = jnp.dot(flat_rows, up_proj, preferred_element_type=jnp.float32)
    activated = (jax.nn.silu(gate_part) * up_part).astype(jnp.bfloat16)
    produced = jnp.dot(activated, down_proj, preferred_element_type=jnp.float32).astype(
        jnp.bfloat16
    )
    return produced.reshape(sources, slot_count, width)


def shards(
    queries,
    token_key_heads,
    token_value_heads,
    residual,
    out_weight,
    norm_gain,
    w_gate,
    w_up,
    w_down,
    expert_ids,
    gate_weights,
    doc_of_block,
):
    token_rows = queries.shape[0]
    blocks = lax.axis_size("seq")
    own_index = lax.axis_index("seq")
    local_pos = jnp.arange(token_rows, dtype=jnp.int32)
    query_pos = own_index * token_rows + local_pos
    own_doc = doc_of_block[own_index]
    key_head_width = token_key_heads.shape[1]
    key_token_rows, value_token_rows = (
        lax.all_gather(token_key_heads, "seq", axis=0, tiled=True),
        lax.all_gather(token_value_heads, "seq", axis=0, tiled=True),
    )
    key_pos = jnp.arange(blocks * token_rows, dtype=jnp.int32)
    key_block = key_pos // token_rows
    allowed = (key_block <= own_index) & ((doc_of_block[key_block] == own_doc) | (key_block == 0))
    key_token_rows = key_token_rows.reshape(
        key_token_rows.shape[0], KEY_VALUE_HEADS, key_head_width // KEY_VALUE_HEADS
    )
    value_token_rows = value_token_rows.reshape(
        value_token_rows.shape[0], KEY_VALUE_HEADS, key_head_width // KEY_VALUE_HEADS
    )
    attention = attend(queries, key_token_rows, value_token_rows, query_pos, key_pos, allowed)
    width = residual.shape[1]
    projected = jnp.dot(
        attention,
        lax.all_gather(out_weight, "seq", axis=0, tiled=True),
        preferred_element_type=jnp.float32,
    )
    hidden_state = residual.astype(jnp.float32) + projected
    mean_square = jnp.mean(hidden_state * hidden_state, axis=-1, keepdims=True)
    normed = (hidden_state * lax.rsqrt(mean_square + 1e-06) * norm_gain.astype(jnp.float32)).astype(
        jnp.bfloat16
    )
    slot_cap = min(token_rows, 3 * token_rows * TOP // (2 * blocks))
    routed_ids = expert_ids.reshape(-1)
    one_hot = (routed_ids[:, None] == jnp.arange(blocks, dtype=jnp.int32)[None, :]).astype(
        jnp.int32
    )
    earlier = jnp.cumsum(one_hot, axis=0) - one_hot
    slot_pos = jnp.sum(earlier * one_hot, axis=1)
    slot_index = routed_ids * slot_cap + slot_pos
    token_of = jnp.arange(token_rows * TOP, dtype=jnp.int32) // TOP
    outgoing = (
        jnp.zeros((blocks * slot_cap, width), jnp.bfloat16).at[slot_index].set(normed[token_of])
    )
    outgoing = outgoing.reshape(blocks, slot_cap, width)
    arrived = lax.all_to_all(outgoing, "seq", split_axis=0, concat_axis=0, tiled=True)
    served = expert_rows(arrived, w_gate[0], w_up[0], w_down[0])
    returned_rows = lax.all_to_all(served, "seq", split_axis=0, concat_axis=0, tiled=True)
    picked = returned_rows.reshape(blocks * slot_cap, width)[slot_index].astype(jnp.float32)
    weighted = picked * gate_weights.reshape(-1)[:, None]
    expert_mix = jnp.sum(weighted.reshape(token_rows, TOP, width), axis=1).astype(jnp.bfloat16)
    return (attention, hidden_state.astype(jnp.bfloat16), expert_mix)


def solution(mesh):
    in_specs = (
        P(("pack", "seq"), None),
        P(("pack", "seq"), None),
        P(("pack", "seq"), None),
        P(("pack", "seq"), None),
        P("seq", None),
        P(),
        P("seq", None, None),
        P("seq", None, None),
        P("seq", None, None),
        P(("pack", "seq"), None),
        P(("pack", "seq"), None),
        P("pack"),
    )
    out_specs = (P(("pack", "seq"), None), P(("pack", "seq"), None), P(("pack", "seq"), None))
    return jax.shard_map(shards, mesh=mesh, in_specs=in_specs, out_specs=out_specs, check_vma=False)
```

profile of v0, /device:TPU:13, one launch (start us, length us, event | category | flops | bytes accessed | tf_op | source)
XLA Modules:
  0.0 337.1 jit_solution(16530568674873345470)
XLA Ops:
  10.8 2.0 fusion.41
  12.8 4.3 %compare_select_fusion.1 = s32[2048,1]{0,1:T(1,128)S(1)} fusion(s32[]{:T(128)} %bitcast.16, s32[]{:T(128)} %bitcast.17, s32[]{:T(128)} %bitcast.18, s32[]{:T(128)} %bitcast.19, s32[]{:T(128)} %bitcast.20, s32[]{:T(128)} %bitcast.22, s32[]{:T(128)} %bitcast.21), kind=kLoop, calls=%fused_computation.66 | loop fusion | flops 47104 | bytes 8220 | tf_op jit(solution)/shard_map/gather | solution.py:115
  17.1 6.4 %select_compare_fusion = pred[2048]{0:T(1024)(128)(4,1)S(1)} fusion(pred[2048]{0:T(1024)(128)(4,1)S(1)} %compare_reduce_fusion, pred[2048]{0:T(1024)(128)(4,1)S(1)} %compare_reduce_fusion.1, pred[2048]{0:T(1024)(128)(4,1)S(1)} %compare_reduce_fusion.2, pred[2048]{0:T(1024)(128)(4,1)S(1)} %compare_reduce_fusion.3, ...), kind=kLoop, calls=%fused_computation.84 | loop fusion | flops 20480 | bytes 28712 | tf_op jit(solution)/shard_map/eq | solution.py:115
  23.5 1.3 copy.21
  26.7 4.5 %reduce-window.6 = s32[16,8,128]{2,1,0:T(8,128)S(1)} reduce-window(s32[16,8,128]{2,1,0:T(8,128)S(1)} %fusion.37, s32[]{:T(128)} %copy.58), window={size=1x1x128 pad=0_0x0_0x127_0}, to_apply=%region_7.8 | reduce-window | flops 2080768 | bytes 131076 | tf_op jit(solution)/shard_map/reduce-window
  31.7 16.8 %all-gather.4.cloned.1.call-done = bf16[2048,256]{1,0:T(8,128)(2,1)} async-done(((bf16[128,256]{1,0:T(8,128)(2,1)}), bf16[2048,256]{1,0:T(8,128)(2,1)}) %all-gather.4.cloned.1.call-update) | async-done | bytes 1048592 | tf_op jit(solution)/shard_map/all_gather | solution.py:110
  48.5 1.3 reshape_reshape.6
  50.0 37.6 %all-gather.6.cloned.1.call-done = bf16[2048,256]{1,0:T(8,128)(2,1)} async-done(((bf16[128,256]{1,0:T(8,128)(2,1)}), bf16[2048,256]{1,0:T(8,128)(2,1)}) %all-gather.6.cloned.1.call-update) | async-done | bytes 1048592 | tf_op jit(solution)/shard_map/all_gather | solution.py:111
  87.6 1.3 reshape_reshape.7
  88.9 1.1 copy.24
  90.1 15.3 %while.15 = (s32[]{:T(128)}, f32[2,8,128]{2,1,0:T(8,128)S(1)}, f32[2,8,128]{2,1,0:T(8,128)S(1)}, f32[2,8,128,128]{3,2,1,0:T(8,128)S(1)}, pred[4,512]{1,0:T(4,128...) while((s32[]{:T(128)}, f32[2,8,128]{2,1,0:T(8,128)S(1)}, ...), condition=%wide.region_6.7_spmd.clone, body=%wide.region_0.6_spmd.clone.sunk | while | flops 551227520 | bytes 16131331 | solution.py:64
  90.2 0.9 compare_and_fusion.2
  91.7 4.5 %conditional.3 = ((f32[2,8,128]{2,1,0:T(8,128)S(1)}, f32[2,8,128]{2,1,0:T(8,128)S(1)}, f32[2,8,128,128]{3,2,1,0:T(8,128)S(1)})) conditional(s32[]{:T(128)} %convert_element_type.85, (f32[2,8,128]{2,1,0:T(8,128)S(1)}, f32[2,8,128]{2,1,0:T(8,128)S(1)}, f32[2,8,128,128]{3,2,1,0:T(8,128)S(1)}) %tuple.64, (pred[128,512]{0,1:T(8,128)(4,1)S(1)}, ...), branch_computations={%region_2.2_spmd, %region_3.5_spmd} | conditional | flops 551030784 | bytes 16056868 | solution.py:57
  92.5 1.0 fusion.4
  93.5 2.7 fusion.8
  96.2 0.9 compare_and_fusion.2
  97.7 4.5 %conditional.3 = ((f32[2,8,128]{2,1,0:T(8,128)S(1)}, f32[2,8,128]{2,1,0:T(8,128)S(1)}, f32[2,8,128,128]{3,2,1,0:T(8,128)S(1)})) conditional(s32[]{:T(128)} %convert_element_type.85, (f32[2,8,128]{2,1,0:T(8,128)S(1)}, f32[2,8,128]{2,1,0:T(8,128)S(1)}, f32[2,8,128,128]{3,2,1,0:T(8,128)S(1)}) %tuple.64, (pred[128,512]{0,1:T(8,128)(4,1)S(1)}, ...), branch_computations={%region_2.2_spmd, %region_3.5_spmd} | conditional | flops 551030784 | bytes 16056868 | solution.py:57
  98.5 1.0 fusion.4
  99.5 2.6 fusion.8
  102.3 0.9 compare_and_fusion.2
  103.9 0.9 compare_and_fusion.2
  106.3 33.4 %all-gather.8.cloned.1.call-done = bf16[2048,1024]{1,0:T(8,128)(2,1)} async-done(((bf16[128,1024]{1,0:T(8,128)(2,1)}), bf16[2048,1024]{1,0:T(8,128)(2,1)}) %all-gather.8.cloned.1.call-update) | async-done | bytes 4194320 | tf_op jit(solution)/shard_map/all_gather | solution.py:126
  139.7 3.0 multiply_reduce_fusion
  143.5 14.9 %scatter_custom_fusion = bf16[1536,1024]{1,0:T(8,128)(2,1)} fusion(s32[1024]{0:T(1024)S(1)} %bitcast.112, bf16[128,1024]{1,0:T(8,128)(2,1)S(1)} %get-tuple-element.196, s32[1024]{0:T(1024)S(1)} %broadcast_clamp_fusion.1, bf16[]{:T(256)} %constant.107.clone.1), kind=kCustom, calls=%fused_computation.34 | custom fusion | bytes 3145730 | tf_op jit(solution)/shard_map/scatter | solution.py:144
  158.4 74.8 %all_to_all.10 = bf16[16,96,1024]{2,1,0:T(8,128)(2,1)S(1)} all-to-all(bf16[16,96,1024]{2,1,0:T(8,128)(2,1)} %bitcast.99), channel_id=1, replica_groups=mesh['pack'=2,'seq'=16] {'seq'}, dimensions={0} | all-to-all | bytes 6291456 | tf_op jit(solution)/shard_map/all_to_all | solution.py:147
  233.2 1.7 copy-done.1
  234.9 3.3 fusion.31
  238.2 7.8 %convolution_convert_fusion = bf16[1536,1024]{1,0:T(8,128)(2,1)} fusion(bf16[1536,1024]{1,0:T(8,128)(2,1)} %bitcast.102, f32[1536,384]{1,0:T(8,128)} %fusion.31, bf16[1,384,1024]{2,1,0:T(8,128)(2,1)S(1)} %copy-done, bf16[1,1024,384]{2,1,0:T(8,128)(2,1)S(1)} %copy-done.6), kind=kOutput, calls=%fused_computation.31 | convolution fusion | flops 2421030912 | bytes 10223616 | tf_op jit(solution)/shard_map/dot_general | solution.py:82
  246.0 5.3 %all-to-all-start.1 = ((bf16[16,96,1024]{2,1,0:T(8,128)(2,1)}), bf16[16,96,1024]{2,1,0:T(8,128)(2,1)}, u32[]{:S(2)}, u32[]{:S(2)}) async-start(bf16[16,96,1024]{2,1,0:T(8,128)(2,1)} %bitcast.100), calls=%async_computation.1 | async-start | bytes 6291456 | tf_op jit(solution)/shard_map/all_to_all | solution.py:149
  251.4 69.9 %all-to-all-done.1 = bf16[16,96,1024]{2,1,0:T(8,128)(2,1)} async-done(((bf16[16,96,1024]{2,1,0:T(8,128)(2,1)}), bf16[16,96,1024]{2,1,0:T(8,128)(2,1)}, u32[]{:S(2)}, u32[]{:S(2)}) %all-to-all-start.1) | async-done | bytes 3145760 | tf_op jit(solution)/shard_map/all_to_all | solution.py:149
  321.3 7.3 %gather_fusion = bf16[1024,1024]{1,0:T(8,128)(2,1)S(1)} fusion(bf16[1536,1024]{1,0:T(8,128)(2,1)} %bitcast.38, s32[1024]{0:T(1024)S(1)} %broadcast_clamp_fusion), kind=kCustom, calls=%fused_computation.1 | custom fusion | bytes 4198400 | tf_op jit(solution)/shard_map/gather | solution.py:150
  328.6 2.0 fusion.22
  (83 shorter events, 9.6 us)
Async XLA Ops:
  7.2 231.0 %copy-start = (bf16[1,384,1024]{2,1,0:T(8,128)(2,1)S(1)}, bf16[1,384,1024]{2,1,0:T(8,128)(2,1)}, u32[]{:S(2)}) copy-start(bf16[1,384,1024]{2,1,0:T(8,128)(2,1)} %param.24) | copy-start | bytes 2359300
  7.2 41.3 %all-gather.4.cloned.1.call-start = ((), (), s32[]{:S(2)}) async-start(), calls=%async_computation.2 | async-start | bytes 1114112 | tf_op jit(solution)/shard_map/all_gather | solution.py:110
  7.9 79.6 %all-gather.6.cloned.1.call-start = ((), (), s32[]{:S(2)}) async-start(), calls=%async_computation.3 | async-start | bytes 1114112 | tf_op jit(solution)/shard_map/all_gather | solution.py:111
  8.7 131.0 %all-gather.8.cloned.1.call-start = ((), (), s32[]{:S(2)}) async-start(), calls=%async_computation.4 | async-start | bytes 4456448 | tf_op jit(solution)/shard_map/all_gather | solution.py:126
  105.4 34.3 %copy-start.3 = (bf16[128,1024]{1,0:T(8,128)(2,1)S(1)}, bf16[128,1024]{1,0:T(8,128)(2,1)}, u32[]{:S(2)}) copy-start(bf16[128,1024]{1,0:T(8,128)(2,1)} %param.19) | copy-start | bytes 786436
  106.3 37.2 %copy-start.2 = (bf16[16,8,16,128]{3,1,2,0:T(8,128)(2,1)}, bf16[16,8,16,128]{3,1,2,0:T(8,128)(2,1)S(1)}, u32[]{:S(2)}) copy-start(bf16[16,8,16,128]{3,1,2,0:T(8,128)(2,1)S(1)} %copy.39) | copy-start | bytes 1572868
  158.4 76.5 %copy-start.5 = (bf16[1,1024,384]{2,1,0:T(8,128)(2,1)S(1)}, bf16[1,1024,384]{2,1,0:T(8,128)(2,1)}, u32[]{:S(2)}) copy-start(bf16[1,1024,384]{2,1,0:T(8,128)(2,1)} %param.22) | copy-start | bytes 2359300
  233.2 1.7 copy-start.1
  234.9 3.3 copy-start.6
  246.0 5.3 %copy-start.4 = (f32[128,8]{0,1:T(8,128)S(1)}, f32[128,8]{0,1:T(8,128)}, u32[]{:S(2)}) copy-start(f32[128,8]{0,1:T(8,128)} %param.26) | copy-start | bytes 12292
  246.0 75.3 %all-to-all-start.1 = ((bf16[16,96,1024]{2,1,0:T(8,128)(2,1)}), bf16[16,96,1024]{2,1,0:T(8,128)(2,1)}, u32[]{:S(2)}, u32[]{:S(2)}) async-start(bf16[16,96,1024]{2,1,0:T(8,128)(2,1)} %bitcast.100), calls=%async_computation.1 | async-start | bytes 6291456 | tf_op jit(solution)/shard_map/all_to_all | solution.py:149
Sparse Core Ops, SparseCore 0:
  10.2 38.2 all-gather.3
  50.7 36.8 all-gather.5
  89.7 49.9 all-gather.7
where the time goes:
time: 338 us; the launch traced here: 337 us
  waiting for transfers between devices  160 us (47%)
  blocking collectives  74.8 us (22%)
  local copies, waits for them, and re-layouts  33.8 us (10%)
  other arithmetic  25.8 us (8%)
  matrix products  20.8 us (6%)
  between operations  14 us (4%)
  starting transfers between devices  5.46 us (2%)
    all_to_all x1, blocking collectives, shards(): lax.all_to_all(outgoing, 'seq', split_axis=0, concat_axis=0, tiled=True)  74.8 us
    all_to_all x1, waiting for transfers between devices, shards(): lax.all_to_all(served, 'seq', split_axis=0, concat_axis=0, tiled=True)  69.9 us
    all_gather x1, waiting for transfers between devices, shards(): lax.all_gather(token_value_heads, 'seq', axis=0, tiled=True)  37.6 us
    all_gather x1, waiting for transfers between devices, shards(): lax.all_gather(out_weight, 'seq', axis=0, tiled=True)  33.4 us
    all_gather x1, waiting for transfers between devices, shards(): lax.all_gather(token_key_heads, 'seq', axis=0, tiled=True)  16.8 us
    scatter x1, local copies, waits for them, and re-layouts, shards(): jnp.zeros((blocks * slot_cap, width), jnp.bfloat16).at[slot_index]  14.9 us
    dot_general x1, matrix products, expert_rows(): jnp.dot(activated, down_proj, preferred_element_type=jnp.float32)  7.78 us
    gather x1, local copies, waits for them, and re-layouts, shards(): returned_rows.reshape(blocks * slot_cap, width)[slot_index]  7.27 us
  transfers between devices with their start and end apart: 4, of which 4 were waited for; matrix products, arithmetic and copies ran while one was open for 12% of the time, Pallas kernels for 0%

commit v1 on v0

v1 whole, which is shorter than its diff:
```python
import functools
import math

import jax
import jax.numpy as jnp
from jax import lax
from jax.experimental import pallas as pl
from jax.experimental.pallas import tpu as pltpu
from jax.sharding import PartitionSpec as P

QUERY_HEADS = 16
KEY_VALUE_HEADS = 2
HEAD_SIZE = 128
MOST_BLK = 8
GROUP = QUERY_HEADS // KEY_VALUE_HEADS
F32 = jnp.float32
BF16 = jnp.bfloat16
VMEM_LIMIT = 48 * 1024 * 1024


def chip_at(place, chips):
    half = chips // 2
    return jnp.where(place < half, 2 * place, 2 * (chips - 1 - place) + 1)


def place_of(chip, chips):
    return jnp.where(chip % 2 == 0, chip // 2, chips - 1 - chip // 2)


def ring_steps(chips):
    order = [2 * i for i in range(chips // 2)] + [2 * i + 1 for i in reversed(range(chips // 2))]
    forward = [
        (2 * order[i] + k, 2 * order[(i + 1) % chips] + k) for i in range(chips) for k in range(2)
    ]
    return forward, [(b, a) for a, b in forward]


def core_step(devices):
    return [(i, i ^ 1) for i in range(devices)]


def piece_places(chips):
    places = [0]
    for j in range(1, chips // 2):
        places += [-j, j]
    return places + [chips // 2]


def ring_gather(piece, devices):
    chips = devices // 2
    forward, backward = ring_steps(chips)
    rows = piece.shape[0]
    cut = rows // 2 // 16 * 16
    pieces = {0: piece}
    ahead = behind = piece
    for j in range(1, chips // 2):
        ahead = lax.ppermute(ahead, "seq", forward)
        behind = lax.ppermute(behind, "seq", backward)
        pieces[-j], pieces[j] = ahead, behind
    far = (
        lax.ppermute(ahead[:cut], "seq", forward),
        lax.ppermute(behind[cut:], "seq", backward),
    )
    return pieces, far


def gather_all(piece, devices):
    chips = devices // 2
    pieces, far = ring_gather(piece, devices)
    pieces[chips // 2] = jnp.concatenate(far, axis=0)
    swap = core_step(devices)
    return [(pieces[d], lax.ppermute(pieces[d], "seq", swap)) for d in piece_places(chips)]


def block_of(own, offset, other, devices):
    chips = devices // 2
    place = (place_of(own // 2, chips) + offset + chips) % chips
    return chip_at(place, chips) * 2 + (own % 2 if other == 0 else 1 - own % 2)


def attend_kernel(offsets, devices, own_ref, doc_ref, q_ref, *refs):
    count = 2 * len(offsets)
    kv_refs = refs[:count]
    out_ref, keys, values, bias = refs[count:]
    rows = q_ref.shape[0]
    width = KEY_VALUE_HEADS * HEAD_SIZE
    window = keys.shape[1]
    own = own_ref[0]
    own_doc = doc_ref[own]
    lane = lax.broadcasted_iota(jnp.int32, (window, HEAD_SIZE), 1)
    one_column = jnp.where(lane == 0, 1.0, 0.0).astype(BF16)
    for g in range(KEY_VALUE_HEADS):
        keys[g] = jnp.zeros((window, HEAD_SIZE), BF16)
        values[g, :, :HEAD_SIZE] = jnp.zeros((window, HEAD_SIZE), BF16)
        values[g, :, HEAD_SIZE:] = one_column

    def put(ref, slot):
        start = pl.multiple_of(slot * rows, rows)
        for g in range(KEY_VALUE_HEADS):
            keys[g, pl.ds(start, rows), :] = ref[:rows, g * HEAD_SIZE : (g + 1) * HEAD_SIZE]
            values[g, pl.ds(start, rows), :HEAD_SIZE] = ref[
                :rows, width + g * HEAD_SIZE : width + (g + 1) * HEAD_SIZE
            ]

    put(kv_refs[0], 0)
    slot = jnp.int32(1)
    for i in range(1, count):
        block = block_of(own, offsets[i // 2], i % 2, devices)
        seen = (block < own) & ((block == 0) | (doc_ref[block] == own_doc))
        pl.when(seen)(functools.partial(put, kv_refs[i], slot))
        slot = slot + seen.astype(jnp.int32)
    query_row = lax.broadcasted_iota(jnp.int32, (rows, rows), 0)
    key_row = lax.broadcasted_iota(jnp.int32, (rows, rows), 1)
    bias[:, :rows] = jnp.where(key_row <= query_row, 0.0, -1e30)
    later_row = lax.broadcasted_iota(jnp.int32, (rows, window - rows), 1)
    bias[:, rows:] = jnp.where(later_row < (slot - 1) * rows, 0.0, -1e30)
    factor = math.log2(math.e) / HEAD_SIZE**0.5
    heads = 4
    for first in range(0, QUERY_HEADS, heads):
        g = first // GROUP
        q = jnp.concatenate(
            [
                q_ref[:, (first + h) * HEAD_SIZE : (first + h + 1) * HEAD_SIZE]
                for h in range(heads)
            ],
            axis=0,
        )
        scores = lax.dot_general(
            q, keys[g], (((1,), (1,)), ((), ())), preferred_element_type=F32
        )
        scores = scores.reshape(heads, rows, window) * factor + bias[...][None]
        top = jnp.max(scores, axis=-1, keepdims=True)
        probs = jnp.exp2(scores - top).astype(BF16).reshape(heads * rows, window)
        summed = jnp.dot(probs, values[g], preferred_element_type=F32)
        result = (summed[:, :HEAD_SIZE] / summed[:, HEAD_SIZE : HEAD_SIZE + 1]).astype(BF16)
        for h in range(heads):
            out_ref[:, (first + h) * HEAD_SIZE : (first + h + 1) * HEAD_SIZE] = result[
                h * rows : (h + 1) * rows
            ]


def attend(own, docs, queries, kv_pieces, devices):
    rows = queries.shape[0]
    offsets = piece_places(devices // 2)
    window = (min(MOST_BLK, devices) + 1) * rows
    flat = [p for pair in kv_pieces for p in pair]
    vmem = pl.BlockSpec(memory_space=pltpu.VMEM)
    smem = pl.BlockSpec(memory_space=pltpu.SMEM)
    return pl.pallas_call(
        functools.partial(attend_kernel, offsets, devices),
        out_shape=jax.ShapeDtypeStruct(queries.shape, BF16),
        in_specs=[smem, smem, vmem] + [vmem] * len(flat),
        out_specs=vmem,
        scratch_shapes=[
            pltpu.VMEM((KEY_VALUE_HEADS, window, HEAD_SIZE), BF16),
            pltpu.VMEM((KEY_VALUE_HEADS, window, 2 * HEAD_SIZE), BF16),
            pltpu.VMEM((rows, window), F32),
        ],
        compiler_params=pltpu.CompilerParams(vmem_limit_bytes=VMEM_LIMIT),
        cost_estimate=pl.CostEstimate(
            flops=4 * QUERY_HEADS * rows * window * HEAD_SIZE,
            bytes_accessed=8 * 2**20,
            transcendentals=QUERY_HEADS * rows * window,
        ),
        name="attend",
    )(own, docs, queries, *flat)


def project_kernel(offsets, devices, own_ref, att_ref, res_ref, gain_ref, *refs):
    count = 2 * len(offsets)
    w_refs = refs[:count]
    hidden_ref, normed_ref, weight, sems = refs[count:]
    own = own_ref[0]
    rows = w_refs[0].shape[0]
    copies = []
    for i in range(count):
        block = block_of(own, offsets[i // 2], i % 2, devices)
        copies.append(
            pltpu.make_async_copy(
                w_refs[i],
                weight.at[pl.ds(pl.multiple_of(block * rows, rows), rows), :],
                sems.at[i],
            )
        )
        copies[-1].start()
    for c in copies:
        c.wait()
    hidden = res_ref[...].astype(F32) + jnp.dot(
        att_ref[...], weight[...], preferred_element_type=F32
    )
    hidden_ref[...] = hidden.astype(BF16)
    mean_square = jnp.mean(hidden * hidden, axis=-1, keepdims=True)
    normed_ref[...] = (
        hidden * lax.rsqrt(mean_square + 1e-06) * gain_ref[...].astype(F32)
    ).astype(BF16)


def project(own, attention, residual, gain, w_pieces, devices):
    offsets = piece_places(devices // 2)
    flat = [p for pair in w_pieces for p in pair]
    vmem = pl.BlockSpec(memory_space=pltpu.VMEM)
    smem = pl.BlockSpec(memory_space=pltpu.SMEM)
    hbm = pl.BlockSpec(memory_space=pl.ANY)
    total = flat[0].shape[0] * devices
    return pl.pallas_call(
        functools.partial(project_kernel, offsets, devices),
        out_shape=(
            jax.ShapeDtypeStruct(residual.shape, BF16),
            jax.ShapeDtypeStruct(residual.shape, BF16),
        ),
        in_specs=[smem, vmem, vmem, vmem] + [hbm] * len(flat),
        out_specs=(vmem, vmem),
        scratch_shapes=[
            pltpu.VMEM((total, residual.shape[1]), BF16),
            pltpu.SemaphoreType.DMA((len(flat),)),
        ],
        compiler_params=pltpu.CompilerParams(vmem_limit_bytes=VMEM_LIMIT),
        cost_estimate=pl.CostEstimate(
            flops=2 * residual.shape[0] * total * residual.shape[1],
            bytes_accessed=6 * 2**20,
            transcendentals=0,
        ),
        name="project",
    )(own, attention, residual, gain.reshape(1, -1), *flat)


def expert_kernel(first, count, scale_ref, gate_ref, up_ref, down_ref, *refs):
    x_refs, out_refs = refs[:count], refs[count:]
    rows = x_refs[0].shape[0]
    x = jnp.concatenate([r[...] for r in x_refs], axis=0)
    gate_part = jnp.dot(x, gate_ref[...], preferred_element_type=F32)
    up_part = jnp.dot(x, up_ref[...], preferred_element_type=F32)
    activated = (gate_part / (1.0 + jnp.exp(-gate_part)) * up_part).astype(BF16)
    produced = jnp.dot(activated, down_ref[...], preferred_element_type=F32)
    for i in range(count):
        out_refs[i][...] = (
            produced[i * rows : (i + 1) * rows] * scale_ref[:, first + i : first + i + 1]
        ).astype(BF16)


def expert(scale, gate_proj, up_proj, down_proj, first, pieces):
    vmem = pl.BlockSpec(memory_space=pltpu.VMEM)
    count = len(pieces)
    shape = jax.ShapeDtypeStruct(pieces[0].shape, BF16)
    rows = count * shape.shape[0]
    return pl.pallas_call(
        functools.partial(expert_kernel, first, count),
        out_shape=(shape,) * count,
        in_specs=[vmem] * (4 + count),
        out_specs=(vmem,) * count,
        compiler_params=pltpu.CompilerParams(vmem_limit_bytes=VMEM_LIMIT),
        cost_estimate=pl.CostEstimate(
            flops=6 * rows * gate_proj.shape[0] * gate_proj.shape[1],
            bytes_accessed=4 * 2**20,
            transcendentals=rows * gate_proj.shape[1],
        ),
        name="expert",
    )(scale, gate_proj, up_proj, down_proj, *pieces)


def added(*terms):
    return functools.reduce(lambda a, b: a + b, [t.astype(F32) for t in terms])


def ring_scatter_sum(parts, devices):
    chips = devices // 2
    half = chips // 2
    forward, backward = ring_steps(chips)
    swap = core_step(devices)
    terms = {d: (own, lax.ppermute(other, "seq", swap)) for d, (own, other) in parts.items()}
    far = added(*terms[half]).astype(BF16)
    cut = far.shape[0] // 2
    ahead = lax.ppermute(far[:cut], "seq", forward)
    behind = lax.ppermute(far[cut:], "seq", backward)
    pad = jnp.zeros((cut, far.shape[1]), BF16)
    ahead = jnp.concatenate([ahead, pad], axis=0)
    behind = jnp.concatenate([pad, behind], axis=0)
    for j in range(half - 1, 0, -1):
        ahead = lax.ppermute(added(ahead, *terms[j]).astype(BF16), "seq", forward)
        behind = lax.ppermute(added(behind, *terms[-j]).astype(BF16), "seq", backward)
    return added(ahead, behind, *terms[0]).astype(BF16)


def shards(
    queries,
    token_key_heads,
    token_value_heads,
    residual,
    out_weight,
    norm_gain,
    w_gate,
    w_up,
    w_down,
    expert_ids,
    gate_weights,
    doc_of_block,
):
    devices = lax.axis_size("seq")
    chips = devices // 2
    rows = queries.shape[0]
    own = lax.axis_index("seq").astype(jnp.int32)
    own_ref = own.reshape(1)

    experts = jnp.arange(devices, dtype=jnp.int32)
    by_expert = jnp.sum(
        jnp.where(expert_ids[None] == experts[:, None, None], gate_weights[None], 0.0), axis=-1
    )
    high = by_expert.astype(BF16)
    low = (by_expert - high.astype(F32)).astype(BF16)
    kv_width = 2 * token_key_heads.shape[1]
    split = jnp.concatenate([high, low], axis=0).reshape(-1, kv_width)
    extra = split.shape[0]
    padded = -(-extra // 16) * 16
    split = jnp.pad(split, ((0, padded - extra), (0, 0)))
    packed = jnp.concatenate(
        [jnp.concatenate([token_key_heads, token_value_heads], axis=1), split], axis=0
    )
    kv_pieces = gather_all(packed, devices)
    w_pieces = gather_all(out_weight, devices)

    attention = attend(own_ref, doc_of_block, queries, kv_pieces, devices)
    hidden, normed = project(own_ref, attention, residual, norm_gain, w_pieces, devices)

    scales = jnp.stack([p[rows : rows + extra] for pair in kv_pieces for p in pair])
    scales = scales.reshape(devices, 2, devices, rows)
    scales = lax.dynamic_index_in_dim(scales, own, axis=2, keepdims=False).astype(F32)
    scales = jnp.transpose(scales[:, 0] + scales[:, 1])

    tokens = gather_all(normed, devices)
    offsets = piece_places(chips)
    groups = [[0]] + [[i, i + 1] for i in range(1, chips - 1, 2)] + [[chips - 1]]
    parts = {}
    for group in groups:
        pieces = [p for i in group for p in tokens[i]]
        outs = expert(scales, w_gate[0], w_up[0], w_down[0], 2 * group[0], pieces)
        for n, i in enumerate(group):
            parts[offsets[i]] = (outs[2 * n], outs[2 * n + 1])
    mix = ring_scatter_sum(parts, devices)
    return (attention, hidden, mix)


def solution(mesh):
    in_specs = (
        P(("pack", "seq"), None),
        P(("pack", "seq"), None),
        P(("pack", "seq"), None),
        P(("pack", "seq"), None),
        P("seq", None),
        P(),
        P("seq", None, None),
        P("seq", None, None),
        P("seq", None, None),
        P(("pack", "seq"), None),
        P(("pack", "seq"), None),
        P("pack"),
    )
    out_specs = (P(("pack", "seq"), None), P(("pack", "seq"), None), P(("pack", "seq"), None))
    return jax.shard_map(shards, mesh=mesh, in_specs=in_specs, out_specs=out_specs, check_vma=False)
```

time: 338 us -> 164 us (0.49)
  the two profiles are of different devices: /device:TPU:13 before, /device:TPU:0 now
where the time goes in v1:
time: 164 us; the launch traced here: 162 us
  local copies, waits for them, and re-layouts  52.6 us (32%)
  waiting for transfers between devices  47.9 us (29%)
  starting transfers between devices  39.4 us (24%)
  Pallas kernels  17.8 us (11%)
  other arithmetic  3.24 us (2%)
    unnamed x113, local copies, waits for them, and re-layouts  34.9 us
    ppermute x9, starting transfers between devices, ring_gather(): ahead = lax.ppermute(ahead, 'seq', forward)  16.6 us
    ppermute x3, waiting for transfers between devices, ring_scatter_sum(): ahead = lax.ppermute(added(ahead, *terms[j]).astype(BF16), 'seq', forward)  12.6 us
    ppermute x9, waiting for transfers between devices, ring_gather(): ahead = lax.ppermute(ahead, 'seq', forward)  11.1 us
    pallas_call x5, Pallas kernels, expert(): pl.pallas_call(functools.partial(expert_kernel, first, count), out_shape=...  8.53 us
    slice x21, local copies, waits for them, and re-layouts, shards(): p[rows:rows + extra]  8.15 us
    ppermute x9, waiting for transfers between devices, ring_gather(): behind = lax.ppermute(behind, 'seq', backward)  8.09 us
    pallas_call x1, Pallas kernels, attend(): pl.pallas_call(functools.partial(attend_kernel, offsets, devices), out_sh...  6.28 us
  transfers between devices with their start and end apart: 64, of which 21 were waited for; matrix products, arithmetic and copies ran while one was open for 16% of the time, Pallas kernels for 9%

profile of v1, /device:TPU:0, one launch (start us, length us, event | category | flops | bytes accessed | tf_op | source)
XLA Modules:
  0.0 162.2 jit_solution(8984333558963299879)
XLA Ops:
  0.6 3.1 %collective-permute-start.17 = (bf16[128,1024]{1,0:T(8,128)(2,1)}, bf16[128,1024]{1,0:T(8,128)(2,1)S(1)}, u32[]{:S(2)}, u32[]{:S(2)}) collective-permute-start(bf16[128,1024]{1,0:T(8,128)(2,1)} %refs_0_.1), channel_id=1, source_target_pairs={{0,4},{1,5},{4,8},{5,9},{8,12},{9,13},{12,14},{13,15},{14,10},{15,... | collective-permute-start | bytes 786440 | tf_op jit(solution)/shard_map/ppermute | solution.py:57
  5.4 2.1 %collective-permute-start.1 = (bf16[144,512]{1,0:T(8,128)(2,1)S(1)}, bf16[144,512]{1,0:T(8,128)(2,1)S(1)}, u32[]{:S(2)}, u32[]{:S(2)}) collective-permute-start(bf16[144,512]{1,0:T(8,128)(2,1)S(1)} %fusion.1.refs_0_), channel_id=1, source_target_pairs={{0,4},{1,5},{4,8},{5,9},{8,12},{9,13},{12,14},{13,15},{14,10},{15,... | collective-permute-start | bytes 442376 | tf_op jit(solution)/shard_map/ppermute | solution.py:57
  7.5 3.6 %collective-permute-done.17.refs_2_ = bf16[128,1024]{1,0:T(8,128)(2,1)S(1)} collective-permute-done((bf16[128,1024]{1,0:T(8,128)(2,1)}, bf16[128,1024]{1,0:T(8,128)(2,1)S(1)}, u32[]{:S(2)}, u32[]{:S(2)}) %collective-permute-start.17) | collective-permute-done | bytes 262176 | tf_op jit(solution)/shard_map/ppermute | solution.py:57
  11.0 2.1 %collective-permute-start.21 = (bf16[128,1024]{1,0:T(8,128)(2,1)S(1)}, bf16[128,1024]{1,0:T(8,128)(2,1)S(1)}, u32[]{:S(2)}, u32[]{:S(2)}) collective-permute-start(bf16[128,1024]{1,0:T(8,128)(2,1)S(1)} %collective-permute-done.17.refs_2_), channel_id=1, source_target_pairs={{0,4},{1,5},{4,8},{5,9},{8,12},{9,13},{12,14},{13,15},{14,10},{15,... | collective-permute-start | bytes 786440 | tf_op jit(solution)/shard_map/ppermute | solution.py:57
  13.1 2.0 %collective-permute-start.23 = (bf16[128,1024]{1,0:T(8,128)(2,1)S(1)}, bf16[128,1024]{1,0:T(8,128)(2,1)S(1)}, u32[]{:S(2)}, u32[]{:S(2)}) collective-permute-start(bf16[128,1024]{1,0:T(8,128)(2,1)S(1)} %collective-permute-done.19.refs_4_), channel_id=1, source_target_pairs={{4,0},{5,1},{8,4},{9,5},{12,8},{13,9},{14,12},{15,13},{10,14},{11,... | collective-permute-start | bytes 786440 | tf_op jit(solution)/shard_map/ppermute | solution.py:58
  16.3 3.6 %collective-permute-done.3.refs_4_ = bf16[144,512]{1,0:T(8,128)(2,1)S(1)} collective-permute-done((bf16[144,512]{1,0:T(8,128)(2,1)S(1)}, bf16[144,512]{1,0:T(8,128)(2,1)S(1)}, u32[]{:S(2)}, u32[]{:S(2)}) %collective-permute-start.3) | collective-permute-done | bytes 147488 | tf_op jit(solution)/shard_map/ppermute | solution.py:58
  19.9 2.3 %collective-permute-done.5.refs_6_ = bf16[144,512]{1,0:T(8,128)(2,1)} collective-permute-done((bf16[144,512]{1,0:T(8,128)(2,1)S(1)}, bf16[144,512]{1,0:T(8,128)(2,1)}, u32[]{:S(2)}, u32[]{:S(2)}) %collective-permute-start.5) | collective-permute-done | bytes 147488 | tf_op jit(solution)/shard_map/ppermute | solution.py:57
  22.2 1.8 %collective-permute-start.9 = (bf16[144,512]{1,0:T(8,128)(2,1)}, bf16[144,512]{1,0:T(8,128)(2,1)}, u32[]{:S(2)}, u32[]{:S(2)}) collective-permute-start(bf16[144,512]{1,0:T(8,128)(2,1)} %collective-permute-done.5.refs_6_), channel_id=1, source_target_pairs={{0,4},{1,5},{4,8},{5,9},{8,12},{9,13},{12,14},{13,15},{14,10},{15,... | collective-permute-start | bytes 442376 | tf_op jit(solution)/shard_map/ppermute | solution.py:57
  24.0 1.6 collective-permute-start.25
  32.6 2.5 %collective-permute-done.11.refs_12_ = bf16[144,512]{1,0:T(8,128)(2,1)} collective-permute-done((bf16[144,512]{1,0:T(8,128)(2,1)S(1)}, bf16[144,512]{1,0:T(8,128)(2,1)}, u32[]{:S(2)}, u32[]{:S(2)}) %collective-permute-start.11) | collective-permute-done | bytes 147488 | tf_op jit(solution)/shard_map/ppermute | solution.py:58
  35.1 1.6 collective-permute-start.13
  38.2 2.0 %collective-permute-done.27.refs_12_ = bf16[128,1024]{1,0:T(8,128)(2,1)S(1)} collective-permute-done((bf16[128,1024]{1,0:T(8,128)(2,1)S(1)}, bf16[128,1024]{1,0:T(8,128)(2,1)S(1)}, u32[]{:S(2)}, u32[]{:S(2)}) %collective-permute-start.27) | collective-permute-done | bytes 262176 | tf_op jit(solution)/shard_map/ppermute | solution.py:58
  40.7 1.6 collective-permute-start.29
  43.4 2.0 %collective-permute-done.14 = bf16[80,512]{1,0:T(8,128)(2,1)S(1)} collective-permute-done((bf16[80,512]{1,0:T(8,128)(2,1)S(1)}, bf16[80,512]{1,0:T(8,128)(2,1)S(1)}, u32[]{:S(2)}, u32[]{:S(2)}) %collective-permute-start.14) | collective-permute-done | bytes 81952 | tf_op jit(solution)/shard_map/ppermute | solution.py:62
  71.3 6.3 %attend.1.att_ref = bf16[128,2048]{1,0:T(8,128)(2,1)} custom-call(s32[1]{0:T(128)} %bitcast.own_ref, s32[16]{0:T(128)S(1)} %copy-done.42, bf16[128,2048]{1,0:T(8,128)(2,1)S(1)} %copy-done.39, bf16[144,512]{1,0:T(8,128)(2,1)S(1)} %fusion.1.refs_0_, bf16[144,512]{1,0:T(8,128)(2,1)S(1)} %copy-done.24, bf16[144,512]{1,0:T(8,128)(2,1)S(1)} %copy-done.20, ...), custom_call_target="tpu_custom_call" | custom-call | flops 1207959552 | bytes 8388608 | tf_op jit(solution)/shard_map/attend/pallas_call | solution.py:149
  83.9 3.0 %project.1 = (bf16[128,1024]{1,0:T(8,128)(2,1)}, bf16[128,1024]{1,0:T(8,128)(2,1)S(1)}) custom-call(s32[1]{0:T(128)} %bitcast.own_ref, bf16[128,2048]{1,0:T(8,128)(2,1)S(1)} %copy-done.3, bf16[128,1024]{1,0:T(8,128)(2,1)S(1)} %copy-done.4, bf16[1,1024]{1,0:T(2,128)(2,1)S(1)} %copy-done.16, bf16[128,1024]{1,0:T(8,128)(2,1)S(1)} %copy-done.5, ...), custom_call_target="tpu_custom_call" | custom-call | flops 536870912 | bytes 6291456 | tf_op jit(solution)/shard_map/project/pallas_call | solution.py:205
  86.9 1.7 %collective-permute-start.32 = (bf16[128,1024]{1,0:T(8,128)(2,1)S(1)}, bf16[128,1024]{1,0:T(8,128)(2,1)S(1)}, u32[]{:S(2)}, u32[]{:S(2)}) collective-permute-start(bf16[128,1024]{1,0:T(8,128)(2,1)S(1)} %get-tuple-element.22.refs_0_), channel_id=1, source_target_pairs={{0,4},{1,5},{4,8},{5,9},{8,12},{9,13},{12,14},{13,15},{14,10},{15,... | collective-permute-start | bytes 786440 | tf_op jit(solution)/shard_map/ppermute | solution.py:57
  92.3 3.0 %collective-permute-done.32.refs_0_ = bf16[128,1024]{1,0:T(8,128)(2,1)S(1)} collective-permute-done((bf16[128,1024]{1,0:T(8,128)(2,1)S(1)}, bf16[128,1024]{1,0:T(8,128)(2,1)S(1)}, u32[]{:S(2)}, u32[]{:S(2)}) %collective-permute-start.32) | collective-permute-done | bytes 262176 | tf_op jit(solution)/shard_map/ppermute | solution.py:57
  95.3 1.6 collective-permute-start.33
  102.9 1.5 collective-permute-start.34
  108.2 1.4 collective-permute-done.34.refs_0_
  110.3 1.4 collective-permute-start.35
  116.5 1.8 %collective-permute-done.39 = bf16[64,1024]{1,0:T(8,128)(2,1)} collective-permute-done((bf16[64,1024]{1,0:T(8,128)(2,1)}, bf16[64,1024]{1,0:T(8,128)(2,1)}, u32[]{:S(2)}, u32[]{:S(2)}) %collective-permute-start.39) | collective-permute-done | bytes 131104 | tf_op jit(solution)/shard_map/ppermute | solution.py:62
  122.6 1.8 %expert.6 = (bf16[128,1024]{1,0:T(8,128)(2,1)S(1)}, bf16[128,1024]{1,0:T(8,128)(2,1)S(1)}, bf16[128,1024]{1,0:T(8,128)(2,1)S(1)}, bf16[128,1024]{1,0:T(8,128)(2,1)S(1)}) custom-call(f32[128,16]{1,0:T(8,128)S(1)} %fusion.2.scale_ref, bf16[1024,384]{1,0:T(8,128)(2,1)S(1)} %bitcast.13, bf16[1024,384]{1,0:T(8,128)(2,1)S(1)} %bitcast.18, ...), custom_call_target="tpu_custom_call" | custom-call | flops 1207959552 | bytes 4194304 | tf_op jit(solution)/shard_map/expert/pallas_call | solution.py:246
  125.0 1.7 %collective-permute-start.42 = (bf16[64,1024]{1,0:T(8,128)(2,1)S(1)}, bf16[64,1024]{1,0:T(8,128)(2,1)S(1)}, u32[]{:S(2)}, u32[]{:S(2)}) collective-permute-start(bf16[64,1024]{1,0:T(8,128)(2,1)S(1)} %get-tuple-element.41), channel_id=1, source_target_pairs={{0,4},{1,5},{4,8},{5,9},{8,12},{9,13},{12,14},{13,15},{14,10},{15,... | collective-permute-start | bytes 393224 | tf_op jit(solution)/shard_map/ppermute | solution.py:273
  127.3 2.8 %expert.7 = (bf16[128,1024]{1,0:T(8,128)(2,1)S(1)}, bf16[128,1024]{1,0:T(8,128)(2,1)S(1)}, bf16[128,1024]{1,0:T(8,128)(2,1)S(1)}, bf16[128,1024]{1,0:T(8,128)(2,1)S(1)}) custom-call(f32[128,16]{1,0:T(8,128)S(1)} %fusion.2.scale_ref, bf16[1024,384]{1,0:T(8,128)(2,1)S(1)} %bitcast.14, bf16[1024,384]{1,0:T(8,128)(2,1)S(1)} %bitcast.19, ...), custom_call_target="tpu_custom_call" | custom-call | flops 1207959552 | bytes 4194304 | tf_op jit(solution)/shard_map/expert/pallas_call | solution.py:246
  131.3 4.8 %collective-permute-done.55 = bf16[64,1024]{1,0:T(8,128)(2,1)S(1)} collective-permute-done((bf16[64,1024]{1,0:T(8,128)(2,1)S(1)}, bf16[64,1024]{1,0:T(8,128)(2,1)S(1)}, u32[]{:S(2)}, u32[]{:S(2)}) %collective-permute-start.55) | collective-permute-done | bytes 131104 | tf_op jit(solution)/shard_map/ppermute | solution.py:274
  138.4 1.8 %expert.8 = (bf16[128,1024]{1,0:T(8,128)(2,1)S(1)}, bf16[128,1024]{1,0:T(8,128)(2,1)S(1)}, bf16[128,1024]{1,0:T(8,128)(2,1)S(1)}, bf16[128,1024]{1,0:T(8,128)(2,1)S(1)}) custom-call(f32[128,16]{1,0:T(8,128)S(1)} %fusion.2.scale_ref, bf16[1024,384]{1,0:T(8,128)(2,1)S(1)} %bitcast.15, bf16[1024,384]{1,0:T(8,128)(2,1)S(1)} %bitcast.20, ...), custom_call_target="tpu_custom_call" | custom-call | flops 1207959552 | bytes 4194304 | tf_op jit(solution)/shard_map/expert/pallas_call | solution.py:246
  140.4 3.1 %collective-permute-done.46 = bf16[128,1024]{1,0:T(8,128)(2,1)S(1)} collective-permute-done((bf16[128,1024]{1,0:T(8,128)(2,1)S(1)}, bf16[128,1024]{1,0:T(8,128)(2,1)S(1)}, u32[]{:S(2)}, u32[]{:S(2)}) %collective-permute-start.46) | collective-permute-done | bytes 262176 | tf_op jit(solution)/shard_map/ppermute | solution.py:279
  144.1 2.0 %collective-permute-done.57 = bf16[128,1024]{1,0:T(8,128)(2,1)S(1)} collective-permute-done((bf16[128,1024]{1,0:T(8,128)(2,1)S(1)}, bf16[128,1024]{1,0:T(8,128)(2,1)S(1)}, u32[]{:S(2)}, u32[]{:S(2)}) %collective-permute-start.57) | collective-permute-done | bytes 262176 | tf_op jit(solution)/shard_map/ppermute | solution.py:280
  148.4 4.1 %collective-permute-done.50 = bf16[128,1024]{1,0:T(8,128)(2,1)S(1)} collective-permute-done((bf16[128,1024]{1,0:T(8,128)(2,1)S(1)}, bf16[128,1024]{1,0:T(8,128)(2,1)S(1)}, u32[]{:S(2)}, u32[]{:S(2)}) %collective-permute-start.50) | collective-permute-done | bytes 262176 | tf_op jit(solution)/shard_map/ppermute | solution.py:279
  155.3 5.3 %collective-permute-done.54 = bf16[128,1024]{1,0:T(8,128)(2,1)S(1)} collective-permute-done((bf16[128,1024]{1,0:T(8,128)(2,1)S(1)}, bf16[128,1024]{1,0:T(8,128)(2,1)S(1)}, u32[]{:S(2)}, u32[]{:S(2)}) %collective-permute-start.54) | collective-permute-done | bytes 262176 | tf_op jit(solution)/shard_map/ppermute | solution.py:279
  (280 shorter events, 80.0 us)
Async XLA Ops:
  0.6 10.4 %collective-permute-start.17 = (bf16[128,1024]{1,0:T(8,128)(2,1)}, bf16[128,1024]{1,0:T(8,128)(2,1)S(1)}, u32[]{:S(2)}, u32[]{:S(2)}) collective-permute-start(bf16[128,1024]{1,0:T(8,128)(2,1)} %refs_0_.1), channel_id=1, source_target_pairs={{0,4},{1,5},{4,8},{5,9},{8,12},{9,13},{12,14},{13,15},{14,10},{15,... | collective-permute-start | bytes 786440 | tf_op jit(solution)/shard_map/ppermute | solution.py:57
  3.7 9.4 %collective-permute-start.19 = (bf16[128,1024]{1,0:T(8,128)(2,1)}, bf16[128,1024]{1,0:T(8,128)(2,1)S(1)}, u32[]{:S(2)}, u32[]{:S(2)}) collective-permute-start(bf16[128,1024]{1,0:T(8,128)(2,1)} %refs_0_.1), channel_id=1, source_target_pairs={{4,0},{5,1},{8,4},{9,5},{12,8},{13,9},{14,12},{15,13},{10,14},{11,... | collective-permute-start | bytes 786440 | tf_op jit(solution)/shard_map/ppermute | solution.py:58
  5.4 9.7 %collective-permute-start.1 = (bf16[144,512]{1,0:T(8,128)(2,1)S(1)}, bf16[144,512]{1,0:T(8,128)(2,1)S(1)}, u32[]{:S(2)}, u32[]{:S(2)}) collective-permute-start(bf16[144,512]{1,0:T(8,128)(2,1)S(1)} %fusion.1.refs_0_), channel_id=1, source_target_pairs={{0,4},{1,5},{4,8},{5,9},{8,12},{9,13},{12,14},{13,15},{14,10},{15,... | collective-permute-start | bytes 442376 | tf_op jit(solution)/shard_map/ppermute | solution.py:57
  11.0 13.0 %collective-permute-start.21 = (bf16[128,1024]{1,0:T(8,128)(2,1)S(1)}, bf16[128,1024]{1,0:T(8,128)(2,1)S(1)}, u32[]{:S(2)}, u32[]{:S(2)}) collective-permute-start(bf16[128,1024]{1,0:T(8,128)(2,1)S(1)} %collective-permute-done.17.refs_2_), channel_id=1, source_target_pairs={{0,4},{1,5},{4,8},{5,9},{8,12},{9,13},{12,14},{13,15},{14,10},{15,... | collective-permute-start | bytes 786440 | tf_op jit(solution)/shard_map/ppermute | solution.py:57
  13.1 15.6 %collective-permute-start.23 = (bf16[128,1024]{1,0:T(8,128)(2,1)S(1)}, bf16[128,1024]{1,0:T(8,128)(2,1)S(1)}, u32[]{:S(2)}, u32[]{:S(2)}) collective-permute-start(bf16[128,1024]{1,0:T(8,128)(2,1)S(1)} %collective-permute-done.19.refs_4_), channel_id=1, source_target_pairs={{4,0},{5,1},{8,4},{9,5},{12,8},{13,9},{14,12},{15,13},{10,14},{11,... | collective-permute-start | bytes 786440 | tf_op jit(solution)/shard_map/ppermute | solution.py:58
  19.8 8.3 %collective-permute-start.7 = (bf16[144,512]{1,0:T(8,128)(2,1)S(1)}, bf16[144,512]{1,0:T(8,128)(2,1)S(1)}, u32[]{:S(2)}, u32[]{:S(2)}) collective-permute-start(bf16[144,512]{1,0:T(8,128)(2,1)S(1)} %collective-permute-done.3.refs_4_), channel_id=1, source_target_pairs={{4,0},{5,1},{8,4},{9,5},{12,8},{13,9},{14,12},{15,13},{10,14},{11,... | collective-permute-start | bytes 442376 | tf_op jit(solution)/shard_map/ppermute | solution.py:58
  19.9 8.4 %collective-permute-start.2 = (bf16[144,512]{1,0:T(8,128)(2,1)S(1)}, bf16[144,512]{1,0:T(8,128)(2,1)S(1)}, u32[]{:S(2)}, u32[]{:S(2)}) collective-permute-start(bf16[144,512]{1,0:T(8,128)(2,1)S(1)} %collective-permute-done.1.refs_2_), channel_id=1, source_target_pairs={{0,1},{1,0},{2,3},{3,2},{4,5},{5,4},{6,7},{7,6},{8,9},{9,8},{10,11... | collective-permute-start | bytes 442376 | tf_op jit(solution)/shard_map/ppermute | solution.py:72
  22.2 7.5 %collective-permute-start.9 = (bf16[144,512]{1,0:T(8,128)(2,1)}, bf16[144,512]{1,0:T(8,128)(2,1)}, u32[]{:S(2)}, u32[]{:S(2)}) collective-permute-start(bf16[144,512]{1,0:T(8,128)(2,1)} %collective-permute-done.5.refs_6_), channel_id=1, source_target_pairs={{0,4},{1,5},{4,8},{5,9},{8,12},{9,13},{12,14},{13,15},{14,10},{15,... | collective-permute-start | bytes 442376 | tf_op jit(solution)/shard_map/ppermute | solution.py:57
  24.0 11.1 %collective-permute-start.25 = (bf16[128,1024]{1,0:T(8,128)(2,1)S(1)}, bf16[128,1024]{1,0:T(8,128)(2,1)S(1)}, u32[]{:S(2)}, u32[]{:S(2)}) collective-permute-start(bf16[128,1024]{1,0:T(8,128)(2,1)S(1)} %collective-permute-done.21.refs_6_), channel_id=1, source_target_pairs={{0,4},{1,5},{4,8},{5,9},{8,12},{9,13},{12,14},{13,15},{14,10},{15,... | collective-permute-start | bytes 786440 | tf_op jit(solution)/shard_map/ppermute | solution.py:57
  28.2 12.0 %collective-permute-start.16 = (bf16[128,1024]{1,0:T(8,128)(2,1)S(1)}, bf16[128,1024]{1,0:T(8,128)(2,1)S(1)}, u32[]{:S(2)}, u32[]{:S(2)}) collective-permute-start(bf16[128,1024]{1,0:T(8,128)(2,1)S(1)} %copy-done.5), channel_id=1, source_target_pairs={{0,1},{1,0},{2,3},{3,2},{4,5},{5,4},{6,7},{7,6},{8,9},{9,8},{10,11... | collective-permute-start | bytes 786440 | tf_op jit(solution)/shard_map/ppermute | solution.py:72
  28.8 11.4 %collective-permute-start.27 = (bf16[128,1024]{1,0:T(8,128)(2,1)S(1)}, bf16[128,1024]{1,0:T(8,128)(2,1)S(1)}, u32[]{:S(2)}, u32[]{:S(2)}) collective-permute-start(bf16[128,1024]{1,0:T(8,128)(2,1)S(1)} %collective-permute-done.23.refs_8_), channel_id=1, source_target_pairs={{4,0},{5,1},{8,4},{9,5},{12,8},{13,9},{14,12},{15,13},{10,14},{11,... | collective-permute-start | bytes 786440 | tf_op jit(solution)/shard_map/ppermute | solution.py:58
  29.7 10.9 %collective-permute-start.4 = (bf16[144,512]{1,0:T(8,128)(2,1)S(1)}, bf16[144,512]{1,0:T(8,128)(2,1)S(1)}, u32[]{:S(2)}, u32[]{:S(2)}) collective-permute-start(bf16[144,512]{1,0:T(8,128)(2,1)S(1)} %collective-permute-done.3.refs_4_), channel_id=1, source_target_pairs={{0,1},{1,0},{2,3},{3,2},{4,5},{5,4},{6,7},{7,6},{8,9},{9,8},{10,11... | collective-permute-start | bytes 442376 | tf_op jit(solution)/shard_map/ppermute | solution.py:72
  35.1 7.6 %collective-permute-start.8 = (bf16[144,512]{1,0:T(8,128)(2,1)S(1)}, bf16[144,512]{1,0:T(8,128)(2,1)S(1)}, u32[]{:S(2)}, u32[]{:S(2)}) collective-permute-start(bf16[144,512]{1,0:T(8,128)(2,1)S(1)} %collective-permute-done.7.refs_8_), channel_id=1, source_target_pairs={{0,1},{1,0},{2,3},{3,2},{4,5},{5,4},{6,7},{7,6},{8,9},{9,8},{10,11... | collective-permute-start | bytes 442376 | tf_op jit(solution)/shard_map/ppermute | solution.py:72
  48.0 29.6 %collective-permute-start.22 = (bf16[128,1024]{1,0:T(8,128)(2,1)S(1)}, bf16[128,1024]{1,0:T(8,128)(2,1)S(1)}, u32[]{:S(2)}, u32[]{:S(2)}) collective-permute-start(bf16[128,1024]{1,0:T(8,128)(2,1)S(1)} %collective-permute-done.21.refs_6_), channel_id=1, source_target_pairs={{0,1},{1,0},{2,3},{3,2},{4,5},{5,4},{6,7},{7,6},{8,9},{9,8},{10,11... | collective-permute-start | bytes 786440 | tf_op jit(solution)/shard_map/ppermute | solution.py:72
  48.6 29.8 %collective-permute-start.24 = (bf16[128,1024]{1,0:T(8,128)(2,1)S(1)}, bf16[128,1024]{1,0:T(8,128)(2,1)S(1)}, u32[]{:S(2)}, u32[]{:S(2)}) collective-permute-start(bf16[128,1024]{1,0:T(8,128)(2,1)S(1)} %collective-permute-done.23.refs_8_), channel_id=1, source_target_pairs={{0,1},{1,0},{2,3},{3,2},{4,5},{5,4},{6,7},{7,6},{8,9},{9,8},{10,11... | collective-permute-start | bytes 786440 | tf_op jit(solution)/shard_map/ppermute | solution.py:72
  49.3 29.7 %collective-permute-start.26 = (bf16[128,1024]{1,0:T(8,128)(2,1)S(1)}, bf16[128,1024]{1,0:T(8,128)(2,1)}, u32[]{:S(2)}, u32[]{:S(2)}) collective-permute-start(bf16[128,1024]{1,0:T(8,128)(2,1)S(1)} %collective-permute-done.25.refs_10_), channel_id=1, source_target_pairs={{0,1},{1,0},{2,3},{3,2},{4,5},{5,4},{6,7},{7,6},{8,9},{9,8},{10,11... | collective-permute-start | bytes 786440 | tf_op jit(solution)/shard_map/ppermute | solution.py:72
  50.4 28.7 %collective-permute-start.28 = (bf16[128,1024]{1,0:T(8,128)(2,1)S(1)}, bf16[128,1024]{1,0:T(8,128)(2,1)}, u32[]{:S(2)}, u32[]{:S(2)}) collective-permute-start(bf16[128,1024]{1,0:T(8,128)(2,1)S(1)} %collective-permute-done.27.refs_12_), channel_id=1, source_target_pairs={{0,1},{1,0},{2,3},{3,2},{4,5},{5,4},{6,7},{7,6},{8,9},{9,8},{10,11... | collective-permute-start | bytes 786440 | tf_op jit(solution)/shard_map/ppermute | solution.py:72
  51.2 27.9 %collective-permute-start.31 = (bf16[128,1024]{1,0:T(8,128)(2,1)S(1)}, bf16[128,1024]{1,0:T(8,128)(2,1)}, u32[]{:S(2)}, u32[]{:S(2)}) collective-permute-start(bf16[128,1024]{1,0:T(8,128)(2,1)S(1)} %constant_dynamic-update-slice_fusion.2.refs_14_), channel_id=1, source_target_pairs={{0,1},{1,0},{2,3},{3,2},{4,5},{5,4},{6,7},{7,6},{8,9},{9,8},{10,11... | collective-permute-start | bytes 786440 | tf_op jit(solution)/shard_map/ppermute | solution.py:72
  86.9 8.4 %collective-permute-start.32 = (bf16[128,1024]{1,0:T(8,128)(2,1)S(1)}, bf16[128,1024]{1,0:T(8,128)(2,1)S(1)}, u32[]{:S(2)}, u32[]{:S(2)}) collective-permute-start(bf16[128,1024]{1,0:T(8,128)(2,1)S(1)} %get-tuple-element.22.refs_0_), channel_id=1, source_target_pairs={{0,4},{1,5},{4,8},{5,9},{8,12},{9,13},{12,14},{13,15},{14,10},{15,... | collective-permute-start | bytes 786440 | tf_op jit(solution)/shard_map/ppermute | solution.py:57
  90.0 8.2 %collective-permute-start.36 = (bf16[128,1024]{1,0:T(8,128)(2,1)S(1)}, bf16[128,1024]{1,0:T(8,128)(2,1)S(1)}, u32[]{:S(2)}, u32[]{:S(2)}) collective-permute-start(bf16[128,1024]{1,0:T(8,128)(2,1)S(1)} %get-tuple-element.22.refs_0_), channel_id=1, source_target_pairs={{4,0},{5,1},{8,4},{9,5},{12,8},{13,9},{14,12},{15,13},{10,14},{11,... | collective-permute-start | bytes 786440 | tf_op jit(solution)/shard_map/ppermute | solution.py:58
  95.3 7.6 %collective-permute-start.33 = (bf16[128,1024]{1,0:T(8,128)(2,1)S(1)}, bf16[128,1024]{1,0:T(8,128)(2,1)}, u32[]{:S(2)}, u32[]{:S(2)}) collective-permute-start(bf16[128,1024]{1,0:T(8,128)(2,1)S(1)} %collective-permute-done.32.refs_0_), channel_id=1, source_target_pairs={{0,4},{1,5},{4,8},{5,9},{8,12},{9,13},{12,14},{13,15},{14,10},{15,... | collective-permute-start | bytes 786440 | tf_op jit(solution)/shard_map/ppermute | solution.py:57
  98.2 7.5 %collective-permute-start.37 = (bf16[128,1024]{1,0:T(8,128)(2,1)S(1)}, bf16[128,1024]{1,0:T(8,128)(2,1)}, u32[]{:S(2)}, u32[]{:S(2)}) collective-permute-start(bf16[128,1024]{1,0:T(8,128)(2,1)S(1)} %collective-permute-done.36.refs_2_), channel_id=1, source_target_pairs={{4,0},{5,1},{8,4},{9,5},{12,8},{13,9},{14,12},{15,13},{10,14},{11,... | collective-permute-start | bytes 786440 | tf_op jit(solution)/shard_map/ppermute | solution.py:58
  126.7 20.5 %collective-permute-start.62 = (bf16[128,1024]{1,0:T(8,128)(2,1)S(1)}, bf16[128,1024]{1,0:T(8,128)(2,1)S(1)}, u32[]{:S(2)}, u32[]{:S(2)}) collective-permute-start(bf16[128,1024]{1,0:T(8,128)(2,1)S(1)} %get-tuple-element.22.refs_0_), channel_id=1, source_target_pairs={{0,1},{1,0},{2,3},{3,2},{4,5},{5,4},{6,7},{7,6},{8,9},{9,8},{10,11... | collective-permute-start | bytes 786440 | tf_op jit(solution)/shard_map/ppermute | solution.py:72
  126.7 10.6 %collective-permute-start.52 = (bf16[128,1024]{1,0:T(8,128)(2,1)S(1)}, bf16[128,1024]{1,0:T(8,128)(2,1)S(1)}, u32[]{:S(2)}, u32[]{:S(2)}) collective-permute-start(bf16[128,1024]{1,0:T(8,128)(2,1)S(1)} %copy-done.41), channel_id=1, source_target_pairs={{0,1},{1,0},{2,3},{3,2},{4,5},{5,4},{6,7},{7,6},{8,9},{9,8},{10,11... | collective-permute-start | bytes 786440 | tf_op jit(solution)/shard_map/ppermute | solution.py:72
  131.3 9.0 %collective-permute-start.49 = (bf16[128,1024]{1,0:T(8,128)(2,1)S(1)}, bf16[128,1024]{1,0:T(8,128)(2,1)S(1)}, u32[]{:S(2)}, u32[]{:S(2)}) collective-permute-start(bf16[128,1024]{1,0:T(8,128)(2,1)S(1)} %get-tuple-element.28), channel_id=1, source_target_pairs={{0,1},{1,0},{2,3},{3,2},{4,5},{5,4},{6,7},{7,6},{8,9},{9,8},{10,11... | collective-permute-start | bytes 786440 | tf_op jit(solution)/shard_map/ppermute | solution.py:270
  136.1 7.4 %collective-permute-start.46 = (bf16[128,1024]{1,0:T(8,128)(2,1)S(1)}, bf16[128,1024]{1,0:T(8,128)(2,1)S(1)}, u32[]{:S(2)}, u32[]{:S(2)}) collective-permute-start(bf16[128,1024]{1,0:T(8,128)(2,1)S(1)} %add_convert_fusion.6), channel_id=1, source_target_pairs={{0,4},{1,5},{4,8},{5,9},{8,12},{9,13},{12,14},{13,15},{14,10},{15,... | collective-permute-start | bytes 786440 | tf_op jit(solution)/shard_map/ppermute | solution.py:279
  137.4 8.7 %collective-permute-start.57 = (bf16[128,1024]{1,0:T(8,128)(2,1)S(1)}, bf16[128,1024]{1,0:T(8,128)(2,1)S(1)}, u32[]{:S(2)}, u32[]{:S(2)}) collective-permute-start(bf16[128,1024]{1,0:T(8,128)(2,1)S(1)} %add_convert_fusion.3), channel_id=1, source_target_pairs={{4,0},{5,1},{8,4},{9,5},{12,8},{13,9},{14,12},{15,13},{10,14},{11,... | collective-permute-start | bytes 786440 | tf_op jit(solution)/shard_map/ppermute | solution.py:280
  140.2 8.2 %collective-permute-start.53 = (bf16[128,1024]{1,0:T(8,128)(2,1)S(1)}, bf16[128,1024]{1,0:T(8,128)(2,1)S(1)}, u32[]{:S(2)}, u32[]{:S(2)}) collective-permute-start(bf16[128,1024]{1,0:T(8,128)(2,1)S(1)} %get-tuple-element.30), channel_id=1, source_target_pairs={{0,1},{1,0},{2,3},{3,2},{4,5},{5,4},{6,7},{7,6},{8,9},{9,8},{10,11... | collective-permute-start | bytes 786440 | tf_op jit(solution)/shard_map/ppermute | solution.py:270
  143.6 9.4 %collective-permute-start.60 = (bf16[128,1024]{1,0:T(8,128)(2,1)S(1)}, bf16[128,1024]{1,0:T(8,128)(2,1)S(1)}, u32[]{:S(2)}, u32[]{:S(2)}) collective-permute-start(bf16[128,1024]{1,0:T(8,128)(2,1)S(1)} %get-tuple-element.36), channel_id=1, source_target_pairs={{0,1},{1,0},{2,3},{3,2},{4,5},{5,4},{6,7},{7,6},{8,9},{9,8},{10,11... | collective-permute-start | bytes 786440 | tf_op jit(solution)/shard_map/ppermute | solution.py:270
  143.7 8.8 %collective-permute-start.50 = (bf16[128,1024]{1,0:T(8,128)(2,1)S(1)}, bf16[128,1024]{1,0:T(8,128)(2,1)S(1)}, u32[]{:S(2)}, u32[]{:S(2)}) collective-permute-start(bf16[128,1024]{1,0:T(8,128)(2,1)S(1)} %add_convert_fusion.5), channel_id=1, source_target_pairs={{0,4},{1,5},{4,8},{5,9},{8,12},{9,13},{12,14},{13,15},{14,10},{15,... | collective-permute-start | bytes 786440 | tf_op jit(solution)/shard_map/ppermute | solution.py:279
  146.2 7.9 %collective-permute-start.59 = (bf16[128,1024]{1,0:T(8,128)(2,1)S(1)}, bf16[128,1024]{1,0:T(8,128)(2,1)S(1)}, u32[]{:S(2)}, u32[]{:S(2)}) collective-permute-start(bf16[128,1024]{1,0:T(8,128)(2,1)S(1)} %add_convert_fusion.2), channel_id=1, source_target_pairs={{4,0},{5,1},{8,4},{9,5},{12,8},{13,9},{14,12},{15,13},{10,14},{11,... | collective-permute-start | bytes 786440 | tf_op jit(solution)/shard_map/ppermute | solution.py:280
  152.6 8.0 %collective-permute-start.54 = (bf16[128,1024]{1,0:T(8,128)(2,1)S(1)}, bf16[128,1024]{1,0:T(8,128)(2,1)S(1)}, u32[]{:S(2)}, u32[]{:S(2)}) collective-permute-start(bf16[128,1024]{1,0:T(8,128)(2,1)S(1)} %add_convert_fusion.4), channel_id=1, source_target_pairs={{0,4},{1,5},{4,8},{5,9},{8,12},{9,13},{12,14},{13,15},{14,10},{15,... | collective-permute-start | bytes 786440 | tf_op jit(solution)/shard_map/ppermute | solution.py:279
  (85 other events, 439.7 us)

commit v2 on v1

v2 whole, which is shorter than its diff:
```python
import functools
import math

import jax
import jax.numpy as jnp
from jax import lax
from jax.experimental import pallas as pl
from jax.experimental.pallas import tpu as pltpu
from jax.sharding import PartitionSpec as P

QUERY_HEADS = 16
KEY_VALUE_HEADS = 2
HEAD_SIZE = 128
MOST_BLK = 8
GROUP = QUERY_HEADS // KEY_VALUE_HEADS
F32 = jnp.float32
BF16 = jnp.bfloat16
VMEM_LIMIT = 60 * 1024 * 1024
VMEM = pl.BlockSpec(memory_space=pltpu.VMEM)
SMEM = pl.BlockSpec(memory_space=pltpu.SMEM)
HBM = pl.BlockSpec(memory_space=pl.ANY)
PARAMS = pltpu.CompilerParams(vmem_limit_bytes=VMEM_LIMIT)


def ring_steps(chips):
    order = [2 * i for i in range(chips // 2)] + [2 * i + 1 for i in reversed(range(chips // 2))]
    steps = []
    for i in range(chips):
        steps.append((2 * order[i], 2 * order[(i + 1) % chips]))
        steps.append((2 * order[i] + 1, 2 * order[i - 1] + 1))
    return steps


def swap_steps(devices):
    return [(i, i ^ 1) for i in range(devices)]


def piece_groups(chips):
    groups = [[(0, 0), (0, 1)]]
    for j in range(1, chips // 2):
        groups.append([(-j, 0), (-j, 1), (j, 1), (j, 0)])
    return groups + [[(-(chips // 2), 0), (chips // 2, 1)]]


def piece_names(devices):
    return [name for group in piece_groups(devices // 2) for name in group]


def block_of(own, name, devices):
    chips = devices // 2
    chip, core = own // 2, own % 2
    place = jnp.where(chip % 2 == 0, chip // 2, chips - 1 - chip // 2)
    place = (place + jnp.where(core == 0, name[0], -name[0]) + chips) % chips
    chip = jnp.where(place < chips // 2, 2 * place, 2 * (chips - 1 - place) + 1)
    return 2 * chip + (core if name[1] == 0 else 1 - core)


def ring_gather(piece, devices):
    half = devices // 4
    ring, swap = ring_steps(devices // 2), swap_steps(devices)
    other = lax.ppermute(piece, "seq", swap)
    pieces = {(0, 0): piece, (0, 1): other}
    first, second = piece, other
    for j in range(1, half + 1):
        first = lax.ppermute(first, "seq", ring)
        pieces[-j, 0], pieces[j, 1] = first, lax.ppermute(first, "seq", swap)
        if j < half:
            second = lax.ppermute(second, "seq", ring)
            pieces[-j, 1], pieces[j, 0] = second, lax.ppermute(second, "seq", swap)
    return pieces


def added(*terms):
    return functools.reduce(lambda a, b: a + b, [t.astype(F32) for t in terms])


def ring_scatter_sum(kept, sent, devices):
    half = devices // 4
    back = [(b, a) for a, b in ring_steps(devices // 2)]
    swap = swap_steps(devices)
    got = {j: lax.ppermute(sent[j], "seq", swap) for j in range(half, 0, -1)}
    rows = sent[half].shape[0]
    first, second = [], []
    for j in range(half, 0, -1):
        first = [lax.ppermute(added(kept[j][:rows], got[j][:rows], *first).astype(BF16), "seq", back)]
        if j < half:
            terms = added(kept[j][rows:], got[j][rows:], *second)
            second = [lax.ppermute(terms.astype(BF16), "seq", back)]
    last = lax.ppermute(added(kept[0][rows:], *second).astype(BF16), "seq", swap)
    return added(kept[0][:rows], last, *first).astype(BF16)


def pack_kernel(devices, key_ref, value_ref, id_ref, weight_ref, out_ref):
    rows, width = key_ref.shape
    out_ref[:rows, :width] = key_ref[...]
    out_ref[:rows, width:] = value_ref[...]
    ids = jnp.transpose(id_ref[...].astype(F32))
    weights = jnp.transpose(weight_ref[...])
    by_expert = [
        jnp.sum(jnp.where(ids == e, weights, 0.0), axis=0, keepdims=True) for e in range(devices)
    ]
    in_row = 2 * width // rows
    lines = []
    for first in range(0, devices, in_row):
        lines.append(jnp.concatenate(by_expert[first : first + in_row], axis=1))
    high = [line.astype(BF16).astype(F32) for line in lines]
    low = [line - h for line, h in zip(lines, high)]
    extra = out_ref.shape[0] - rows
    filled = 2 * len(lines)
    if extra > filled:
        low.append(jnp.zeros((extra - filled, 2 * width), F32))
    out_ref[rows:, :] = jnp.concatenate(high + low, axis=0).astype(BF16)


def pack(keys, values, ids, weights, devices):
    rows, width = keys.shape
    lines = 2 * (devices * rows // (2 * width))
    return pl.pallas_call(
        functools.partial(pack_kernel, devices),
        out_shape=jax.ShapeDtypeStruct((rows + -(-lines // 16) * 16, 2 * width), BF16),
        in_specs=[VMEM] * 4,
        out_specs=VMEM,
        compiler_params=PARAMS,
        cost_estimate=pl.CostEstimate(flops=10**6, bytes_accessed=2**19, transcendentals=0),
        name="pack",
    )(keys, values, ids, weights)


def attend_kernel(devices, own_ref, doc_ref, q_ref, *refs):
    names = piece_names(devices)
    kv_refs = refs[: len(names)]
    out_ref, scale_ref, keys, values, bias, lines, sems = refs[len(names) :]
    rows = q_ref.shape[0]
    width = KEY_VALUE_HEADS * HEAD_SIZE
    window = keys.shape[1]
    own = own_ref[0]
    own_doc = doc_ref[own]

    def copies(i, slot):
        start = pl.multiple_of(slot * rows, rows)
        made = []
        for g in range(KEY_VALUE_HEADS):
            for part, buffer in enumerate((keys, values)):
                column = part * width + g * HEAD_SIZE
                made.append(
                    pltpu.make_async_copy(
                        kv_refs[i].at[pl.ds(0, rows), pl.ds(column, HEAD_SIZE)],
                        buffer.at[g, pl.ds(start, rows), pl.ds(0, HEAD_SIZE)],
                        sems.at[i, len(made)],
                    )
                )
        return made

    def line_copy(i):
        extra = lines.shape[1]
        return pltpu.make_async_copy(
            kv_refs[i].at[pl.ds(rows, extra), :], lines.at[i], sems.at[i, 4]
        )

    for i in range(len(names)):
        line_copy(i).start()
    slots, seen = [jnp.int32(0)], [True]
    for c in copies(0, 0):
        c.start()
    filled = jnp.int32(1)
    for i in range(1, len(names)):
        block = block_of(own, names[i], devices)
        shown = (block < own) & ((block == 0) | (doc_ref[block] == own_doc))
        slots.append(filled)
        seen.append(shown)

        @pl.when(shown)
        def _(i=i, slot=filled):
            for c in copies(i, slot):
                c.start()

        filled = filled + shown.astype(jnp.int32)

    for s in range(1, window // rows):

        @pl.when(s >= filled)
        def _(s=s):
            for g in range(KEY_VALUE_HEADS):
                blank = jnp.zeros((rows, HEAD_SIZE), BF16)
                keys[g, s * rows : (s + 1) * rows, :] = blank
                values[g, s * rows : (s + 1) * rows, :HEAD_SIZE] = blank

    lane = lax.broadcasted_iota(jnp.int32, (window, HEAD_SIZE), 1)
    one_column = jnp.where(lane == 0, 1.0, 0.0).astype(BF16)
    for g in range(KEY_VALUE_HEADS):
        values[g, :, HEAD_SIZE:] = one_column
    query_row = lax.broadcasted_iota(jnp.int32, (rows, rows), 0)
    key_row = lax.broadcasted_iota(jnp.int32, (rows, rows), 1)
    bias[:, :rows] = jnp.where(key_row <= query_row, 0.0, -1e30)
    later_row = lax.broadcasted_iota(jnp.int32, (rows, window - rows), 1)
    bias[:, rows:] = jnp.where(later_row < (filled - 1) * rows, 0.0, -1e30)

    for i in range(len(names)):
        line_copy(i).wait()
    count = devices * rows // (2 * width)
    in_row = 2 * width // rows
    line = lax.broadcasted_iota(jnp.int32, (lines.shape[1], 2 * width), 0)
    wanted = (line == own // in_row) | (line == count + own // in_row)
    picked = []
    for i in range(len(names)):
        both = jnp.sum(jnp.where(wanted, lines[i].astype(F32), 0.0), axis=0, keepdims=True)
        picked.append(
            sum(
                jnp.where(own % in_row == n, both[:, n * rows : (n + 1) * rows], 0.0)
                for n in range(in_row)
            )
        )
    picked.append(jnp.zeros((rows - len(names), rows), F32))
    scale_ref[...] = jnp.transpose(jnp.concatenate(picked, axis=0))

    for i in range(len(names)):
        if i == 0:
            for c in copies(0, 0):
                c.wait()
        else:

            @pl.when(seen[i])
            def _(i=i):
                for c in copies(i, slots[i]):
                    c.wait()

    factor = math.log2(math.e) / HEAD_SIZE**0.5
    heads = 4
    for first in range(0, QUERY_HEADS, heads):
        g = first // GROUP
        q = jnp.concatenate(
            [
                q_ref[:, (first + h) * HEAD_SIZE : (first + h + 1) * HEAD_SIZE]
                for h in range(heads)
            ],
            axis=0,
        )
        scores = lax.dot_general(
            q, keys[g], (((1,), (1,)), ((), ())), preferred_element_type=F32
        )
        scores = scores.reshape(heads, rows, window) * factor + bias[...][None]
        top = jnp.max(scores, axis=-1, keepdims=True)
        probs = jnp.exp2(scores - top).astype(BF16).reshape(heads * rows, window)
        summed = jnp.dot(probs, values[g], preferred_element_type=F32)
        result = (summed[:, :HEAD_SIZE] / summed[:, HEAD_SIZE : HEAD_SIZE + 1]).astype(BF16)
        for h in range(heads):
            out_ref[:, (first + h) * HEAD_SIZE : (first + h + 1) * HEAD_SIZE] = result[
                h * rows : (h + 1) * rows
            ]


def attend(own, docs, queries, kv_pieces, devices):
    rows = queries.shape[0]
    window = (min(MOST_BLK, devices) + 1) * rows
    names = piece_names(devices)
    packed = kv_pieces[names[0]]
    return pl.pallas_call(
        functools.partial(attend_kernel, devices),
        out_shape=(
            jax.ShapeDtypeStruct(queries.shape, BF16),
            jax.ShapeDtypeStruct((rows, rows), F32),
        ),
        in_specs=[SMEM, SMEM, VMEM] + [HBM] * len(names),
        out_specs=(VMEM, VMEM),
        scratch_shapes=[
            pltpu.VMEM((KEY_VALUE_HEADS, window, HEAD_SIZE), BF16),
            pltpu.VMEM((KEY_VALUE_HEADS, window, 2 * HEAD_SIZE), BF16),
            pltpu.VMEM((rows, window), F32),
            pltpu.VMEM((len(names), packed.shape[0] - rows, packed.shape[1]), BF16),
            pltpu.SemaphoreType.DMA((len(names), 5)),
        ],
        compiler_params=PARAMS,
        cost_estimate=pl.CostEstimate(
            flops=4 * QUERY_HEADS * rows * window * HEAD_SIZE,
            bytes_accessed=8 * 2**20,
            transcendentals=QUERY_HEADS * rows * window,
        ),
        name="attend",
    )(own, docs, queries, *[kv_pieces[n] for n in names])


def project_kernel(devices, own_ref, att_ref, res_ref, gain_ref, *refs):
    names = piece_names(devices)
    w_refs = refs[: len(names)]
    hidden_ref, normed_ref, weight, sems = refs[len(names) :]
    own = own_ref[0]
    rows = w_refs[0].shape[0]
    copies = []
    for i, name in enumerate(names):
        start = pl.multiple_of(block_of(own, name, devices) * rows, rows)
        copies.append(
            pltpu.make_async_copy(w_refs[i], weight.at[pl.ds(start, rows), :], sems.at[i])
        )
        copies[-1].start()
    for c in copies:
        c.wait()
    hidden = res_ref[...].astype(F32) + jnp.dot(
        att_ref[...], weight[...], preferred_element_type=F32
    )
    hidden_ref[...] = hidden.astype(BF16)
    mean_square = jnp.mean(hidden * hidden, axis=-1, keepdims=True)
    normed_ref[...] = (
        hidden * lax.rsqrt(mean_square + 1e-06) * gain_ref[...].astype(F32)
    ).astype(BF16)


def project(own, attention, residual, gain, w_pieces, devices):
    names = piece_names(devices)
    total = w_pieces[names[0]].shape[0] * devices
    shape = jax.ShapeDtypeStruct(residual.shape, BF16)
    return pl.pallas_call(
        functools.partial(project_kernel, devices),
        out_shape=(shape, shape),
        in_specs=[SMEM, VMEM, VMEM, VMEM] + [HBM] * len(names),
        out_specs=(VMEM, VMEM),
        scratch_shapes=[
            pltpu.VMEM((total, residual.shape[1]), BF16),
            pltpu.SemaphoreType.DMA((len(names),)),
        ],
        compiler_params=PARAMS,
        cost_estimate=pl.CostEstimate(
            flops=2 * residual.shape[0] * total * residual.shape[1],
            bytes_accessed=6 * 2**20,
            transcendentals=0,
        ),
        name="project",
    )(own, attention, residual, gain.reshape(1, -1), *[w_pieces[n] for n in names])


def expert_kernel(first, count, scale_ref, gate_ref, up_ref, down_ref, *refs):
    x_refs = refs[:count]
    kept_ref, sent_ref = refs[count : count + 2]
    rows = x_refs[0].shape[0]
    x = jnp.concatenate([r[...] for r in x_refs], axis=0)
    gate_part = jnp.dot(x, gate_ref[...], preferred_element_type=F32)
    up_part = jnp.dot(x, up_ref[...], preferred_element_type=F32)
    activated = (gate_part / (1.0 + jnp.exp(-gate_part)) * up_part).astype(BF16)
    produced = jnp.dot(activated, down_ref[...], preferred_element_type=F32)
    kept = kept_ref.shape[0] // rows
    for i in range(count):
        part = (
            produced[i * rows : (i + 1) * rows] * scale_ref[:, first + i : first + i + 1]
        ).astype(BF16)
        if i < kept:
            kept_ref[i * rows : (i + 1) * rows, :] = part
        else:
            sent_ref[(i - kept) * rows : (i - kept + 1) * rows, :] = part


def expert(scale, gate_proj, up_proj, down_proj, first, pieces, kept):
    count = len(pieces)
    rows, width = pieces[0].shape
    sent = max(count - kept, 1)
    return pl.pallas_call(
        functools.partial(expert_kernel, first, count),
        out_shape=(
            jax.ShapeDtypeStruct((kept * rows, width), BF16),
            jax.ShapeDtypeStruct((sent * rows if count > kept else 16, width), BF16),
        ),
        in_specs=[VMEM] * (4 + count),
        out_specs=(VMEM, VMEM),
        compiler_params=PARAMS,
        cost_estimate=pl.CostEstimate(
            flops=6 * count * rows * gate_proj.shape[0] * gate_proj.shape[1],
            bytes_accessed=4 * 2**20,
            transcendentals=count * rows * gate_proj.shape[1],
        ),
        name="expert",
    )(scale, gate_proj, up_proj, down_proj, *pieces)


def shards(
    queries,
    token_key_heads,
    token_value_heads,
    residual,
    out_weight,
    norm_gain,
    w_gate,
    w_up,
    w_down,
    expert_ids,
    gate_weights,
    doc_of_block,
):
    devices = lax.axis_size("seq")
    own = lax.axis_index("seq").astype(jnp.int32).reshape(1)
    packed = pack(token_key_heads, token_value_heads, expert_ids, gate_weights, devices)
    kv_pieces = ring_gather(packed, devices)
    w_pieces = ring_gather(out_weight, devices)
    attention, scales = attend(own, doc_of_block, queries, kv_pieces, devices)
    hidden, normed = project(own, attention, residual, norm_gain, w_pieces, devices)

    tokens = ring_gather(normed, devices)
    kept, sent = {}, {}
    first = 0
    for j, group in enumerate(piece_groups(devices // 2)):
        pieces = [tokens[name] for name in group]
        stays = len(pieces) if j == 0 else len(pieces) // 2
        kept[j], sent[j] = expert(scales, w_gate[0], w_up[0], w_down[0], first, pieces, stays)
        first += len(pieces)
    mix = ring_scatter_sum(kept, sent, devices)
    return (attention, hidden, mix)


def solution(mesh):
    in_specs = (
        P(("pack", "seq"), None),
        P(("pack", "seq"), None),
        P(("pack", "seq"), None),
        P(("pack", "seq"), None),
        P("seq", None),
        P(),
        P("seq", None, None),
        P("seq", None, None),
        P("seq", None, None),
        P(("pack", "seq"), None),
        P(("pack", "seq"), None),
        P("pack"),
    )
    out_specs = (P(("pack", "seq"), None), P(("pack", "seq"), None), P(("pack", "seq"), None))
    return jax.shard_map(shards, mesh=mesh, in_specs=in_specs, out_specs=out_specs, check_vma=False)
```

time: 164 us -> 143 us (0.87); the launches traced: 162 us -> 143 us
  local copies, waits for them, and re-layouts: 52.6 us -> 9.03 us
  Pallas kernels: 17.8 us -> 35.6 us
  starting transfers between devices: 39.4 us -> 48.5 us
  waiting for transfers between devices: 47.9 us -> 45.9 us
    unnamed x113 -> x102, local copies, waits for them, and re-layouts: 34.9 us -> 8.44 us
    pallas_call x5, Pallas kernels: 8.53 us -> 21.1 us  [expert(): pl.pallas_call(functools.partial(expert_kernel, first, count), out_shape=...]
    slice x28 -> x0, local copies, waits for them, and re-layouts: 11.2 us -> none  [the longest x21 8.15 us: shards(): p[rows:rows + extra]]
    ppermute x64 -> x57, starting transfers between devices: 39.4 us -> 48.5 us  [the longest x12 19.4 us: ring_gather(): first = lax.ppermute(first, 'seq', ring)]
    pallas_call x2 -> x3, Pallas kernels: 9.25 us -> 14.5 us  [the longest x1 7.85 us: attend(): pl.pallas_call(functools.partial(attend_kernel, devices), out_shape=(jax....]
    another operation x16 -> x0, local copies, waits for them, and re-layouts: 4.06 us -> none  [shards(): jnp.stack([p[rows:rows + extra] for pair in kv_pieces for p in pair])]
    ppermute x64 -> x57, waiting for transfers between devices: 47.9 us -> 45.9 us  [the longest x12 23.3 us: ring_gather(): first = lax.ppermute(first, 'seq', ring)]
  transfers between devices with their start and end apart: 64 -> 57, of which waited for: 21 -> 20; matrix products, arithmetic and copies ran while one was open for 16% -> 3% of each run, Pallas kernels for 9% -> 21%
where the time goes in v2:
time: 143 us
  starting transfers between devices  48.5 us (34%)
  waiting for transfers between devices  45.9 us (32%)
  Pallas kernels  35.6 us (25%)
  local copies, waits for them, and re-layouts  9.03 us (6%)
  other arithmetic  2.69 us (2%)
    ppermute x12, waiting for transfers between devices, ring_gather(): first = lax.ppermute(first, 'seq', ring)  23.3 us
    pallas_call x5, Pallas kernels, expert(): pl.pallas_call(functools.partial(expert_kernel, first, count), out_shape=...  21.1 us
    ppermute x12, starting transfers between devices, ring_gather(): first = lax.ppermute(first, 'seq', ring)  19.4 us
    ppermute x9, starting transfers between devices, ring_gather(): second = lax.ppermute(second, 'seq', ring)  13 us
    ppermute x9, waiting for transfers between devices, ring_gather(): second = lax.ppermute(second, 'seq', ring)  11.3 us
    unnamed x102, local copies, waits for them, and re-layouts  8.44 us
    pallas_call x1, Pallas kernels, attend(): pl.pallas_call(functools.partial(attend_kernel, devices), out_shape=(jax....  7.85 us
    ppermute x4, waiting for transfers between devices, ring_scatter_sum(): lax.ppermute(added(kept[j][:rows], got[j][:rows], *first).astype(BF16), '...  6.63 us
  transfers between devices with their start and end apart: 57, of which 20 were waited for; matrix products, arithmetic and copies ran while one was open for 3% of the time, Pallas kernels for 21%

profile of v2, /device:TPU:0, one launch (start us, length us, event | category | flops | bytes accessed | tf_op | source)
XLA Modules:
  0.0 142.9 jit_solution(17076341054322982431)
XLA Ops:
  1.2 2.6 %collective-permute-start.16 = (bf16[128,1024]{1,0:T(8,128)(2,1)}, bf16[128,1024]{1,0:T(8,128)(2,1)S(1)}, u32[]{:S(2)}, u32[]{:S(2)}) collective-permute-start(bf16[128,1024]{1,0:T(8,128)(2,1)} %refs_0_.1), channel_id=1, source_target_pairs={{0,4},{1,3},{4,8},{5,1},{8,12},{9,5},{12,14},{13,9},{14,10},{15,13... | collective-permute-start | bytes 786440 | tf_op jit(solution)/shard_map/ppermute | solution.py:65
  5.9 1.7 %pack.1.refs_0_ = bf16[144,512]{1,0:T(8,128)(2,1)} custom-call(bf16[128,256]{1,0:T(8,128)(2,1)} %key_ref.1, bf16[128,256]{1,0:T(8,128)(2,1)} %value_ref.1, s32[128,8]{1,0:T(8,128)} %copy.15.id_ref, f32[128,8]{1,0:T(8,128)} %copy.16.weight_ref), custom_call_target="tpu_custom_call" | custom-call | flops 1000000 | bytes 524288 | tf_op jit(solution)/shard_map/pack/pallas_call | solution.py:118
  9.2 1.6 %collective-permute-start.2 = (bf16[144,512]{1,0:T(8,128)(2,1)S(1)}, bf16[144,512]{1,0:T(8,128)(2,1)S(1)}, u32[]{:S(2)}, u32[]{:S(2)}) collective-permute-start(bf16[144,512]{1,0:T(8,128)(2,1)S(1)} %collective-permute-done.refs_1_), channel_id=1, source_target_pairs={{0,4},{1,3},{4,8},{5,1},{8,12},{9,5},{12,14},{13,9},{14,10},{15,13... | collective-permute-start | bytes 442376 | tf_op jit(solution)/shard_map/ppermute | solution.py:68
  10.8 2.3 %collective-permute-done.1.refs_2_ = bf16[144,512]{1,0:T(8,128)(2,1)S(1)} collective-permute-done((bf16[144,512]{1,0:T(8,128)(2,1)}, bf16[144,512]{1,0:T(8,128)(2,1)S(1)}, u32[]{:S(2)}, u32[]{:S(2)}) %collective-permute-start.1) | collective-permute-done | bytes 147488 | tf_op jit(solution)/shard_map/ppermute | solution.py:65
  14.7 1.6 %collective-permute-start.20 = (bf16[128,1024]{1,0:T(8,128)(2,1)S(1)}, bf16[128,1024]{1,0:T(8,128)(2,1)S(1)}, u32[]{:S(2)}, u32[]{:S(2)}) collective-permute-start(bf16[128,1024]{1,0:T(8,128)(2,1)S(1)} %collective-permute-done.16.refs_2_), channel_id=1, source_target_pairs={{0,4},{1,3},{4,8},{5,1},{8,12},{9,5},{12,14},{13,9},{14,10},{15,13... | collective-permute-start | bytes 786440 | tf_op jit(solution)/shard_map/ppermute | solution.py:65
  18.5 5.4 %collective-permute-done.5.refs_6_ = bf16[144,512]{1,0:T(8,128)(2,1)S(1)} collective-permute-done((bf16[144,512]{1,0:T(8,128)(2,1)S(1)}, bf16[144,512]{1,0:T(8,128)(2,1)S(1)}, u32[]{:S(2)}, u32[]{:S(2)}) %collective-permute-start.5) | collective-permute-done | bytes 147488 | tf_op jit(solution)/shard_map/ppermute | solution.py:65
  27.0 1.6 %collective-permute-start.21 = (bf16[128,1024]{1,0:T(8,128)(2,1)S(1)}, bf16[128,1024]{1,0:T(8,128)(2,1)S(1)}, u32[]{:S(2)}, u32[]{:S(2)}) collective-permute-start(bf16[128,1024]{1,0:T(8,128)(2,1)S(1)} %collective-permute-done.17.refs_3_), channel_id=1, source_target_pairs={{0,4},{1,3},{4,8},{5,1},{8,12},{9,5},{12,14},{13,9},{14,10},{15,13... | collective-permute-start | bytes 786440 | tf_op jit(solution)/shard_map/ppermute | solution.py:68
  32.2 1.6 %collective-permute-start.13 = (bf16[144,512]{1,0:T(8,128)(2,1)S(1)}, bf16[144,512]{1,0:T(8,128)(2,1)S(1)}, u32[]{:S(2)}, u32[]{:S(2)}) collective-permute-start(bf16[144,512]{1,0:T(8,128)(2,1)S(1)} %collective-permute-done.9.refs_10_), channel_id=1, source_target_pairs={{0,4},{1,3},{4,8},{5,1},{8,12},{9,5},{12,14},{13,9},{14,10},{15,13... | collective-permute-start | bytes 442376 | tf_op jit(solution)/shard_map/ppermute | solution.py:65
  33.8 4.1 %collective-permute-done.10.refs_11_ = bf16[144,512]{1,0:T(8,128)(2,1)S(1)} collective-permute-done((bf16[144,512]{1,0:T(8,128)(2,1)S(1)}, bf16[144,512]{1,0:T(8,128)(2,1)S(1)}, u32[]{:S(2)}, u32[]{:S(2)}) %collective-permute-start.10) | collective-permute-done | bytes 147488 | tf_op jit(solution)/shard_map/ppermute | solution.py:68
  39.4 1.6 %collective-permute-start.28 = (bf16[128,1024]{1,0:T(8,128)(2,1)S(1)}, bf16[128,1024]{1,0:T(8,128)(2,1)S(1)}, u32[]{:S(2)}, u32[]{:S(2)}) collective-permute-start(bf16[128,1024]{1,0:T(8,128)(2,1)S(1)} %collective-permute-done.24.refs_10_), channel_id=1, source_target_pairs={{0,4},{1,3},{4,8},{5,1},{8,12},{9,5},{12,14},{13,9},{14,10},{15,13... | collective-permute-start | bytes 786440 | tf_op jit(solution)/shard_map/ppermute | solution.py:65
  44.3 2.8 %collective-permute-done.28.refs_14_ = bf16[128,1024]{1,0:T(8,128)(2,1)S(1)} collective-permute-done((bf16[128,1024]{1,0:T(8,128)(2,1)S(1)}, bf16[128,1024]{1,0:T(8,128)(2,1)S(1)}, u32[]{:S(2)}, u32[]{:S(2)}) %collective-permute-start.28) | collective-permute-done | bytes 262176 | tf_op jit(solution)/shard_map/ppermute | solution.py:65
  48.6 7.8 %attend.1 = (bf16[128,2048]{1,0:T(8,128)(2,1)}, f32[128,128]{1,0:T(8,128)}) custom-call(s32[1]{0:T(128)} %bitcast.own_ref, s32[16]{0:T(128)} %doc_ref.1, bf16[128,2048]{1,0:T(8,128)(2,1)} %q_ref.1, bf16[144,512]{1,0:T(8,128)(2,1)} %pack.1.refs_0_, bf16[144,512]{1,0:T(8,128)(2,1)} %copy-done.35, bf16[144,512]{1,0:T(8,128)(2,1)} %copy-done.36, ...), custom_call_target="tpu_custom_call" | custom-call | flops 1207959552 | bytes 8388608 | tf_op jit(solution)/shard_map/attend/pallas_call | solution.py:257
  57.4 4.9 %project.1 = (bf16[128,1024]{1,0:T(8,128)(2,1)}, bf16[128,1024]{1,0:T(8,128)(2,1)}) custom-call(s32[1]{0:T(128)} %bitcast.own_ref, bf16[128,2048]{1,0:T(8,128)(2,1)} %get-tuple-element.13.att_ref, bf16[128,1024]{1,0:T(8,128)(2,1)} %res_ref.1, bf16[1,1024]{1,0:T(2,128)(2,1)} %reshape.13.gain_ref, bf16[128,1024]{1,0:T(8,128)(2,1)} %refs_0_.1, ...), custom_call_target="tpu_custom_call" | custom-call | flops 536870912 | bytes 6291456 | tf_op jit(solution)/shard_map/project/pallas_call | solution.py:311
  64.2 4.8 %collective-permute-done.31.refs_0_ = bf16[128,1024]{1,0:T(8,128)(2,1)S(1)} collective-permute-done((bf16[128,1024]{1,0:T(8,128)(2,1)}, bf16[128,1024]{1,0:T(8,128)(2,1)S(1)}, u32[]{:S(2)}, u32[]{:S(2)}) %collective-permute-start.31) | collective-permute-done | bytes 262176 | tf_op jit(solution)/shard_map/ppermute | solution.py:65
  70.5 1.7 %collective-permute-start.32 = (bf16[128,1024]{1,0:T(8,128)(2,1)S(1)}, bf16[128,1024]{1,0:T(8,128)(2,1)S(1)}, u32[]{:S(2)}, u32[]{:S(2)}) collective-permute-start(bf16[128,1024]{1,0:T(8,128)(2,1)S(1)} %collective-permute-done.30.refs_1_), channel_id=1, source_target_pairs={{0,4},{1,3},{4,8},{5,1},{8,12},{9,5},{12,14},{13,9},{14,10},{15,13... | collective-permute-start | bytes 786440 | tf_op jit(solution)/shard_map/ppermute | solution.py:68
  72.2 3.2 %collective-permute-done.36.refs_0_ = bf16[128,1024]{1,0:T(8,128)(2,1)S(1)} collective-permute-done((bf16[128,1024]{1,0:T(8,128)(2,1)S(1)}, bf16[128,1024]{1,0:T(8,128)(2,1)S(1)}, u32[]{:S(2)}, u32[]{:S(2)}) %collective-permute-start.36) | collective-permute-done | bytes 262176 | tf_op jit(solution)/shard_map/ppermute | solution.py:65
  79.7 2.1 %collective-permute-done.41.refs_0_ = bf16[128,1024]{1,0:T(8,128)(2,1)S(1)} collective-permute-done((bf16[128,1024]{1,0:T(8,128)(2,1)S(1)}, bf16[128,1024]{1,0:T(8,128)(2,1)S(1)}, u32[]{:S(2)}, u32[]{:S(2)}) %collective-permute-start.41) | collective-permute-done | bytes 262176 | tf_op jit(solution)/shard_map/ppermute | solution.py:65
  86.0 2.1 %collective-permute-done.50.refs_0_ = bf16[128,1024]{1,0:T(8,128)(2,1)S(1)} collective-permute-done((bf16[128,1024]{1,0:T(8,128)(2,1)S(1)}, bf16[128,1024]{1,0:T(8,128)(2,1)S(1)}, u32[]{:S(2)}, u32[]{:S(2)}) %collective-permute-start.50) | collective-permute-done | bytes 262176 | tf_op jit(solution)/shard_map/ppermute | solution.py:65
  88.6 2.3 %collective-permute-done.42.refs_1_ = bf16[128,1024]{1,0:T(8,128)(2,1)S(1)} collective-permute-done((bf16[128,1024]{1,0:T(8,128)(2,1)S(1)}, bf16[128,1024]{1,0:T(8,128)(2,1)S(1)}, u32[]{:S(2)}, u32[]{:S(2)}) %collective-permute-start.42) | collective-permute-done | bytes 262176 | tf_op jit(solution)/shard_map/ppermute | solution.py:68
  91.7 3.6 %expert.9 = (bf16[128,1024]{1,0:T(8,128)(2,1)}, bf16[128,1024]{1,0:T(8,128)(2,1)}) custom-call(f32[128,128]{1,0:T(8,128)} %get-tuple-element.18.scale_ref, bf16[1024,384]{1,0:T(8,128)(2,1)} %bitcast.4, bf16[1024,384]{1,0:T(8,128)(2,1)} %bitcast.9, bf16[384,1024]{1,0:T(8,128)(2,1)} %bitcast.14, bf16[128,1024]{1,0:T(8,128)(2,1)} %copy-done.19, ...), custom_call_target="tpu_custom_call" | custom-call | flops 603979776 | bytes 4194304 | tf_op jit(solution)/shard_map/expert/pallas_call | solution.py:354
  97.2 4.6 %expert.8 = (bf16[256,1024]{1,0:T(8,128)(2,1)}, bf16[256,1024]{1,0:T(8,128)(2,1)}) custom-call(f32[128,128]{1,0:T(8,128)} %get-tuple-element.18.scale_ref, bf16[1024,384]{1,0:T(8,128)(2,1)} %bitcast.5, bf16[1024,384]{1,0:T(8,128)(2,1)} %bitcast.10, bf16[384,1024]{1,0:T(8,128)(2,1)} %bitcast.15, bf16[128,1024]{1,0:T(8,128)(2,1)} %copy-done.27, ...), custom_call_target="tpu_custom_call" | custom-call | flops 1207959552 | bytes 4194304 | tf_op jit(solution)/shard_map/expert/pallas_call | solution.py:354
  102.5 1.6 %collective-permute-start.53 = (bf16[128,1024]{1,0:T(8,128)(2,1)S(1)}, bf16[128,1024]{1,0:T(8,128)(2,1)S(1)}, u32[]{:S(2)}, u32[]{:S(2)}) collective-permute-start(bf16[128,1024]{1,0:T(8,128)(2,1)S(1)} %add_convert_fusion.4), channel_id=1, source_target_pairs={{4,0},{3,1},{8,4},{1,5},{12,8},{5,9},{14,12},{9,13},{10,14},{13,15... | collective-permute-start | bytes 786440 | tf_op jit(solution)/shard_map/ppermute | solution.py:85
  105.6 4.6 %expert.7 = (bf16[256,1024]{1,0:T(8,128)(2,1)}, bf16[256,1024]{1,0:T(8,128)(2,1)}) custom-call(f32[128,128]{1,0:T(8,128)} %get-tuple-element.18.scale_ref, bf16[1024,384]{1,0:T(8,128)(2,1)} %bitcast.6, bf16[1024,384]{1,0:T(8,128)(2,1)} %bitcast.11, bf16[384,1024]{1,0:T(8,128)(2,1)} %bitcast.16, bf16[128,1024]{1,0:T(8,128)(2,1)} %copy-done.25, ...), custom_call_target="tpu_custom_call" | custom-call | flops 1207959552 | bytes 4194304 | tf_op jit(solution)/shard_map/expert/pallas_call | solution.py:354
  111.1 1.6 %collective-permute-start.46 = (bf16[128,1024]{1,0:T(8,128)(2,1)S(1)}, bf16[128,1024]{1,0:T(8,128)(2,1)S(1)}, u32[]{:S(2)}, u32[]{:S(2)}) collective-permute-start(bf16[128,1024]{1,0:T(8,128)(2,1)S(1)} %get-tuple-element.33), channel_id=1, source_target_pairs={{4,0},{3,1},{8,4},{1,5},{12,8},{5,9},{14,12},{9,13},{10,14},{13,15... | collective-permute-start | bytes 786440 | tf_op jit(solution)/shard_map/ppermute | solution.py:88
  112.7 1.7 %collective-permute-start.54 = (bf16[128,1024]{1,0:T(8,128)(2,1)S(1)}, bf16[128,1024]{1,0:T(8,128)(2,1)S(1)}, u32[]{:S(2)}, u32[]{:S(2)}) collective-permute-start(bf16[128,1024]{1,0:T(8,128)(2,1)S(1)} %get-tuple-element.34), channel_id=1, source_target_pairs={{4,0},{3,1},{8,4},{1,5},{12,8},{5,9},{14,12},{9,13},{10,14},{13,15... | collective-permute-start | bytes 786440 | tf_op jit(solution)/shard_map/ppermute | solution.py:85
  115.9 4.6 %expert.6 = (bf16[256,1024]{1,0:T(8,128)(2,1)}, bf16[256,1024]{1,0:T(8,128)(2,1)}) custom-call(f32[128,128]{1,0:T(8,128)} %get-tuple-element.18.scale_ref, bf16[1024,384]{1,0:T(8,128)(2,1)} %bitcast.7, bf16[1024,384]{1,0:T(8,128)(2,1)} %bitcast.12, bf16[384,1024]{1,0:T(8,128)(2,1)} %bitcast.17, bf16[128,1024]{1,0:T(8,128)(2,1)} %copy-done.23, ...), custom_call_target="tpu_custom_call" | custom-call | flops 1207959552 | bytes 4194304 | tf_op jit(solution)/shard_map/expert/pallas_call | solution.py:354
  120.8 1.7 %collective-permute-start.47 = (bf16[128,1024]{1,0:T(8,128)(2,1)S(1)}, bf16[128,1024]{1,0:T(8,128)(2,1)S(1)}, u32[]{:S(2)}, u32[]{:S(2)}) collective-permute-start(bf16[128,1024]{1,0:T(8,128)(2,1)S(1)} %get-tuple-element.31), channel_id=1, source_target_pairs={{4,0},{3,1},{8,4},{1,5},{12,8},{5,9},{14,12},{9,13},{10,14},{13,15... | collective-permute-start | bytes 786440 | tf_op jit(solution)/shard_map/ppermute | solution.py:88
  123.9 3.3 %collective-permute-done.47 = bf16[128,1024]{1,0:T(8,128)(2,1)S(1)} collective-permute-done((bf16[128,1024]{1,0:T(8,128)(2,1)S(1)}, bf16[128,1024]{1,0:T(8,128)(2,1)S(1)}, u32[]{:S(2)}, u32[]{:S(2)}) %collective-permute-start.47) | collective-permute-done | bytes 262176 | tf_op jit(solution)/shard_map/ppermute | solution.py:88
  127.2 2.8 %collective-permute-done.55 = bf16[128,1024]{1,0:T(8,128)(2,1)S(1)} collective-permute-done((bf16[128,1024]{1,0:T(8,128)(2,1)S(1)}, bf16[128,1024]{1,0:T(8,128)(2,1)S(1)}, u32[]{:S(2)}, u32[]{:S(2)}) %collective-permute-start.55) | collective-permute-done | bytes 262176 | tf_op jit(solution)/shard_map/ppermute | solution.py:85
  130.3 1.7 %collective-permute-start.48 = (bf16[128,1024]{1,0:T(8,128)(2,1)S(1)}, bf16[128,1024]{1,0:T(8,128)(2,1)S(1)}, u32[]{:S(2)}, u32[]{:S(2)}) collective-permute-start(bf16[128,1024]{1,0:T(8,128)(2,1)S(1)} %get-tuple-element.29), channel_id=1, source_target_pairs={{4,0},{3,1},{8,4},{1,5},{12,8},{5,9},{14,12},{9,13},{10,14},{13,15... | collective-permute-start | bytes 786440 | tf_op jit(solution)/shard_map/ppermute | solution.py:88
  132.0 3.6 %expert.5 = (bf16[256,1024]{1,0:T(8,128)(2,1)}, bf16[16,1024]{1,0:T(8,128)(2,1)}) custom-call(f32[128,128]{1,0:T(8,128)} %get-tuple-element.18.scale_ref, bf16[1024,384]{1,0:T(8,128)(2,1)} %bitcast.8, bf16[1024,384]{1,0:T(8,128)(2,1)} %bitcast.13, bf16[384,1024]{1,0:T(8,128)(2,1)} %bitcast.18, bf16[128,1024]{1,0:T(8,128)(2,1)} %get-tuple-element.19.refs_0_, ...), custom_call_target="tpu_custom_call" | custom-call | flops 603979776 | bytes 4194304 | tf_op jit(solution)/shard_map/expert/pallas_call | solution.py:354
  138.2 3.8 %collective-permute-done.56 = bf16[128,1024]{1,0:T(8,128)(2,1)S(1)} collective-permute-done((bf16[128,1024]{1,0:T(8,128)(2,1)S(1)}, bf16[128,1024]{1,0:T(8,128)(2,1)S(1)}, u32[]{:S(2)}, u32[]{:S(2)}) %collective-permute-start.56) | collective-permute-done | bytes 262176 | tf_op jit(solution)/shard_map/ppermute | solution.py:85
  (199 shorter events, 46.5 us)
Async XLA Ops:
  0.6 12.5 %collective-permute-start.15 = (bf16[128,1024]{1,0:T(8,128)(2,1)}, bf16[128,1024]{1,0:T(8,128)(2,1)S(1)}, u32[]{:S(2)}, u32[]{:S(2)}) collective-permute-start(bf16[128,1024]{1,0:T(8,128)(2,1)} %refs_0_.1), channel_id=1, source_target_pairs={{0,1},{1,0},{2,3},{3,2},{4,5},{5,4},{6,7},{7,6},{8,9},{9,8},{10,11... | collective-permute-start | bytes 786440 | tf_op jit(solution)/shard_map/ppermute | solution.py:61
  1.2 13.5 %collective-permute-start.16 = (bf16[128,1024]{1,0:T(8,128)(2,1)}, bf16[128,1024]{1,0:T(8,128)(2,1)S(1)}, u32[]{:S(2)}, u32[]{:S(2)}) collective-permute-start(bf16[128,1024]{1,0:T(8,128)(2,1)} %refs_0_.1), channel_id=1, source_target_pairs={{0,4},{1,3},{4,8},{5,1},{8,12},{9,5},{12,14},{13,9},{14,10},{15,13... | collective-permute-start | bytes 786440 | tf_op jit(solution)/shard_map/ppermute | solution.py:65
  9.2 8.5 %collective-permute-start.2 = (bf16[144,512]{1,0:T(8,128)(2,1)S(1)}, bf16[144,512]{1,0:T(8,128)(2,1)S(1)}, u32[]{:S(2)}, u32[]{:S(2)}) collective-permute-start(bf16[144,512]{1,0:T(8,128)(2,1)S(1)} %collective-permute-done.refs_1_), channel_id=1, source_target_pairs={{0,4},{1,3},{4,8},{5,1},{8,12},{9,5},{12,14},{13,9},{14,10},{15,13... | collective-permute-start | bytes 442376 | tf_op jit(solution)/shard_map/ppermute | solution.py:68
  13.1 13.9 %collective-permute-start.17 = (bf16[128,1024]{1,0:T(8,128)(2,1)S(1)}, bf16[128,1024]{1,0:T(8,128)(2,1)S(1)}, u32[]{:S(2)}, u32[]{:S(2)}) collective-permute-start(bf16[128,1024]{1,0:T(8,128)(2,1)S(1)} %collective-permute-done.15.refs_1_), channel_id=1, source_target_pairs={{0,4},{1,3},{4,8},{5,1},{8,12},{9,5},{12,14},{13,9},{14,10},{15,13... | collective-permute-start | bytes 786440 | tf_op jit(solution)/shard_map/ppermute | solution.py:68
  14.7 13.9 %collective-permute-start.20 = (bf16[128,1024]{1,0:T(8,128)(2,1)S(1)}, bf16[128,1024]{1,0:T(8,128)(2,1)S(1)}, u32[]{:S(2)}, u32[]{:S(2)}) collective-permute-start(bf16[128,1024]{1,0:T(8,128)(2,1)S(1)} %collective-permute-done.16.refs_2_), channel_id=1, source_target_pairs={{0,4},{1,3},{4,8},{5,1},{8,12},{9,5},{12,14},{13,9},{14,10},{15,13... | collective-permute-start | bytes 786440 | tf_op jit(solution)/shard_map/ppermute | solution.py:65
  16.2 7.7 %collective-permute-start.5 = (bf16[144,512]{1,0:T(8,128)(2,1)S(1)}, bf16[144,512]{1,0:T(8,128)(2,1)S(1)}, u32[]{:S(2)}, u32[]{:S(2)}) collective-permute-start(bf16[144,512]{1,0:T(8,128)(2,1)S(1)} %collective-permute-done.1.refs_2_), channel_id=1, source_target_pairs={{0,4},{1,3},{4,8},{5,1},{8,12},{9,5},{12,14},{13,9},{14,10},{15,13... | collective-permute-start | bytes 442376 | tf_op jit(solution)/shard_map/ppermute | solution.py:65
  17.8 7.7 %collective-permute-start.6 = (bf16[144,512]{1,0:T(8,128)(2,1)S(1)}, bf16[144,512]{1,0:T(8,128)(2,1)S(1)}, u32[]{:S(2)}, u32[]{:S(2)}) collective-permute-start(bf16[144,512]{1,0:T(8,128)(2,1)S(1)} %collective-permute-done.2.refs_3_), channel_id=1, source_target_pairs={{0,4},{1,3},{4,8},{5,1},{8,12},{9,5},{12,14},{13,9},{14,10},{15,13... | collective-permute-start | bytes 442376 | tf_op jit(solution)/shard_map/ppermute | solution.py:68
  24.0 8.2 %collective-permute-start.18 = (bf16[128,1024]{1,0:T(8,128)(2,1)S(1)}, bf16[128,1024]{1,0:T(8,128)(2,1)S(1)}, u32[]{:S(2)}, u32[]{:S(2)}) collective-permute-start(bf16[128,1024]{1,0:T(8,128)(2,1)S(1)} %collective-permute-done.16.refs_2_), channel_id=1, source_target_pairs={{0,1},{1,0},{2,3},{3,2},{4,5},{5,4},{6,7},{7,6},{8,9},{9,8},{10,11... | collective-permute-start | bytes 786440 | tf_op jit(solution)/shard_map/ppermute | solution.py:66
  27.0 10.9 %collective-permute-start.21 = (bf16[128,1024]{1,0:T(8,128)(2,1)S(1)}, bf16[128,1024]{1,0:T(8,128)(2,1)S(1)}, u32[]{:S(2)}, u32[]{:S(2)}) collective-permute-start(bf16[128,1024]{1,0:T(8,128)(2,1)S(1)} %collective-permute-done.17.refs_3_), channel_id=1, source_target_pairs={{0,4},{1,3},{4,8},{5,1},{8,12},{9,5},{12,14},{13,9},{14,10},{15,13... | collective-permute-start | bytes 786440 | tf_op jit(solution)/shard_map/ppermute | solution.py:68
  28.6 10.8 %collective-permute-start.24 = (bf16[128,1024]{1,0:T(8,128)(2,1)S(1)}, bf16[128,1024]{1,0:T(8,128)(2,1)S(1)}, u32[]{:S(2)}, u32[]{:S(2)}) collective-permute-start(bf16[128,1024]{1,0:T(8,128)(2,1)S(1)} %collective-permute-done.20.refs_6_), channel_id=1, source_target_pairs={{0,4},{1,3},{4,8},{5,1},{8,12},{9,5},{12,14},{13,9},{14,10},{15,13... | collective-permute-start | bytes 786440 | tf_op jit(solution)/shard_map/ppermute | solution.py:65
  30.7 7.2 %collective-permute-start.10 = (bf16[144,512]{1,0:T(8,128)(2,1)S(1)}, bf16[144,512]{1,0:T(8,128)(2,1)S(1)}, u32[]{:S(2)}, u32[]{:S(2)}) collective-permute-start(bf16[144,512]{1,0:T(8,128)(2,1)S(1)} %collective-permute-done.6.refs_7_), channel_id=1, source_target_pairs={{0,4},{1,3},{4,8},{5,1},{8,12},{9,5},{12,14},{13,9},{14,10},{15,13... | collective-permute-start | bytes 442376 | tf_op jit(solution)/shard_map/ppermute | solution.py:68
  32.1 8.8 %collective-permute-start.11 = (bf16[144,512]{1,0:T(8,128)(2,1)S(1)}, bf16[144,512]{1,0:T(8,128)(2,1)S(1)}, u32[]{:S(2)}, u32[]{:S(2)}) collective-permute-start(bf16[144,512]{1,0:T(8,128)(2,1)S(1)} %collective-permute-done.9.refs_10_), channel_id=1, source_target_pairs={{0,1},{1,0},{2,3},{3,2},{4,5},{5,4},{6,7},{7,6},{8,9},{9,8},{10,11... | collective-permute-start | bytes 442376 | tf_op jit(solution)/shard_map/ppermute | solution.py:66
  32.2 8.8 %collective-permute-start.13 = (bf16[144,512]{1,0:T(8,128)(2,1)S(1)}, bf16[144,512]{1,0:T(8,128)(2,1)S(1)}, u32[]{:S(2)}, u32[]{:S(2)}) collective-permute-start(bf16[144,512]{1,0:T(8,128)(2,1)S(1)} %collective-permute-done.9.refs_10_), channel_id=1, source_target_pairs={{0,4},{1,3},{4,8},{5,1},{8,12},{9,5},{12,14},{13,9},{14,10},{15,13... | collective-permute-start | bytes 442376 | tf_op jit(solution)/shard_map/ppermute | solution.py:65
  37.9 6.4 %collective-permute-start.25 = (bf16[128,1024]{1,0:T(8,128)(2,1)S(1)}, bf16[128,1024]{1,0:T(8,128)(2,1)S(1)}, u32[]{:S(2)}, u32[]{:S(2)}) collective-permute-start(bf16[128,1024]{1,0:T(8,128)(2,1)S(1)} %collective-permute-done.21.refs_7_), channel_id=1, source_target_pairs={{0,4},{1,3},{4,8},{5,1},{8,12},{9,5},{12,14},{13,9},{14,10},{15,13... | collective-permute-start | bytes 786440 | tf_op jit(solution)/shard_map/ppermute | solution.py:68
  39.4 7.7 %collective-permute-start.28 = (bf16[128,1024]{1,0:T(8,128)(2,1)S(1)}, bf16[128,1024]{1,0:T(8,128)(2,1)S(1)}, u32[]{:S(2)}, u32[]{:S(2)}) collective-permute-start(bf16[128,1024]{1,0:T(8,128)(2,1)S(1)} %collective-permute-done.24.refs_10_), channel_id=1, source_target_pairs={{0,4},{1,3},{4,8},{5,1},{8,12},{9,5},{12,14},{13,9},{14,10},{15,13... | collective-permute-start | bytes 786440 | tf_op jit(solution)/shard_map/ppermute | solution.py:65
  42.4 14.1 %collective-permute-start.22 = (bf16[128,1024]{1,0:T(8,128)(2,1)S(1)}, bf16[128,1024]{1,0:T(8,128)(2,1)S(1)}, u32[]{:S(2)}, u32[]{:S(2)}) collective-permute-start(bf16[128,1024]{1,0:T(8,128)(2,1)S(1)} %collective-permute-done.20.refs_6_), channel_id=1, source_target_pairs={{0,1},{1,0},{2,3},{3,2},{4,5},{5,4},{6,7},{7,6},{8,9},{9,8},{10,11... | collective-permute-start | bytes 786440 | tf_op jit(solution)/shard_map/ppermute | solution.py:66
  42.6 13.9 %collective-permute-start.23 = (bf16[128,1024]{1,0:T(8,128)(2,1)S(1)}, bf16[128,1024]{1,0:T(8,128)(2,1)S(1)}, u32[]{:S(2)}, u32[]{:S(2)}) collective-permute-start(bf16[128,1024]{1,0:T(8,128)(2,1)S(1)} %collective-permute-done.21.refs_7_), channel_id=1, source_target_pairs={{0,1},{1,0},{2,3},{3,2},{4,5},{5,4},{6,7},{7,6},{8,9},{9,8},{10,11... | collective-permute-start | bytes 786440 | tf_op jit(solution)/shard_map/ppermute | solution.py:69
  42.9 13.7 %collective-permute-start.26 = (bf16[128,1024]{1,0:T(8,128)(2,1)S(1)}, bf16[128,1024]{1,0:T(8,128)(2,1)S(1)}, u32[]{:S(2)}, u32[]{:S(2)}) collective-permute-start(bf16[128,1024]{1,0:T(8,128)(2,1)S(1)} %collective-permute-done.24.refs_10_), channel_id=1, source_target_pairs={{0,1},{1,0},{2,3},{3,2},{4,5},{5,4},{6,7},{7,6},{8,9},{9,8},{10,11... | collective-permute-start | bytes 786440 | tf_op jit(solution)/shard_map/ppermute | solution.py:66
  44.3 12.3 %collective-permute-start.27 = (bf16[128,1024]{1,0:T(8,128)(2,1)S(1)}, bf16[128,1024]{1,0:T(8,128)(2,1)}, u32[]{:S(2)}, u32[]{:S(2)}) collective-permute-start(bf16[128,1024]{1,0:T(8,128)(2,1)S(1)} %collective-permute-done.25.refs_11_), channel_id=1, source_target_pairs={{0,1},{1,0},{2,3},{3,2},{4,5},{5,4},{6,7},{7,6},{8,9},{9,8},{10,11... | collective-permute-start | bytes 786440 | tf_op jit(solution)/shard_map/ppermute | solution.py:69
  47.1 9.5 %collective-permute-start.29 = (bf16[128,1024]{1,0:T(8,128)(2,1)S(1)}, bf16[128,1024]{1,0:T(8,128)(2,1)}, u32[]{:S(2)}, u32[]{:S(2)}) collective-permute-start(bf16[128,1024]{1,0:T(8,128)(2,1)S(1)} %collective-permute-done.28.refs_14_), channel_id=1, source_target_pairs={{0,1},{1,0},{2,3},{3,2},{4,5},{5,4},{6,7},{7,6},{8,9},{9,8},{10,11... | collective-permute-start | bytes 786440 | tf_op jit(solution)/shard_map/ppermute | solution.py:66
  62.4 6.6 %collective-permute-start.31 = (bf16[128,1024]{1,0:T(8,128)(2,1)}, bf16[128,1024]{1,0:T(8,128)(2,1)S(1)}, u32[]{:S(2)}, u32[]{:S(2)}) collective-permute-start(bf16[128,1024]{1,0:T(8,128)(2,1)} %get-tuple-element.19.refs_0_), channel_id=1, source_target_pairs={{0,4},{1,3},{4,8},{5,1},{8,12},{9,5},{12,14},{13,9},{14,10},{15,13... | collective-permute-start | bytes 786440 | tf_op jit(solution)/shard_map/ppermute | solution.py:65
  63.9 6.6 %collective-permute-start.30 = (bf16[128,1024]{1,0:T(8,128)(2,1)}, bf16[128,1024]{1,0:T(8,128)(2,1)S(1)}, u32[]{:S(2)}, u32[]{:S(2)}) collective-permute-start(bf16[128,1024]{1,0:T(8,128)(2,1)} %get-tuple-element.19.refs_0_), channel_id=1, source_target_pairs={{0,1},{1,0},{2,3},{3,2},{4,5},{5,4},{6,7},{7,6},{8,9},{9,8},{10,11... | collective-permute-start | bytes 786440 | tf_op jit(solution)/shard_map/ppermute | solution.py:61
  70.5 7.7 %collective-permute-start.32 = (bf16[128,1024]{1,0:T(8,128)(2,1)S(1)}, bf16[128,1024]{1,0:T(8,128)(2,1)S(1)}, u32[]{:S(2)}, u32[]{:S(2)}) collective-permute-start(bf16[128,1024]{1,0:T(8,128)(2,1)S(1)} %collective-permute-done.30.refs_1_), channel_id=1, source_target_pairs={{0,4},{1,3},{4,8},{5,1},{8,12},{9,5},{12,14},{13,9},{14,10},{15,13... | collective-permute-start | bytes 786440 | tf_op jit(solution)/shard_map/ppermute | solution.py:68
  88.1 7.7 %collective-permute-start.43 = (bf16[128,1024]{1,0:T(8,128)(2,1)S(1)}, bf16[128,1024]{1,0:T(8,128)(2,1)S(1)}, u32[]{:S(2)}, u32[]{:S(2)}) collective-permute-start(bf16[128,1024]{1,0:T(8,128)(2,1)S(1)} %collective-permute-done.41.refs_0_), channel_id=1, source_target_pairs={{0,1},{1,0},{2,3},{3,2},{4,5},{5,4},{6,7},{7,6},{8,9},{9,8},{10,11... | collective-permute-start | bytes 786440 | tf_op jit(solution)/shard_map/ppermute | solution.py:66
  95.3 7.1 %collective-permute-start.52 = (bf16[128,1024]{1,0:T(8,128)(2,1)}, bf16[128,1024]{1,0:T(8,128)(2,1)S(1)}, u32[]{:S(2)}, u32[]{:S(2)}) collective-permute-start(bf16[128,1024]{1,0:T(8,128)(2,1)} %get-tuple-element.28), channel_id=1, source_target_pairs={{0,1},{1,0},{2,3},{3,2},{4,5},{5,4},{6,7},{7,6},{8,9},{9,8},{10,11... | collective-permute-start | bytes 786440 | tf_op jit(solution)/shard_map/ppermute | solution.py:81
  101.9 9.0 %collective-permute-start.45 = (bf16[256,1024]{1,0:T(8,128)(2,1)}, bf16[256,1024]{1,0:T(8,128)(2,1)S(1)}, u32[]{:S(2)}, u32[]{:S(2)}) collective-permute-start(bf16[256,1024]{1,0:T(8,128)(2,1)} %get-tuple-element.26), channel_id=1, source_target_pairs={{0,1},{1,0},{2,3},{3,2},{4,5},{5,4},{6,7},{7,6},{8,9},{9,8},{10,11... | collective-permute-start | bytes 1572872 | tf_op jit(solution)/shard_map/ppermute | solution.py:81
  102.5 8.3 %collective-permute-start.53 = (bf16[128,1024]{1,0:T(8,128)(2,1)S(1)}, bf16[128,1024]{1,0:T(8,128)(2,1)S(1)}, u32[]{:S(2)}, u32[]{:S(2)}) collective-permute-start(bf16[128,1024]{1,0:T(8,128)(2,1)S(1)} %add_convert_fusion.4), channel_id=1, source_target_pairs={{4,0},{3,1},{8,4},{1,5},{12,8},{5,9},{14,12},{9,13},{10,14},{13,15... | collective-permute-start | bytes 786440 | tf_op jit(solution)/shard_map/ppermute | solution.py:85
  110.2 10.3 %collective-permute-start.40 = (bf16[256,1024]{1,0:T(8,128)(2,1)}, bf16[256,1024]{1,0:T(8,128)(2,1)S(1)}, u32[]{:S(2)}, u32[]{:S(2)}) collective-permute-start(bf16[256,1024]{1,0:T(8,128)(2,1)} %get-tuple-element.24), channel_id=1, source_target_pairs={{0,1},{1,0},{2,3},{3,2},{4,5},{5,4},{6,7},{7,6},{8,9},{9,8},{10,11... | collective-permute-start | bytes 1572872 | tf_op jit(solution)/shard_map/ppermute | solution.py:81
  111.1 9.4 %collective-permute-start.46 = (bf16[128,1024]{1,0:T(8,128)(2,1)S(1)}, bf16[128,1024]{1,0:T(8,128)(2,1)S(1)}, u32[]{:S(2)}, u32[]{:S(2)}) collective-permute-start(bf16[128,1024]{1,0:T(8,128)(2,1)S(1)} %get-tuple-element.33), channel_id=1, source_target_pairs={{4,0},{3,1},{8,4},{1,5},{12,8},{5,9},{14,12},{9,13},{10,14},{13,15... | collective-permute-start | bytes 786440 | tf_op jit(solution)/shard_map/ppermute | solution.py:88
  112.7 7.8 %collective-permute-start.54 = (bf16[128,1024]{1,0:T(8,128)(2,1)S(1)}, bf16[128,1024]{1,0:T(8,128)(2,1)S(1)}, u32[]{:S(2)}, u32[]{:S(2)}) collective-permute-start(bf16[128,1024]{1,0:T(8,128)(2,1)S(1)} %get-tuple-element.34), channel_id=1, source_target_pairs={{4,0},{3,1},{8,4},{1,5},{12,8},{5,9},{14,12},{9,13},{10,14},{13,15... | collective-permute-start | bytes 786440 | tf_op jit(solution)/shard_map/ppermute | solution.py:85
  122.5 7.6 %collective-permute-start.55 = (bf16[128,1024]{1,0:T(8,128)(2,1)S(1)}, bf16[128,1024]{1,0:T(8,128)(2,1)S(1)}, u32[]{:S(2)}, u32[]{:S(2)}) collective-permute-start(bf16[128,1024]{1,0:T(8,128)(2,1)S(1)} %get-tuple-element.32), channel_id=1, source_target_pairs={{4,0},{3,1},{8,4},{1,5},{12,8},{5,9},{14,12},{9,13},{10,14},{13,15... | collective-permute-start | bytes 786440 | tf_op jit(solution)/shard_map/ppermute | solution.py:85
  130.3 6.8 %collective-permute-start.48 = (bf16[128,1024]{1,0:T(8,128)(2,1)S(1)}, bf16[128,1024]{1,0:T(8,128)(2,1)S(1)}, u32[]{:S(2)}, u32[]{:S(2)}) collective-permute-start(bf16[128,1024]{1,0:T(8,128)(2,1)S(1)} %get-tuple-element.29), channel_id=1, source_target_pairs={{4,0},{3,1},{8,4},{1,5},{12,8},{5,9},{14,12},{9,13},{10,14},{13,15... | collective-permute-start | bytes 786440 | tf_op jit(solution)/shard_map/ppermute | solution.py:88
  (75 other events, 842.9 us)

commit v3 on v2

v3 whole, which is shorter than its diff:
```python
import functools
import math

import jax
import jax.numpy as jnp
from jax import lax
from jax.experimental import pallas as pl
from jax.experimental.pallas import tpu as pltpu
from jax.sharding import PartitionSpec as P

QUERY_HEADS = 16
KEY_VALUE_HEADS = 2
HEAD_SIZE = 128
MOST_BLK = 8
GROUP = QUERY_HEADS // KEY_VALUE_HEADS
F32 = jnp.float32
BF16 = jnp.bfloat16
VMEM_LIMIT = 60 * 1024 * 1024
VMEM = pl.BlockSpec(memory_space=pltpu.VMEM)
SMEM = pl.BlockSpec(memory_space=pltpu.SMEM)
HBM = pl.BlockSpec(memory_space=pl.ANY)
PARAMS = pltpu.CompilerParams(vmem_limit_bytes=VMEM_LIMIT)


def ring_steps(chips):
    order = [2 * i for i in range(chips // 2)] + [2 * i + 1 for i in reversed(range(chips // 2))]
    steps, across = [], []
    for i in range(chips):
        ahead, behind = 2 * order[(i + 1) % chips], 2 * order[i - 1] + 1
        steps += [(2 * order[i], ahead), (2 * order[i] + 1, behind)]
        across += [(2 * order[i] + 1, ahead), (2 * order[i], behind)]
    return steps, across


def swap_steps(devices):
    return [(i, i ^ 1) for i in range(devices)]


def piece_groups(chips):
    groups = [[(0, 0), (0, 1)]]
    for j in range(1, chips // 2):
        groups.append([(-j, 0), (-j, 1), (j, 1), (j, 0)])
    return groups


def piece_names(devices):
    names = [name for group in piece_groups(devices // 2) for name in group]
    return names + [(-(devices // 4), 0), (-(devices // 4), 1)]


def source_of(name, tail, devices):
    half = devices // 4
    if name == (-half, 0):
        return name if tail else (half, 0)
    if name == (-half, 1):
        return (half, 1) if tail else name
    return name


def block_of(own, name, devices):
    chips = devices // 2
    chip, core = own // 2, own % 2
    place = jnp.where(chip % 2 == 0, chip // 2, chips - 1 - chip // 2)
    place = (place + jnp.where(core == 0, name[0], -name[0]) + chips) % chips
    chip = jnp.where(place < chips // 2, 2 * place, 2 * (chips - 1 - place) + 1)
    return 2 * chip + (core if name[1] == 0 else 1 - core)


def ring_gather(piece, cut, devices):
    half = devices // 4
    (ring, across), swap = ring_steps(devices // 2), swap_steps(devices)
    pieces = {(0, 0): piece}
    first = second = piece
    for j in range(1, half + 1):
        first = lax.ppermute(first if j < half else first[cut:], "seq", ring)
        second = lax.ppermute(
            second if j < half else second[:cut], "seq", across if j == 1 else ring
        )
        pieces[-j, 0], pieces[-j, 1] = first, second
    pieces[0, 1] = lax.ppermute(piece, "seq", swap)
    for j in range(1, half + 1):
        pieces[j, 1] = lax.ppermute(pieces[-j, 0], "seq", swap)
        pieces[j, 0] = lax.ppermute(pieces[-j, 1], "seq", swap)
    return pieces


def added(*terms):
    return functools.reduce(lambda a, b: a + b, [t.astype(F32) for t in terms])


def ring_scatter_sum(kept, sent, cut, devices):
    half = devices // 4
    ring, across = ring_steps(devices // 2)
    ring, across = [(b, a) for a, b in ring], [(b, a) for a, b in across]
    swap = swap_steps(devices)
    got = {j: lax.ppermute(sent[j], "seq", swap) for j in range(half, -1, -1)}
    rows = kept[0].shape[0]
    first, second = [], []
    for j in range(half, 0, -1):
        if j == half - 1:
            first = [jnp.pad(first[0], ((cut, 0), (0, 0)))]
            second = [jnp.pad(second[0], ((0, rows - cut), (0, 0)))]
        at = rows - cut if j == half else rows
        total = added(kept[j][:at], got[j][:at], *first).astype(BF16)
        _, received = lax.optimization_barrier((total, [got[j][at:], *second]))
        others = added(kept[j][at:], *received).astype(BF16)
        first = [lax.ppermute(total, "seq", ring)]
        second = [lax.ppermute(others, "seq", across if j == 1 else ring)]
    return added(kept[0], got[0], *first, *second).astype(BF16)


def pack_kernel(devices, key_ref, value_ref, id_ref, weight_ref, out_weight_ref, out_ref):
    rows, width = key_ref.shape
    out_ref[:rows, :width] = key_ref[...]
    out_ref[:rows, width:] = value_ref[...]
    ids, weights = id_ref[...], weight_ref[...]
    by_expert = [
        jnp.sum(jnp.where(ids == e, weights, 0.0), axis=0, keepdims=True) for e in range(devices)
    ]
    in_row = 2 * width // rows
    lines = []
    for first in range(0, devices, in_row):
        lines.append(jnp.concatenate(by_expert[first : first + in_row], axis=1))
    high = [line.astype(BF16).astype(F32) for line in lines]
    low = [line - h for line, h in zip(lines, high)]
    extra = line_rows(devices, rows, width)
    if extra > 2 * len(lines):
        low.append(jnp.zeros((extra - 2 * len(lines), 2 * width), F32))
    out_ref[rows : rows + extra, :] = jnp.concatenate(high + low, axis=0).astype(BF16)
    depth = out_weight_ref.shape[0]
    for n in range(out_weight_ref.shape[1] // (2 * width)):
        start = rows + extra + n * depth
        out_ref[start : start + depth, :] = out_weight_ref[:, 2 * width * n : 2 * width * (n + 1)]


def line_rows(devices, rows, width):
    lines = 2 * (devices * rows // (2 * width))
    return -(-lines // 16) * 16


def pack(keys, values, ids, weights, out_weight, devices):
    rows, width = keys.shape
    total = rows + line_rows(devices, rows, width)
    total += out_weight.shape[0] * out_weight.shape[1] // (2 * width)
    return pl.pallas_call(
        functools.partial(pack_kernel, devices),
        out_shape=jax.ShapeDtypeStruct((total, 2 * width), BF16),
        in_specs=[VMEM] * 5,
        out_specs=VMEM,
        compiler_params=PARAMS,
        cost_estimate=pl.CostEstimate(flops=10**6, bytes_accessed=2**20, transcendentals=0),
        name="pack",
    )(keys, values, jnp.transpose(ids), jnp.transpose(weights), out_weight)


def attend_kernel(devices, own_ref, doc_ref, q_ref, res_ref, gain_ref, *refs):
    names = piece_names(devices)
    head_refs, tail_refs = refs[: len(names)], refs[len(names) : 2 * len(names)]
    out_ref, scale_ref, hidden_ref, normed_ref = refs[2 * len(names) : 2 * len(names) + 4]
    keys, values, weight, lines, sems = refs[2 * len(names) + 4 :]
    rows = q_ref.shape[0]
    width = KEY_VALUE_HEADS * HEAD_SIZE
    extra = lines.shape[1]
    window = keys.shape[1]
    depth = weight.shape[0] // devices
    own = own_ref[0]
    own_doc = doc_ref[own]

    def copies(i, slot):
        start = pl.multiple_of(slot * rows, rows)
        made = []
        for g in range(KEY_VALUE_HEADS):
            for part, buffer in enumerate((keys, values)):
                column = part * width + g * HEAD_SIZE
                made.append(
                    pltpu.make_async_copy(
                        head_refs[i].at[pl.ds(0, rows), pl.ds(column, HEAD_SIZE)],
                        buffer.at[g, pl.ds(start, rows), pl.ds(0, HEAD_SIZE)],
                        sems.at[i, len(made)],
                    )
                )
        return made

    def line_copy(i):
        return pltpu.make_async_copy(
            head_refs[i].at[pl.ds(rows, extra), :], lines.at[i], sems.at[i, 4]
        )

    def weight_copies(i):
        start = pl.multiple_of(block_of(own, names[i], devices) * depth, depth)
        behind = tail_refs[i].shape[0] - weight.shape[1] // (2 * width) * depth
        return [
            pltpu.make_async_copy(
                tail_refs[i].at[pl.ds(behind + n * depth, depth), :],
                weight.at[pl.ds(start, depth), pl.ds(2 * width * n, 2 * width)],
                sems.at[i, 5 + n],
            )
            for n in range(weight.shape[1] // (2 * width))
        ]

    for c in copies(0, 0):
        c.start()
    slots, seen = [jnp.int32(0)], [True]
    filled = jnp.int32(1)
    for i in range(1, len(names)):
        block = block_of(own, names[i], devices)
        shown = (block < own) & ((block == 0) | (doc_ref[block] == own_doc))
        slots.append(filled)
        seen.append(shown)

        @pl.when(shown)
        def _(i=i, slot=filled):
            for c in copies(i, slot):
                c.start()

        filled = filled + shown.astype(jnp.int32)
    for i in range(len(names)):
        line_copy(i).start()
    for i in range(len(names)):
        for c in weight_copies(i):
            c.start()

    lane = lax.broadcasted_iota(jnp.int32, (window, HEAD_SIZE), 1)
    row = lax.broadcasted_iota(jnp.int32, (window, HEAD_SIZE), 0)
    one_column = jnp.where((lane == 0) & (row < filled * rows), 1.0, 0.0).astype(BF16)
    for g in range(KEY_VALUE_HEADS):
        values[g, :, HEAD_SIZE:] = one_column
    for c in copies(0, 0):
        c.wait()
    for s in range(1, window // rows):

        @pl.when(s >= filled)
        def _(s=s):
            for g in range(KEY_VALUE_HEADS):
                keys[g, s * rows : (s + 1) * rows, :] = jnp.broadcast_to(
                    keys[g, :1, :].astype(F32), (rows, HEAD_SIZE)
                ).astype(BF16)
                values[g, s * rows : (s + 1) * rows, :HEAD_SIZE] = jnp.zeros(
                    (rows, HEAD_SIZE), BF16
                )

    for i in range(1, len(names)):

        @pl.when(seen[i])
        def _(i=i):
            for c in copies(i, slots[i]):
                c.wait()

    query_row = lax.broadcasted_iota(jnp.int32, (rows, rows), 0)
    key_row = lax.broadcasted_iota(jnp.int32, (rows, rows), 1)
    bias = jnp.where(key_row <= query_row, 0.0, -1e30)
    factor = math.log2(math.e) / HEAD_SIZE**0.5
    heads = 4
    for first in range(0, QUERY_HEADS, heads):
        g = first // GROUP
        q = jnp.concatenate(
            [
                q_ref[:, (first + h) * HEAD_SIZE : (first + h + 1) * HEAD_SIZE]
                for h in range(heads)
            ],
            axis=0,
        )
        scores = lax.dot_general(
            q, keys[g], (((1,), (1,)), ((), ())), preferred_element_type=F32
        )
        scores = scores.reshape(heads, rows, window)
        scores = jnp.concatenate([scores[:, :, :rows] + bias[None], scores[:, :, rows:]], axis=2)
        top = jnp.max(scores, axis=-1, keepdims=True)
        probs = jnp.exp2((scores - top) * factor).astype(BF16).reshape(heads * rows, window)
        summed = jnp.dot(probs, values[g], preferred_element_type=F32)
        result = (summed[:, :HEAD_SIZE] / summed[:, HEAD_SIZE : HEAD_SIZE + 1]).astype(BF16)
        for h in range(heads):
            out_ref[:, (first + h) * HEAD_SIZE : (first + h + 1) * HEAD_SIZE] = result[
                h * rows : (h + 1) * rows
            ]

    for i in range(len(names)):
        line_copy(i).wait()
    count = devices * rows // (2 * width)
    in_row = 2 * width // rows
    line = lax.broadcasted_iota(jnp.int32, (extra, 2 * width), 0)
    wanted = (line == own // in_row) | (line == count + own // in_row)
    picked = []
    for i in range(len(names)):
        both = jnp.sum(jnp.where(wanted, lines[i].astype(F32), 0.0), axis=0, keepdims=True)
        picked.append(
            sum(
                jnp.where(own % in_row == n, both[:, n * rows : (n + 1) * rows], 0.0)
                for n in range(in_row)
            )
        )
    picked.append(jnp.zeros((rows - len(names), rows), F32))
    scale_ref[...] = jnp.transpose(jnp.concatenate(picked, axis=0))

    for i in range(len(names)):
        for c in weight_copies(i):
            c.wait()
    hidden = res_ref[...].astype(F32) + jnp.dot(
        out_ref[...], weight[...], preferred_element_type=F32
    )
    hidden_ref[...] = hidden.astype(BF16)
    mean_square = jnp.mean(hidden * hidden, axis=-1, keepdims=True)
    normed_ref[...] = (
        hidden * lax.rsqrt(mean_square + 1e-06) * gain_ref[...].astype(F32)
    ).astype(BF16)


def attend(own, docs, queries, residual, gain, packed, depth, devices):
    rows, model = residual.shape
    window = (min(MOST_BLK, devices) + 1) * rows
    names = piece_names(devices)
    width = KEY_VALUE_HEADS * HEAD_SIZE
    shape = jax.ShapeDtypeStruct(residual.shape, BF16)
    return pl.pallas_call(
        functools.partial(attend_kernel, devices),
        out_shape=(
            jax.ShapeDtypeStruct(queries.shape, BF16),
            jax.ShapeDtypeStruct((rows, rows), F32),
            shape,
            shape,
        ),
        in_specs=[SMEM, SMEM, VMEM, VMEM, VMEM] + [HBM] * (2 * len(names)),
        out_specs=(VMEM,) * 4,
        scratch_shapes=[
            pltpu.VMEM((KEY_VALUE_HEADS, window, HEAD_SIZE), BF16),
            pltpu.VMEM((KEY_VALUE_HEADS, window, 2 * HEAD_SIZE), BF16),
            pltpu.VMEM((depth * devices, model), BF16),
            pltpu.VMEM((len(names), line_rows(devices, rows, width), 2 * width), BF16),
            pltpu.SemaphoreType.DMA((len(names), 5 + model // (2 * width))),
        ],
        compiler_params=PARAMS,
        cost_estimate=pl.CostEstimate(
            flops=4 * QUERY_HEADS * rows * window * HEAD_SIZE + 2 * rows * depth * devices * model,
            bytes_accessed=8 * 2**20,
            transcendentals=QUERY_HEADS * rows * window,
        ),
        name="attend",
    )(
        own,
        docs,
        queries,
        residual,
        gain.reshape(1, -1),
        *[packed[source_of(name, False, devices)] for name in names],
        *[packed[source_of(name, True, devices)] for name in names],
    )


def expert_kernel(parts, scale_ref, gate_ref, up_ref, down_ref, *refs):
    x_refs, out_refs = refs[: len(parts)], refs[len(parts) :]
    x = jnp.concatenate([r[...] for r in x_refs], axis=0)
    gate_part = jnp.dot(x, gate_ref[...], preferred_element_type=F32)
    up_part = jnp.dot(x, up_ref[...], preferred_element_type=F32)
    activated = (gate_part / (1.0 + jnp.exp(-gate_part)) * up_part).astype(BF16)
    produced = jnp.dot(activated, down_ref[...], preferred_element_type=F32)
    half = produced.shape[0] // 2
    at = 0
    for column, start, count in parts:
        part = produced[at : at + count] * scale_ref[start : start + count, column : column + 1]
        out_refs[at // half][at % half : at % half + count, :] = part.astype(BF16)
        at += count


def expert(scale, gate_proj, up_proj, down_proj, parts, pieces):
    rows, width = sum(p.shape[0] for p in pieces), pieces[0].shape[1]
    shape = jax.ShapeDtypeStruct((rows // 2, width), BF16)
    return pl.pallas_call(
        functools.partial(expert_kernel, parts),
        out_shape=(shape, shape),
        in_specs=[VMEM] * (4 + len(pieces)),
        out_specs=(VMEM, VMEM),
        compiler_params=pltpu.CompilerParams(vmem_limit_bytes=32 * 2**20),
        cost_estimate=pl.CostEstimate(
            flops=6 * rows * gate_proj.shape[0] * gate_proj.shape[1],
            bytes_accessed=4 * 2**20,
            transcendentals=rows * gate_proj.shape[1],
        ),
        name="expert",
    )(scale, gate_proj, up_proj, down_proj, *pieces)


def shards(
    queries,
    token_key_heads,
    token_value_heads,
    residual,
    out_weight,
    norm_gain,
    w_gate,
    w_up,
    w_down,
    expert_ids,
    gate_weights,
    doc_of_block,
):
    devices = lax.axis_size("seq")
    own = lax.axis_index("seq").astype(jnp.int32).reshape(1)
    packed = pack(
        token_key_heads, token_value_heads, expert_ids, gate_weights, out_weight, devices
    )
    rows = queries.shape[0]
    cut = rows + line_rows(devices, rows, token_key_heads.shape[1])
    attention, scales, hidden, normed = attend(
        own,
        doc_of_block,
        queries,
        residual,
        norm_gain,
        ring_gather(packed, cut, devices),
        out_weight.shape[0],
        devices,
    )

    half, cut = devices // 4, rows // 2
    tokens = ring_gather(normed, cut, devices)
    names = piece_names(devices)
    kept, sent = {}, {}
    for j, group in enumerate(piece_groups(devices // 2)):
        parts = [(names.index(name), 0, rows) for name in group]
        kept[j], sent[j] = expert(
            scales, w_gate[0], w_up[0], w_down[0], parts, [tokens[name] for name in group]
        )
    near, other = names.index((-half, 0)), names.index((-half, 1))
    parts = [(near, cut, rows - cut), (other, 0, cut), (other, cut, rows - cut), (near, 0, cut)]
    group = [(-half, 0), (-half, 1), (half, 1), (half, 0)]
    kept[half], sent[half] = expert(
        scales, w_gate[0], w_up[0], w_down[0], parts, [tokens[name] for name in group]
    )
    mix = ring_scatter_sum(kept, sent, cut, devices)
    return (attention, hidden, mix)


def solution(mesh):
    in_specs = (
        P(("pack", "seq"), None),
        P(("pack", "seq"), None),
        P(("pack", "seq"), None),
        P(("pack", "seq"), None),
        P("seq", None),
        P(),
        P("seq", None, None),
        P("seq", None, None),
        P("seq", None, None),
        P(("pack", "seq"), None),
        P(("pack", "seq"), None),
        P("pack"),
    )
    out_specs = (P(("pack", "seq"), None), P(("pack", "seq"), None), P(("pack", "seq"), None))
    return jax.shard_map(shards, mesh=mesh, in_specs=in_specs, out_specs=out_specs, check_vma=False)
```

time: 143 us -> 122 us (0.85)
  waiting for transfers between devices: 45.9 us -> 62.6 us
  Pallas kernels: 35.6 us -> 19 us
  starting transfers between devices: 48.5 us -> 34.6 us
  local copies, waits for them, and re-layouts: 9.03 us -> 2.17 us
    pallas_call x6 -> x5, Pallas kernels: 26 us -> 7.5 us  [expert(): pl.pallas_call(functools.partial(expert_kernel, parts), out_shape=(shape,...]
    ppermute x57 -> x47, waiting for transfers between devices: 45.9 us -> 62.6 us  [the longest x8 26.1 us: ring_gather(): first = lax.ppermute(first if j < half else first[cut:], 'seq', ring)]
    ppermute x57 -> x47, starting transfers between devices: 48.5 us -> 34.6 us  [the longest x8 10.6 us: ring_gather(): first = lax.ppermute(first if j < half else first[cut:], 'seq', ring)]
    unnamed x102 -> x36, local copies, waits for them, and re-layouts: 8.44 us -> 1.44 us
    pallas_call x1, Pallas kernels: 7.85 us -> 9.62 us  [attend(): pl.pallas_call(functools.partial(attend_kernel, devices), out_shape=(jax....]
  transfers between devices with their start and end apart: 57 -> 47, of which waited for: 20 -> 24; matrix products, arithmetic and copies ran while one was open for 3% -> 1% of each run, Pallas kernels for 21% -> 6%
where the time goes in v3:
time: 122 us; the launch traced here: 121 us
  waiting for transfers between devices  62.6 us (51%)
  starting transfers between devices  34.6 us (28%)
  Pallas kernels  19 us (16%)
  local copies, waits for them, and re-layouts  2.17 us (2%)
  other arithmetic  1.64 us (1%)
    ppermute x8, waiting for transfers between devices, ring_gather(): first = lax.ppermute(first if j < half else first[cut:], 'seq', ring)  26.1 us
    ppermute x8, waiting for transfers between devices, ring_gather(): lax.ppermute(second if j < half else second[:cut], 'seq', across if j ==...  23 us
    ppermute x8, starting transfers between devices, ring_gather(): first = lax.ppermute(first if j < half else first[cut:], 'seq', ring)  10.6 us
    pallas_call x1, Pallas kernels, attend(): pl.pallas_call(functools.partial(attend_kernel, devices), out_shape=(jax....  9.62 us
    ppermute x4, waiting for transfers between devices, ring_scatter_sum(): second = [lax.ppermute(others, 'seq', across if j == 1 else ring)]  7.82 us
    pallas_call x5, Pallas kernels, expert(): pl.pallas_call(functools.partial(expert_kernel, parts), out_shape=(shape,...  7.5 us
    ppermute x8, starting transfers between devices, ring_gather(): lax.ppermute(second if j < half else second[:cut], 'seq', across if j ==...  7.34 us
    ppermute x4, starting transfers between devices, ring_scatter_sum(): first = [lax.ppermute(total, 'seq', ring)]  6.59 us
  transfers between devices with their start and end apart: 47, of which 24 were waited for; matrix products, arithmetic and copies ran while one was open for 1% of the time, Pallas kernels for 6%

profile of v3, /device:TPU:0, one launch (start us, length us, event | category | flops | bytes accessed | tf_op | source)
XLA Modules:
  0.0 121.0 jit_solution(12412625853536697867)
XLA Ops:
  0.6 1.9 %pack.1.refs_0_.refs_16_ = bf16[400,512]{1,0:T(8,128)(2,1)} custom-call(bf16[128,256]{1,0:T(8,128)(2,1)} %key_ref.1, bf16[128,256]{1,0:T(8,128)(2,1)} %value_ref.1, s32[8,128]{1,0:T(8,128)} %bitcast.21, f32[8,128]{1,0:T(8,128)} %bitcast.22, bf16[128,1024]{1,0:T(8,128)(2,1)} %out_weight_ref.1), custom_call_target="tpu_custom_call" | custom-call | flops 1000000 | bytes 1048576 | tf_op jit(solution)/shard_map/pack/pallas_call | solution.py:145
  2.5 3.0 %collective-permute-start.1 = (bf16[400,512]{1,0:T(8,128)(2,1)}, bf16[400,512]{1,0:T(8,128)(2,1)S(1)}, u32[]{:S(2)}, u32[]{:S(2)}) collective-permute-start(bf16[400,512]{1,0:T(8,128)(2,1)} %pack.1.refs_0_.refs_16_), channel_id=1, source_target_pairs={{0,4},{1,3},{4,8},{5,1},{8,12},{9,5},{12,14},{13,9},{14,10},{15,13... | collective-permute-start | bytes 1228808 | tf_op jit(solution)/shard_map/ppermute | solution.py:75
  6.2 8.5 %collective-permute-done.1.refs_2_.refs_18_ = bf16[400,512]{1,0:T(8,128)(2,1)S(1)} collective-permute-done((bf16[400,512]{1,0:T(8,128)(2,1)}, bf16[400,512]{1,0:T(8,128)(2,1)S(1)}, u32[]{:S(2)}, u32[]{:S(2)}) %collective-permute-start.1) | collective-permute-done | bytes 409632 | tf_op jit(solution)/shard_map/ppermute | solution.py:75
  14.7 2.4 %collective-permute-start.5 = (bf16[400,512]{1,0:T(8,128)(2,1)S(1)}, bf16[400,512]{1,0:T(8,128)(2,1)S(1)}, u32[]{:S(2)}, u32[]{:S(2)}) collective-permute-start(bf16[400,512]{1,0:T(8,128)(2,1)S(1)} %collective-permute-done.1.refs_2_.refs_18_), channel_id=1, source_target_pairs={{0,4},{1,3},{4,8},{5,1},{8,12},{9,5},{12,14},{13,9},{14,10},{15,13... | collective-permute-start | bytes 1228808 | tf_op jit(solution)/shard_map/ppermute | solution.py:75
  18.7 5.3 %collective-permute-done.5.refs_6_.refs_22_ = bf16[400,512]{1,0:T(8,128)(2,1)S(1)} collective-permute-done((bf16[400,512]{1,0:T(8,128)(2,1)S(1)}, bf16[400,512]{1,0:T(8,128)(2,1)S(1)}, u32[]{:S(2)}, u32[]{:S(2)}) %collective-permute-start.5) | collective-permute-done | bytes 409632 | tf_op jit(solution)/shard_map/ppermute | solution.py:75
  25.6 2.8 %collective-permute-done.6.refs_7_.refs_23_ = bf16[400,512]{1,0:T(8,128)(2,1)S(1)} collective-permute-done((bf16[400,512]{1,0:T(8,128)(2,1)S(1)}, bf16[400,512]{1,0:T(8,128)(2,1)S(1)}, u32[]{:S(2)}, u32[]{:S(2)}) %collective-permute-start.6) | collective-permute-done | bytes 409632 | tf_op jit(solution)/shard_map/ppermute | solution.py:76
  29.4 3.3 %collective-permute-done.9.refs_10_.refs_26_ = bf16[400,512]{1,0:T(8,128)(2,1)S(1)} collective-permute-done((bf16[400,512]{1,0:T(8,128)(2,1)S(1)}, bf16[400,512]{1,0:T(8,128)(2,1)S(1)}, u32[]{:S(2)}, u32[]{:S(2)}) %collective-permute-start.9) | collective-permute-done | bytes 409632 | tf_op jit(solution)/shard_map/ppermute | solution.py:75
  35.1 2.0 %collective-permute-done.10.refs_11_.refs_27_ = bf16[400,512]{1,0:T(8,128)(2,1)S(1)} collective-permute-done((bf16[400,512]{1,0:T(8,128)(2,1)S(1)}, bf16[400,512]{1,0:T(8,128)(2,1)S(1)}, u32[]{:S(2)}, u32[]{:S(2)}) %collective-permute-start.10) | collective-permute-done | bytes 409632 | tf_op jit(solution)/shard_map/ppermute | solution.py:76
  39.9 3.0 %collective-permute-done.13.refs_15_ = bf16[144,512]{1,0:T(8,128)(2,1)} collective-permute-done((bf16[144,512]{1,0:T(8,128)(2,1)S(1)}, bf16[144,512]{1,0:T(8,128)(2,1)}, u32[]{:S(2)}, u32[]{:S(2)}) %collective-permute-start.13) | collective-permute-done | bytes 147488 | tf_op jit(solution)/shard_map/ppermute | solution.py:76
  45.5 9.6 %attend.1 = (bf16[128,2048]{1,0:T(8,128)(2,1)}, f32[128,128]{1,0:T(8,128)}, bf16[128,1024]{1,0:T(8,128)(2,1)}, bf16[128,1024]{1,0:T(8,128)(2,1)}) custom-call(s32[1]{0:T(128)} %bitcast.own_ref, s32[16]{0:T(128)} %doc_ref.1, bf16[128,2048]{1,0:T(8,128)(2,1)} %q_ref.1, bf16[128,1024]{1,0:T(8,128)(2,1)} %res_ref.1, bf16[1,1024]{1,0:T(2,128)(2,1)} %reshape.13.gain_ref, ...), custom_call_target="tpu_custom_call" | custom-call | flops 1744830464 | bytes 8388608 | tf_op jit(solution)/shard_map/attend/pallas_call | solution.py:314
  55.1 1.8 %collective-permute-start.20 = (bf16[128,1024]{1,0:T(8,128)(2,1)}, bf16[128,1024]{1,0:T(8,128)(2,1)S(1)}, u32[]{:S(2)}, u32[]{:S(2)}) collective-permute-start(bf16[128,1024]{1,0:T(8,128)(2,1)} %get-tuple-element.27.refs_0_), channel_id=1, source_target_pairs={{1,4},{0,3},{5,8},{4,1},{9,12},{8,5},{13,14},{12,9},{15,10},{14,13... | collective-permute-start | bytes 786440 | tf_op jit(solution)/shard_map/ppermute | solution.py:76
  56.9 6.5 %collective-permute-done.20.refs_1_ = bf16[128,1024]{1,0:T(8,128)(2,1)S(1)} collective-permute-done((bf16[128,1024]{1,0:T(8,128)(2,1)}, bf16[128,1024]{1,0:T(8,128)(2,1)S(1)}, u32[]{:S(2)}, u32[]{:S(2)}) %collective-permute-start.20) | collective-permute-done | bytes 262176 | tf_op jit(solution)/shard_map/ppermute | solution.py:76
  64.0 2.3 %collective-permute-start.24 = (bf16[128,1024]{1,0:T(8,128)(2,1)S(1)}, bf16[128,1024]{1,0:T(8,128)(2,1)S(1)}, u32[]{:S(2)}, u32[]{:S(2)}) collective-permute-start(bf16[128,1024]{1,0:T(8,128)(2,1)S(1)} %collective-permute-done.19.refs_0_), channel_id=1, source_target_pairs={{0,4},{1,3},{4,8},{5,1},{8,12},{9,5},{12,14},{13,9},{14,10},{15,13... | collective-permute-start | bytes 786440 | tf_op jit(solution)/shard_map/ppermute | solution.py:75
  66.2 3.6 %collective-permute-done.25.refs_1_ = bf16[128,1024]{1,0:T(8,128)(2,1)S(1)} collective-permute-done((bf16[128,1024]{1,0:T(8,128)(2,1)S(1)}, bf16[128,1024]{1,0:T(8,128)(2,1)S(1)}, u32[]{:S(2)}, u32[]{:S(2)}) %collective-permute-start.25) | collective-permute-done | bytes 262176 | tf_op jit(solution)/shard_map/ppermute | solution.py:76
  70.1 2.5 %collective-permute-done.24.refs_0_ = bf16[128,1024]{1,0:T(8,128)(2,1)S(1)} collective-permute-done((bf16[128,1024]{1,0:T(8,128)(2,1)S(1)}, bf16[128,1024]{1,0:T(8,128)(2,1)S(1)}, u32[]{:S(2)}, u32[]{:S(2)}) %collective-permute-start.24) | collective-permute-done | bytes 262176 | tf_op jit(solution)/shard_map/ppermute | solution.py:75
  72.9 3.2 %collective-permute-done.30.refs_1_ = bf16[128,1024]{1,0:T(8,128)(2,1)S(1)} collective-permute-done((bf16[128,1024]{1,0:T(8,128)(2,1)S(1)}, bf16[128,1024]{1,0:T(8,128)(2,1)S(1)}, u32[]{:S(2)}, u32[]{:S(2)}) %collective-permute-start.30) | collective-permute-done | bytes 262176 | tf_op jit(solution)/shard_map/ppermute | solution.py:76
  76.6 2.4 %collective-permute-done.29.refs_0_ = bf16[128,1024]{1,0:T(8,128)(2,1)S(1)} collective-permute-done((bf16[128,1024]{1,0:T(8,128)(2,1)S(1)}, bf16[128,1024]{1,0:T(8,128)(2,1)S(1)}, u32[]{:S(2)}, u32[]{:S(2)}) %collective-permute-start.29) | collective-permute-done | bytes 262176 | tf_op jit(solution)/shard_map/ppermute | solution.py:75
  79.4 1.8 %collective-permute-done.35.refs_1_ = bf16[64,1024]{1,0:T(8,128)(2,1)S(1)} collective-permute-done((bf16[64,1024]{1,0:T(8,128)(2,1)S(1)}, bf16[64,1024]{1,0:T(8,128)(2,1)S(1)}, u32[]{:S(2)}, u32[]{:S(2)}) %collective-permute-start.35) | collective-permute-done | bytes 131104 | tf_op jit(solution)/shard_map/ppermute | solution.py:76
  81.2 2.8 %collective-permute-done.34.refs_0_ = bf16[64,1024]{1,0:T(8,128)(2,1)S(1)} collective-permute-done((bf16[64,1024]{1,0:T(8,128)(2,1)S(1)}, bf16[64,1024]{1,0:T(8,128)(2,1)S(1)}, u32[]{:S(2)}, u32[]{:S(2)}) %collective-permute-start.34) | collective-permute-done | bytes 131104 | tf_op jit(solution)/shard_map/ppermute | solution.py:75
  87.2 1.8 %expert.8 = (bf16[256,1024]{1,0:T(8,128)(2,1)S(1)}, bf16[256,1024]{1,0:T(8,128)(2,1)S(1)}) custom-call(f32[128,128]{1,0:T(8,128)S(1)} %copy-done.4, bf16[1024,384]{1,0:T(8,128)(2,1)S(1)} %bitcast.7, bf16[1024,384]{1,0:T(8,128)(2,1)S(1)} %bitcast.12, bf16[384,1024]{1,0:T(8,128)(2,1)S(1)} %bitcast.17, bf16[128,1024]{1,0:T(8,128)(2,1)S(1)} %collective-permute-done.29.refs_0_, ...), custom_call_target="tpu_custom_call" | custom-call | flops 1207959552 | bytes 4194304 | tf_op jit(solution)/shard_map/expert/pallas_call | solution.py:367
  89.5 2.0 %collective-permute-start.43 = (bf16[64,1024]{1,0:T(8,128)(2,1)S(1)}, bf16[64,1024]{1,0:T(8,128)(2,1)S(1)}, u32[]{:S(2)}, u32[]{:S(2)}) collective-permute-start(bf16[64,1024]{1,0:T(8,128)(2,1)S(1)} %add_convert_fusion.7), channel_id=1, source_target_pairs={{4,0},{3,1},{8,4},{1,5},{12,8},{5,9},{14,12},{9,13},{10,14},{13,15... | collective-permute-start | bytes 393224 | tf_op jit(solution)/shard_map/ppermute | solution.py:108
  91.5 1.6 %collective-permute-start.39 = (bf16[64,1024]{1,0:T(8,128)(2,1)S(1)}, bf16[64,1024]{1,0:T(8,128)(2,1)S(1)}, u32[]{:S(2)}, u32[]{:S(2)}) collective-permute-start(bf16[64,1024]{1,0:T(8,128)(2,1)S(1)} %add_convert_fusion.8), channel_id=1, source_target_pairs={{4,0},{3,1},{8,4},{1,5},{12,8},{5,9},{14,12},{9,13},{10,14},{13,15... | collective-permute-start | bytes 393224 | tf_op jit(solution)/shard_map/ppermute | solution.py:107
  93.6 1.8 %expert.7 = (bf16[256,1024]{1,0:T(8,128)(2,1)S(1)}, bf16[256,1024]{1,0:T(8,128)(2,1)S(1)}) custom-call(f32[128,128]{1,0:T(8,128)S(1)} %copy-done.4, bf16[1024,384]{1,0:T(8,128)(2,1)S(1)} %bitcast.8, bf16[1024,384]{1,0:T(8,128)(2,1)S(1)} %bitcast.13, bf16[384,1024]{1,0:T(8,128)(2,1)S(1)} %bitcast.18, bf16[128,1024]{1,0:T(8,128)(2,1)S(1)} %collective-permute-done.24.refs_0_, ...), custom_call_target="tpu_custom_call" | custom-call | flops 1207959552 | bytes 4194304 | tf_op jit(solution)/shard_map/expert/pallas_call | solution.py:367
  96.6 1.7 %collective-permute-start.40 = (bf16[128,1024]{1,0:T(8,128)(2,1)S(1)}, bf16[128,1024]{1,0:T(8,128)(2,1)S(1)}, u32[]{:S(2)}, u32[]{:S(2)}) collective-permute-start(bf16[128,1024]{1,0:T(8,128)(2,1)S(1)} %add_convert_fusion.6), channel_id=1, source_target_pairs={{4,0},{3,1},{8,4},{1,5},{12,8},{5,9},{14,12},{9,13},{10,14},{13,15... | collective-permute-start | bytes 786440 | tf_op jit(solution)/shard_map/ppermute | solution.py:107
  98.4 1.7 %collective-permute-start.44 = (bf16[128,1024]{1,0:T(8,128)(2,1)S(1)}, bf16[128,1024]{1,0:T(8,128)(2,1)S(1)}, u32[]{:S(2)}, u32[]{:S(2)}) collective-permute-start(bf16[128,1024]{1,0:T(8,128)(2,1)S(1)} %add_convert_fusion.3), channel_id=1, source_target_pairs={{4,0},{3,1},{8,4},{1,5},{12,8},{5,9},{14,12},{9,13},{10,14},{13,15... | collective-permute-start | bytes 786440 | tf_op jit(solution)/shard_map/ppermute | solution.py:108
  100.1 1.8 %expert.6 = (bf16[256,1024]{1,0:T(8,128)(2,1)S(1)}, bf16[256,1024]{1,0:T(8,128)(2,1)S(1)}) custom-call(f32[128,128]{1,0:T(8,128)S(1)} %copy-done.4, bf16[1024,384]{1,0:T(8,128)(2,1)S(1)} %bitcast.9, bf16[1024,384]{1,0:T(8,128)(2,1)S(1)} %bitcast.14, bf16[384,1024]{1,0:T(8,128)(2,1)S(1)} %bitcast.19, bf16[128,1024]{1,0:T(8,128)(2,1)S(1)} %collective-permute-done.19.refs_0_, ...), custom_call_target="tpu_custom_call" | custom-call | flops 1207959552 | bytes 4194304 | tf_op jit(solution)/shard_map/expert/pallas_call | solution.py:367
  103.1 1.7 %collective-permute-start.41 = (bf16[128,1024]{1,0:T(8,128)(2,1)S(1)}, bf16[128,1024]{1,0:T(8,128)(2,1)S(1)}, u32[]{:S(2)}, u32[]{:S(2)}) collective-permute-start(bf16[128,1024]{1,0:T(8,128)(2,1)S(1)} %add_convert_fusion.5), channel_id=1, source_target_pairs={{4,0},{3,1},{8,4},{1,5},{12,8},{5,9},{14,12},{9,13},{10,14},{13,15... | collective-permute-start | bytes 786440 | tf_op jit(solution)/shard_map/ppermute | solution.py:107
  105.9 1.7 %collective-permute-start.45 = (bf16[128,1024]{1,0:T(8,128)(2,1)S(1)}, bf16[128,1024]{1,0:T(8,128)(2,1)S(1)}, u32[]{:S(2)}, u32[]{:S(2)}) collective-permute-start(bf16[128,1024]{1,0:T(8,128)(2,1)S(1)} %add_convert_fusion.2), channel_id=1, source_target_pairs={{4,0},{3,1},{8,4},{1,5},{12,8},{5,9},{14,12},{9,13},{10,14},{13,15... | collective-permute-start | bytes 786440 | tf_op jit(solution)/shard_map/ppermute | solution.py:108
  109.7 2.7 %collective-permute-done.45 = bf16[128,1024]{1,0:T(8,128)(2,1)S(1)} collective-permute-done((bf16[128,1024]{1,0:T(8,128)(2,1)S(1)}, bf16[128,1024]{1,0:T(8,128)(2,1)S(1)}, u32[]{:S(2)}, u32[]{:S(2)}) %collective-permute-start.45) | collective-permute-done | bytes 262176 | tf_op jit(solution)/shard_map/ppermute | solution.py:108
  112.6 1.7 %collective-permute-start.42 = (bf16[128,1024]{1,0:T(8,128)(2,1)S(1)}, bf16[128,1024]{1,0:T(8,128)(2,1)S(1)}, u32[]{:S(2)}, u32[]{:S(2)}) collective-permute-start(bf16[128,1024]{1,0:T(8,128)(2,1)S(1)} %add_convert_fusion.4), channel_id=1, source_target_pairs={{4,0},{3,1},{8,4},{1,5},{12,8},{5,9},{14,12},{9,13},{10,14},{13,15... | collective-permute-start | bytes 786440 | tf_op jit(solution)/shard_map/ppermute | solution.py:107
  114.2 4.1 %collective-permute-done.46 = bf16[128,1024]{1,0:T(8,128)(2,1)S(1)} collective-permute-done((bf16[128,1024]{1,0:T(8,128)(2,1)S(1)}, bf16[128,1024]{1,0:T(8,128)(2,1)S(1)}, u32[]{:S(2)}, u32[]{:S(2)}) %collective-permute-start.46) | collective-permute-done | bytes 262176 | tf_op jit(solution)/shard_map/ppermute | solution.py:108
  118.3 1.8 %collective-permute-done.42 = bf16[128,1024]{1,0:T(8,128)(2,1)S(1)} collective-permute-done((bf16[128,1024]{1,0:T(8,128)(2,1)S(1)}, bf16[128,1024]{1,0:T(8,128)(2,1)S(1)}, u32[]{:S(2)}, u32[]{:S(2)}) %collective-permute-start.42) | collective-permute-done | bytes 262176 | tf_op jit(solution)/shard_map/ppermute | solution.py:107
  (124 shorter events, 25.5 us)
Async XLA Ops:
  2.5 12.2 %collective-permute-start.1 = (bf16[400,512]{1,0:T(8,128)(2,1)}, bf16[400,512]{1,0:T(8,128)(2,1)S(1)}, u32[]{:S(2)}, u32[]{:S(2)}) collective-permute-start(bf16[400,512]{1,0:T(8,128)(2,1)} %pack.1.refs_0_.refs_16_), channel_id=1, source_target_pairs={{0,4},{1,3},{4,8},{5,1},{8,12},{9,5},{12,14},{13,9},{14,10},{15,13... | collective-permute-start | bytes 1228808 | tf_op jit(solution)/shard_map/ppermute | solution.py:75
  5.5 11.6 %collective-permute-start.2 = (bf16[400,512]{1,0:T(8,128)(2,1)}, bf16[400,512]{1,0:T(8,128)(2,1)S(1)}, u32[]{:S(2)}, u32[]{:S(2)}) collective-permute-start(bf16[400,512]{1,0:T(8,128)(2,1)} %pack.1.refs_0_.refs_16_), channel_id=1, source_target_pairs={{1,4},{0,3},{5,8},{4,1},{9,12},{8,5},{13,14},{12,9},{15,10},{14,13... | collective-permute-start | bytes 1228808 | tf_op jit(solution)/shard_map/ppermute | solution.py:76
  14.7 9.2 %collective-permute-start.5 = (bf16[400,512]{1,0:T(8,128)(2,1)S(1)}, bf16[400,512]{1,0:T(8,128)(2,1)S(1)}, u32[]{:S(2)}, u32[]{:S(2)}) collective-permute-start(bf16[400,512]{1,0:T(8,128)(2,1)S(1)} %collective-permute-done.1.refs_2_.refs_18_), channel_id=1, source_target_pairs={{0,4},{1,3},{4,8},{5,1},{8,12},{9,5},{12,14},{13,9},{14,10},{15,13... | collective-permute-start | bytes 1228808 | tf_op jit(solution)/shard_map/ppermute | solution.py:75
  17.1 11.2 %collective-permute-start.6 = (bf16[400,512]{1,0:T(8,128)(2,1)S(1)}, bf16[400,512]{1,0:T(8,128)(2,1)S(1)}, u32[]{:S(2)}, u32[]{:S(2)}) collective-permute-start(bf16[400,512]{1,0:T(8,128)(2,1)S(1)} %collective-permute-done.2.refs_3_.refs_19_), channel_id=1, source_target_pairs={{0,4},{1,3},{4,8},{5,1},{8,12},{9,5},{12,14},{13,9},{14,10},{15,13... | collective-permute-start | bytes 1228808 | tf_op jit(solution)/shard_map/ppermute | solution.py:76
  23.9 8.8 %collective-permute-start.9 = (bf16[400,512]{1,0:T(8,128)(2,1)S(1)}, bf16[400,512]{1,0:T(8,128)(2,1)S(1)}, u32[]{:S(2)}, u32[]{:S(2)}) collective-permute-start(bf16[400,512]{1,0:T(8,128)(2,1)S(1)} %collective-permute-done.5.refs_6_.refs_22_), channel_id=1, source_target_pairs={{0,4},{1,3},{4,8},{5,1},{8,12},{9,5},{12,14},{13,9},{14,10},{15,13... | collective-permute-start | bytes 1228808 | tf_op jit(solution)/shard_map/ppermute | solution.py:75
  25.0 7.7 %collective-permute-start = (bf16[400,512]{1,0:T(8,128)(2,1)}, bf16[400,512]{1,0:T(8,128)(2,1)S(1)}, u32[]{:S(2)}, u32[]{:S(2)}) collective-permute-start(bf16[400,512]{1,0:T(8,128)(2,1)} %pack.1.refs_0_.refs_16_), channel_id=1, source_target_pairs={{0,1},{1,0},{2,3},{3,2},{4,5},{5,4},{6,7},{7,6},{8,9},{9,8},{10,11... | collective-permute-start | bytes 1228808 | tf_op jit(solution)/shard_map/ppermute | solution.py:80
  25.1 8.9 %collective-permute-start.4 = (bf16[400,512]{1,0:T(8,128)(2,1)S(1)}, bf16[400,512]{1,0:T(8,128)(2,1)S(1)}, u32[]{:S(2)}, u32[]{:S(2)}) collective-permute-start(bf16[400,512]{1,0:T(8,128)(2,1)S(1)} %collective-permute-done.2.refs_3_.refs_19_), channel_id=1, source_target_pairs={{0,1},{1,0},{2,3},{3,2},{4,5},{5,4},{6,7},{7,6},{8,9},{9,8},{10,11... | collective-permute-start | bytes 1228808 | tf_op jit(solution)/shard_map/ppermute | solution.py:83
  28.3 8.8 %collective-permute-start.10 = (bf16[400,512]{1,0:T(8,128)(2,1)S(1)}, bf16[400,512]{1,0:T(8,128)(2,1)S(1)}, u32[]{:S(2)}, u32[]{:S(2)}) collective-permute-start(bf16[400,512]{1,0:T(8,128)(2,1)S(1)} %collective-permute-done.6.refs_7_.refs_23_), channel_id=1, source_target_pairs={{0,4},{1,3},{4,8},{5,1},{8,12},{9,5},{12,14},{13,9},{14,10},{15,13... | collective-permute-start | bytes 1228808 | tf_op jit(solution)/shard_map/ppermute | solution.py:76
  29.4 7.7 %collective-permute-start.3 = (bf16[400,512]{1,0:T(8,128)(2,1)S(1)}, bf16[400,512]{1,0:T(8,128)(2,1)S(1)}, u32[]{:S(2)}, u32[]{:S(2)}) collective-permute-start(bf16[400,512]{1,0:T(8,128)(2,1)S(1)} %collective-permute-done.1.refs_2_.refs_18_), channel_id=1, source_target_pairs={{0,1},{1,0},{2,3},{3,2},{4,5},{5,4},{6,7},{7,6},{8,9},{9,8},{10,11... | collective-permute-start | bytes 1228808 | tf_op jit(solution)/shard_map/ppermute | solution.py:82
  32.8 7.1 %collective-permute-start.15 = (bf16[256,512]{1,0:T(8,128)(2,1)S(1)}, bf16[256,512]{1,0:T(8,128)(2,1)S(1)}, u32[]{:S(2)}, u32[]{:S(2)}) collective-permute-start(bf16[256,512]{1,0:T(8,128)(2,1)S(1)} %slice.81), channel_id=1, source_target_pairs={{0,4},{1,3},{4,8},{5,1},{8,12},{9,5},{12,14},{13,9},{14,10},{15,13... | collective-permute-start | bytes 786440 | tf_op jit(solution)/shard_map/ppermute | solution.py:75
  33.9 10.3 %collective-permute-start.7 = (bf16[400,512]{1,0:T(8,128)(2,1)S(1)}, bf16[400,512]{1,0:T(8,128)(2,1)}, u32[]{:S(2)}, u32[]{:S(2)}) collective-permute-start(bf16[400,512]{1,0:T(8,128)(2,1)S(1)} %collective-permute-done.5.refs_6_.refs_22_), channel_id=1, source_target_pairs={{0,1},{1,0},{2,3},{3,2},{4,5},{5,4},{6,7},{7,6},{8,9},{9,8},{10,11... | collective-permute-start | bytes 1228808 | tf_op jit(solution)/shard_map/ppermute | solution.py:82
  37.1 7.6 %collective-permute-start.12 = (bf16[400,512]{1,0:T(8,128)(2,1)S(1)}, bf16[400,512]{1,0:T(8,128)(2,1)}, u32[]{:S(2)}, u32[]{:S(2)}) collective-permute-start(bf16[400,512]{1,0:T(8,128)(2,1)S(1)} %collective-permute-done.10.refs_11_.refs_27_), channel_id=1, source_target_pairs={{0,1},{1,0},{2,3},{3,2},{4,5},{5,4},{6,7},{7,6},{8,9},{9,8},{10,11... | collective-permute-start | bytes 1228808 | tf_op jit(solution)/shard_map/ppermute | solution.py:83
  37.1 7.6 %collective-permute-start.11 = (bf16[400,512]{1,0:T(8,128)(2,1)S(1)}, bf16[400,512]{1,0:T(8,128)(2,1)}, u32[]{:S(2)}, u32[]{:S(2)}) collective-permute-start(bf16[400,512]{1,0:T(8,128)(2,1)S(1)} %collective-permute-done.9.refs_10_.refs_26_), channel_id=1, source_target_pairs={{0,1},{1,0},{2,3},{3,2},{4,5},{5,4},{6,7},{7,6},{8,9},{9,8},{10,11... | collective-permute-start | bytes 1228808 | tf_op jit(solution)/shard_map/ppermute | solution.py:82
  55.1 8.3 %collective-permute-start.20 = (bf16[128,1024]{1,0:T(8,128)(2,1)}, bf16[128,1024]{1,0:T(8,128)(2,1)S(1)}, u32[]{:S(2)}, u32[]{:S(2)}) collective-permute-start(bf16[128,1024]{1,0:T(8,128)(2,1)} %get-tuple-element.27.refs_0_), channel_id=1, source_target_pairs={{1,4},{0,3},{5,8},{4,1},{9,12},{8,5},{13,14},{12,9},{15,10},{14,13... | collective-permute-start | bytes 786440 | tf_op jit(solution)/shard_map/ppermute | solution.py:76
  56.9 7.1 %collective-permute-start.19 = (bf16[128,1024]{1,0:T(8,128)(2,1)}, bf16[128,1024]{1,0:T(8,128)(2,1)S(1)}, u32[]{:S(2)}, u32[]{:S(2)}) collective-permute-start(bf16[128,1024]{1,0:T(8,128)(2,1)} %get-tuple-element.27.refs_0_), channel_id=1, source_target_pairs={{0,4},{1,3},{4,8},{5,1},{8,12},{9,5},{12,14},{13,9},{14,10},{15,13... | collective-permute-start | bytes 786440 | tf_op jit(solution)/shard_map/ppermute | solution.py:75
  63.4 6.4 %collective-permute-start.25 = (bf16[128,1024]{1,0:T(8,128)(2,1)S(1)}, bf16[128,1024]{1,0:T(8,128)(2,1)S(1)}, u32[]{:S(2)}, u32[]{:S(2)}) collective-permute-start(bf16[128,1024]{1,0:T(8,128)(2,1)S(1)} %collective-permute-done.20.refs_1_), channel_id=1, source_target_pairs={{0,4},{1,3},{4,8},{5,1},{8,12},{9,5},{12,14},{13,9},{14,10},{15,13... | collective-permute-start | bytes 786440 | tf_op jit(solution)/shard_map/ppermute | solution.py:76
  64.0 8.6 %collective-permute-start.24 = (bf16[128,1024]{1,0:T(8,128)(2,1)S(1)}, bf16[128,1024]{1,0:T(8,128)(2,1)S(1)}, u32[]{:S(2)}, u32[]{:S(2)}) collective-permute-start(bf16[128,1024]{1,0:T(8,128)(2,1)S(1)} %collective-permute-done.19.refs_0_), channel_id=1, source_target_pairs={{0,4},{1,3},{4,8},{5,1},{8,12},{9,5},{12,14},{13,9},{14,10},{15,13... | collective-permute-start | bytes 786440 | tf_op jit(solution)/shard_map/ppermute | solution.py:75
  69.8 6.4 %collective-permute-start.30 = (bf16[128,1024]{1,0:T(8,128)(2,1)S(1)}, bf16[128,1024]{1,0:T(8,128)(2,1)S(1)}, u32[]{:S(2)}, u32[]{:S(2)}) collective-permute-start(bf16[128,1024]{1,0:T(8,128)(2,1)S(1)} %collective-permute-done.25.refs_1_), channel_id=1, source_target_pairs={{0,4},{1,3},{4,8},{5,1},{8,12},{9,5},{12,14},{13,9},{14,10},{15,13... | collective-permute-start | bytes 786440 | tf_op jit(solution)/shard_map/ppermute | solution.py:76
  72.6 6.4 %collective-permute-start.29 = (bf16[128,1024]{1,0:T(8,128)(2,1)S(1)}, bf16[128,1024]{1,0:T(8,128)(2,1)S(1)}, u32[]{:S(2)}, u32[]{:S(2)}) collective-permute-start(bf16[128,1024]{1,0:T(8,128)(2,1)S(1)} %collective-permute-done.24.refs_0_), channel_id=1, source_target_pairs={{0,4},{1,3},{4,8},{5,1},{8,12},{9,5},{12,14},{13,9},{14,10},{15,13... | collective-permute-start | bytes 786440 | tf_op jit(solution)/shard_map/ppermute | solution.py:75
  86.7 6.4 %collective-permute-start.27 = (bf16[128,1024]{1,0:T(8,128)(2,1)S(1)}, bf16[128,1024]{1,0:T(8,128)(2,1)S(1)}, u32[]{:S(2)}, u32[]{:S(2)}) collective-permute-start(bf16[128,1024]{1,0:T(8,128)(2,1)S(1)} %collective-permute-done.25.refs_1_), channel_id=1, source_target_pairs={{0,1},{1,0},{2,3},{3,2},{4,5},{5,4},{6,7},{7,6},{8,9},{9,8},{10,11... | collective-permute-start | bytes 786440 | tf_op jit(solution)/shard_map/ppermute | solution.py:83
  87.0 6.1 %collective-permute-start.26 = (bf16[128,1024]{1,0:T(8,128)(2,1)S(1)}, bf16[128,1024]{1,0:T(8,128)(2,1)S(1)}, u32[]{:S(2)}, u32[]{:S(2)}) collective-permute-start(bf16[128,1024]{1,0:T(8,128)(2,1)S(1)} %collective-permute-done.24.refs_0_), channel_id=1, source_target_pairs={{0,1},{1,0},{2,3},{3,2},{4,5},{5,4},{6,7},{7,6},{8,9},{9,8},{10,11... | collective-permute-start | bytes 786440 | tf_op jit(solution)/shard_map/ppermute | solution.py:82
  89.0 7.5 %collective-permute-start.33 = (bf16[256,1024]{1,0:T(8,128)(2,1)S(1)}, bf16[256,1024]{1,0:T(8,128)(2,1)S(1)}, u32[]{:S(2)}, u32[]{:S(2)}) collective-permute-start(bf16[256,1024]{1,0:T(8,128)(2,1)S(1)} %get-tuple-element.35), channel_id=1, source_target_pairs={{0,1},{1,0},{2,3},{3,2},{4,5},{5,4},{6,7},{7,6},{8,9},{9,8},{10,11... | collective-permute-start | bytes 1572872 | tf_op jit(solution)/shard_map/ppermute | solution.py:96
  89.5 5.9 %collective-permute-start.43 = (bf16[64,1024]{1,0:T(8,128)(2,1)S(1)}, bf16[64,1024]{1,0:T(8,128)(2,1)S(1)}, u32[]{:S(2)}, u32[]{:S(2)}) collective-permute-start(bf16[64,1024]{1,0:T(8,128)(2,1)S(1)} %add_convert_fusion.7), channel_id=1, source_target_pairs={{4,0},{3,1},{8,4},{1,5},{12,8},{5,9},{14,12},{9,13},{10,14},{13,15... | collective-permute-start | bytes 393224 | tf_op jit(solution)/shard_map/ppermute | solution.py:108
  93.1 14.5 %collective-permute-start.17 = (bf16[128,1024]{1,0:T(8,128)(2,1)S(1)}, bf16[128,1024]{1,0:T(8,128)(2,1)S(1)}, u32[]{:S(2)}, u32[]{:S(2)}) collective-permute-start(bf16[128,1024]{1,0:T(8,128)(2,1)S(1)} %copy-done.3), channel_id=1, source_target_pairs={{0,1},{1,0},{2,3},{3,2},{4,5},{5,4},{6,7},{7,6},{8,9},{9,8},{10,11... | collective-permute-start | bytes 786440 | tf_op jit(solution)/shard_map/ppermute | solution.py:80
  96.6 6.4 %collective-permute-start.40 = (bf16[128,1024]{1,0:T(8,128)(2,1)S(1)}, bf16[128,1024]{1,0:T(8,128)(2,1)S(1)}, u32[]{:S(2)}, u32[]{:S(2)}) collective-permute-start(bf16[128,1024]{1,0:T(8,128)(2,1)S(1)} %add_convert_fusion.6), channel_id=1, source_target_pairs={{4,0},{3,1},{8,4},{1,5},{12,8},{5,9},{14,12},{9,13},{10,14},{13,15... | collective-permute-start | bytes 786440 | tf_op jit(solution)/shard_map/ppermute | solution.py:107
  98.4 7.4 %collective-permute-start.44 = (bf16[128,1024]{1,0:T(8,128)(2,1)S(1)}, bf16[128,1024]{1,0:T(8,128)(2,1)S(1)}, u32[]{:S(2)}, u32[]{:S(2)}) collective-permute-start(bf16[128,1024]{1,0:T(8,128)(2,1)S(1)} %add_convert_fusion.3), channel_id=1, source_target_pairs={{4,0},{3,1},{8,4},{1,5},{12,8},{5,9},{14,12},{9,13},{10,14},{13,15... | collective-permute-start | bytes 786440 | tf_op jit(solution)/shard_map/ppermute | solution.py:108
  101.9 6.9 %collective-permute-start.23 = (bf16[256,1024]{1,0:T(8,128)(2,1)S(1)}, bf16[256,1024]{1,0:T(8,128)(2,1)S(1)}, u32[]{:S(2)}, u32[]{:S(2)}) collective-permute-start(bf16[256,1024]{1,0:T(8,128)(2,1)S(1)} %get-tuple-element.31), channel_id=1, source_target_pairs={{0,1},{1,0},{2,3},{3,2},{4,5},{5,4},{6,7},{7,6},{8,9},{9,8},{10,11... | collective-permute-start | bytes 1572872 | tf_op jit(solution)/shard_map/ppermute | solution.py:96
  103.1 6.4 %collective-permute-start.41 = (bf16[128,1024]{1,0:T(8,128)(2,1)S(1)}, bf16[128,1024]{1,0:T(8,128)(2,1)S(1)}, u32[]{:S(2)}, u32[]{:S(2)}) collective-permute-start(bf16[128,1024]{1,0:T(8,128)(2,1)S(1)} %add_convert_fusion.5), channel_id=1, source_target_pairs={{4,0},{3,1},{8,4},{1,5},{12,8},{5,9},{14,12},{9,13},{10,14},{13,15... | collective-permute-start | bytes 786440 | tf_op jit(solution)/shard_map/ppermute | solution.py:107
  105.9 6.4 %collective-permute-start.45 = (bf16[128,1024]{1,0:T(8,128)(2,1)S(1)}, bf16[128,1024]{1,0:T(8,128)(2,1)S(1)}, u32[]{:S(2)}, u32[]{:S(2)}) collective-permute-start(bf16[128,1024]{1,0:T(8,128)(2,1)S(1)} %add_convert_fusion.2), channel_id=1, source_target_pairs={{4,0},{3,1},{8,4},{1,5},{12,8},{5,9},{14,12},{9,13},{10,14},{13,15... | collective-permute-start | bytes 786440 | tf_op jit(solution)/shard_map/ppermute | solution.py:108
  108.7 5.6 %collective-permute-start.18 = (bf16[128,1024]{1,0:T(8,128)(2,1)S(1)}, bf16[128,1024]{1,0:T(8,128)(2,1)S(1)}, u32[]{:S(2)}, u32[]{:S(2)}) collective-permute-start(bf16[128,1024]{1,0:T(8,128)(2,1)S(1)} %get-tuple-element.29), channel_id=1, source_target_pairs={{0,1},{1,0},{2,3},{3,2},{4,5},{5,4},{6,7},{7,6},{8,9},{9,8},{10,11... | collective-permute-start | bytes 786440 | tf_op jit(solution)/shard_map/ppermute | solution.py:96
  112.5 5.9 %collective-permute-start.46 = (bf16[128,1024]{1,0:T(8,128)(2,1)S(1)}, bf16[128,1024]{1,0:T(8,128)(2,1)S(1)}, u32[]{:S(2)}, u32[]{:S(2)}) collective-permute-start(bf16[128,1024]{1,0:T(8,128)(2,1)S(1)} %add_convert_fusion.1), channel_id=1, source_target_pairs={{4,1},{3,0},{8,5},{1,4},{12,9},{5,8},{14,13},{9,12},{10,15},{13,14... | collective-permute-start | bytes 786440 | tf_op jit(solution)/shard_map/ppermute | solution.py:108
  112.6 7.6 %collective-permute-start.42 = (bf16[128,1024]{1,0:T(8,128)(2,1)S(1)}, bf16[128,1024]{1,0:T(8,128)(2,1)S(1)}, u32[]{:S(2)}, u32[]{:S(2)}) collective-permute-start(bf16[128,1024]{1,0:T(8,128)(2,1)S(1)} %add_convert_fusion.4), channel_id=1, source_target_pairs={{4,0},{3,1},{8,4},{1,5},{12,8},{5,9},{14,12},{9,13},{10,14},{13,15... | collective-permute-start | bytes 786440 | tf_op jit(solution)/shard_map/ppermute | solution.py:107
  (33 other events, 331.3 us)

commit v4 on v3

--- a/solution.py
+++ b/solution.py
@@ -66,12 +66,14 @@
     return 2 * chip + (core if name[1] == 0 else 1 - core)
 
 
-def ring_gather(piece, cut, devices):
+def ring_gather(piece, cut, devices, aside=None):
     half = devices // 4
     (ring, across), swap = ring_steps(devices // 2), swap_steps(devices)
     pieces = {(0, 0): piece}
     first = second = piece
     for j in range(1, half + 1):
+        if j == half and aside is not None:
+            first, aside = lax.optimization_barrier((first, aside))
         first = lax.ppermute(first if j < half else first[cut:], "seq", ring)
         second = lax.ppermute(
             second if j < half else second[:cut], "seq", across if j == 1 else ring
@@ -81,7 +83,7 @@
     for j in range(1, half + 1):
         pieces[j, 1] = lax.ppermute(pieces[-j, 0], "seq", swap)
         pieces[j, 0] = lax.ppermute(pieces[-j, 1], "seq", swap)
-    return pieces
+    return pieces, aside
 
 
 def added(*terms):
@@ -106,7 +108,8 @@
         others = added(kept[j][at:], *received).astype(BF16)
         first = [lax.ppermute(total, "seq", ring)]
         second = [lax.ppermute(others, "seq", across if j == 1 else ring)]
-    return added(kept[0], got[0], *first, *second).astype(BF16)
+    mix = lax.optimization_barrier(added(kept[0], got[0], *first))
+    return added(mix, *second).astype(BF16)
 
 
 def pack_kernel(devices, key_ref, value_ref, id_ref, weight_ref, out_weight_ref, out_ref):
@@ -156,50 +159,30 @@
 def attend_kernel(devices, own_ref, doc_ref, q_ref, res_ref, gain_ref, *refs):
     names = piece_names(devices)
     head_refs, tail_refs = refs[: len(names)], refs[len(names) : 2 * len(names)]
-    out_ref, scale_ref, hidden_ref, normed_ref = refs[2 * len(names) : 2 * len(names) + 4]
-    keys, values, weight, lines, sems = refs[2 * len(names) + 4 :]
-    rows = q_ref.shape[0]
+    out_ref, hidden_ref, normed_ref, both, weight, sems = refs[2 * len(names) :]
+    rows, model = res_ref.shape
     width = KEY_VALUE_HEADS * HEAD_SIZE
-    extra = lines.shape[1]
-    window = keys.shape[1]
-    depth = weight.shape[0] // devices
+    window = both.shape[0]
+    parts = model // (2 * width)
+    depth = weight.shape[1] // parts
     own = own_ref[0]
     own_doc = doc_ref[own]
 
-    def copies(i, slot):
+    def kv_copy(i, slot):
         start = pl.multiple_of(slot * rows, rows)
-        made = []
-        for g in range(KEY_VALUE_HEADS):
-            for part, buffer in enumerate((keys, values)):
-                column = part * width + g * HEAD_SIZE
-                made.append(
-                    pltpu.make_async_copy(
-                        head_refs[i].at[pl.ds(0, rows), pl.ds(column, HEAD_SIZE)],
-                        buffer.at[g, pl.ds(start, rows), pl.ds(0, HEAD_SIZE)],
-                        sems.at[i, len(made)],
-                    )
-                )
-        return made
-
-    def line_copy(i):
         return pltpu.make_async_copy(
-            head_refs[i].at[pl.ds(rows, extra), :], lines.at[i], sems.at[i, 4]
-        )
-
-    def weight_copies(i):
-        start = pl.multiple_of(block_of(own, names[i], devices) * depth, depth)
-        behind = tail_refs[i].shape[0] - weight.shape[1] // (2 * width) * depth
-        return [
-            pltpu.make_async_copy(
-                tail_refs[i].at[pl.ds(behind + n * depth, depth), :],
-                weight.at[pl.ds(start, depth), pl.ds(2 * width * n, 2 * width)],
-                sems.at[i, 5 + n],
-            )
-            for n in range(weight.shape[1] // (2 * width))
-        ]
-
-    for c in copies(0, 0):
-        c.start()
+            head_refs[i].at[pl.ds(0, rows), :], both.at[pl.ds(start, rows), :], sems.at[i, 0]
+        )
+
+    def weight_copy(i):
+        behind = tail_refs[i].shape[0] - parts * depth
+        return pltpu.make_async_copy(
+            tail_refs[i].at[pl.ds(behind, parts * depth), :],
+            weight.at[block_of(own, names[i], devices)],
+            sems.at[i, 1],
+        )
+
+    kv_copy(0, 0).start()
     slots, seen = [jnp.int32(0)], [True]
     filled = jnp.int32(1)
     for i in range(1, len(names)):
@@ -210,94 +193,86 @@
 
         @pl.when(shown)
         def _(i=i, slot=filled):
-            for c in copies(i, slot):
-                c.start()
+            kv_copy(i, slot).start()
 
         filled = filled + shown.astype(jnp.int32)
     for i in range(len(names)):
-        line_copy(i).start()
-    for i in range(len(names)):
-        for c in weight_copies(i):
-            c.start()
-
+        weight_copy(i).start()
+
+    kv_copy(0, 0).wait()
+    for s in range(1, window // rows):
+
+        @pl.when(s >= filled)
+        def _(s=s):
+            here = slice(s * rows, (s + 1) * rows)
+            both[here, :width] = jnp.broadcast_to(
+                both[:1, :width].astype(F32), (rows, width)
+            ).astype(BF16)
+            both[here, width:] = jnp.zeros((rows, width), BF16)
+
+    for i in range(1, len(names)):
+
+        @pl.when(seen[i])
+        def _(i=i):
+            kv_copy(i, slots[i]).wait()
+
+    query_row = lax.broadcasted_iota(jnp.int32, (rows, rows), 0)
+    key_row = lax.broadcasted_iota(jnp.int32, (rows, rows), 1)
+    bias = jnp.where(key_row <= query_row, 0.0, -1e30)
     lane = lax.broadcasted_iota(jnp.int32, (window, HEAD_SIZE), 1)
     row = lax.broadcasted_iota(jnp.int32, (window, HEAD_SIZE), 0)
     one_column = jnp.where((lane == 0) & (row < filled * rows), 1.0, 0.0).astype(BF16)
+    factor = math.log2(math.e) / HEAD_SIZE**0.5
     for g in range(KEY_VALUE_HEADS):
-        values[g, :, HEAD_SIZE:] = one_column
-    for c in copies(0, 0):
-        c.wait()
-    for s in range(1, window // rows):
-
-        @pl.when(s >= filled)
-        def _(s=s):
-            for g in range(KEY_VALUE_HEADS):
-                keys[g, s * rows : (s + 1) * rows, :] = jnp.broadcast_to(
-                    keys[g, :1, :].astype(F32), (rows, HEAD_SIZE)
-                ).astype(BF16)
-                values[g, s * rows : (s + 1) * rows, :HEAD_SIZE] = jnp.zeros(
-                    (rows, HEAD_SIZE), BF16
-                )
-
-    for i in range(1, len(names)):
-
-        @pl.when(seen[i])
-        def _(i=i):
-            for c in copies(i, slots[i]):
-                c.wait()
-
-    query_row = lax.broadcasted_iota(jnp.int32, (rows, rows), 0)
-    key_row = lax.broadcasted_iota(jnp.int32, (rows, rows), 1)
-    bias = jnp.where(key_row <= query_row, 0.0, -1e30)
-    factor = math.log2(math.e) / HEAD_SIZE**0.5
-    heads = 4
-    for first in range(0, QUERY_HEADS, heads):
-        g = first // GROUP
+        first = g * GROUP
         q = jnp.concatenate(
             [
                 q_ref[:, (first + h) * HEAD_SIZE : (first + h + 1) * HEAD_SIZE]
-                for h in range(heads)
+                for h in range(GROUP)
             ],
             axis=0,
         )
-        scores = lax.dot_general(
-            q, keys[g], (((1,), (1,)), ((), ())), preferred_element_type=F32
-        )
-        scores = scores.reshape(heads, rows, window)
-        scores = jnp.concatenate([scores[:, :, :rows] + bias[None], scores[:, :, rows:]], axis=2)
-        top = jnp.max(scores, axis=-1, keepdims=True)
-        probs = jnp.exp2((scores - top) * factor).astype(BF16).reshape(heads * rows, window)
-        summed = jnp.dot(probs, values[g], preferred_element_type=F32)
+        keys = both[:, g * HEAD_SIZE : (g + 1) * HEAD_SIZE]
+        values = jnp.concatenate(
+            [both[:, width + g * HEAD_SIZE : width + (g + 1) * HEAD_SIZE], one_column], axis=1
+        )
+        scores = lax.dot_general(q, keys, (((1,), (1,)), ((), ())), preferred_element_type=F32)
+        near = (scores[:, :rows].reshape(GROUP, rows, rows) + bias[None]).reshape(-1, rows)
+        rest = scores[:, rows:]
+        top = jnp.maximum(
+            jnp.max(near, axis=-1, keepdims=True), jnp.max(rest, axis=-1, keepdims=True)
+        )
+        summed = jnp.dot(
+            jnp.exp2((near - top) * factor).astype(BF16),
+            values[:rows],
+            preferred_element_type=F32,
+        ) + jnp.dot(
+            jnp.exp2((rest - top) * factor).astype(BF16),
+            values[rows:],
+            preferred_element_type=F32,
+        )
         result = (summed[:, :HEAD_SIZE] / summed[:, HEAD_SIZE : HEAD_SIZE + 1]).astype(BF16)
-        for h in range(heads):
+        for h in range(GROUP):
             out_ref[:, (first + h) * HEAD_SIZE : (first + h + 1) * HEAD_SIZE] = result[
                 h * rows : (h + 1) * rows
             ]
 
     for i in range(len(names)):
-        line_copy(i).wait()
-    count = devices * rows // (2 * width)
-    in_row = 2 * width // rows
-    line = lax.broadcasted_iota(jnp.int32, (extra, 2 * width), 0)
-    wanted = (line == own // in_row) | (line == count + own // in_row)
-    picked = []
-    for i in range(len(names)):
-        both = jnp.sum(jnp.where(wanted, lines[i].astype(F32), 0.0), axis=0, keepdims=True)
-        picked.append(
-            sum(
-                jnp.where(own % in_row == n, both[:, n * rows : (n + 1) * rows], 0.0)
-                for n in range(in_row)
+        weight_copy(i).wait()
+    total = []
+    for n in range(parts):
+        here = res_ref[:, 2 * width * n : 2 * width * (n + 1)].astype(F32)
+        for chip in range(devices // 2):
+            pair = jnp.concatenate(
+                [weight[2 * chip + k, n * depth : (n + 1) * depth, :] for k in range(2)], axis=0
             )
-        )
-    picked.append(jnp.zeros((rows - len(names), rows), F32))
-    scale_ref[...] = jnp.transpose(jnp.concatenate(picked, axis=0))
-
-    for i in range(len(names)):
-        for c in weight_copies(i):
-            c.wait()
-    hidden = res_ref[...].astype(F32) + jnp.dot(
-        out_ref[...], weight[...], preferred_element_type=F32
-    )
+            here += jnp.dot(
+                out_ref[:, 2 * depth * chip : 2 * depth * (chip + 1)],
+                pair,
+                preferred_element_type=F32,
+            )
+        total.append(here)
+    hidden = jnp.concatenate(total, axis=1)
     hidden_ref[...] = hidden.astype(BF16)
     mean_square = jnp.mean(hidden * hidden, axis=-1, keepdims=True)
     normed_ref[...] = (
@@ -310,23 +285,17 @@
     window = (min(MOST_BLK, devices) + 1) * rows
     names = piece_names(devices)
     width = KEY_VALUE_HEADS * HEAD_SIZE
+    parts = model // (2 * width)
     shape = jax.ShapeDtypeStruct(residual.shape, BF16)
     return pl.pallas_call(
         functools.partial(attend_kernel, devices),
-        out_shape=(
-            jax.ShapeDtypeStruct(queries.shape, BF16),
-            jax.ShapeDtypeStruct((rows, rows), F32),
-            shape,
-            shape,
-        ),
+        out_shape=(jax.ShapeDtypeStruct(queries.shape, BF16), shape, shape),
         in_specs=[SMEM, SMEM, VMEM, VMEM, VMEM] + [HBM] * (2 * len(names)),
-        out_specs=(VMEM,) * 4,
+        out_specs=(VMEM,) * 3,
         scratch_shapes=[
-            pltpu.VMEM((KEY_VALUE_HEADS, window, HEAD_SIZE), BF16),
-            pltpu.VMEM((KEY_VALUE_HEADS, window, 2 * HEAD_SIZE), BF16),
-            pltpu.VMEM((depth * devices, model), BF16),
-            pltpu.VMEM((len(names), line_rows(devices, rows, width), 2 * width), BF16),
-            pltpu.SemaphoreType.DMA((len(names), 5 + model // (2 * width))),
+            pltpu.VMEM((window, 2 * width), BF16),
+            pltpu.VMEM((devices, parts * depth, 2 * width), BF16),
+            pltpu.SemaphoreType.DMA((len(names), 2)),
         ],
         compiler_params=PARAMS,
         cost_estimate=pl.CostEstimate(
@@ -344,6 +313,51 @@
         *[packed[source_of(name, False, devices)] for name in names],
         *[packed[source_of(name, True, devices)] for name in names],
     )
+
+
+def scales_kernel(devices, rows, width, own_ref, *refs):
+    head_refs, (scale_ref, lines, sems) = refs[:-3], refs[-3:]
+    own = own_ref[0]
+    copies = [
+        pltpu.make_async_copy(ref.at[pl.ds(rows, lines.shape[1]), :], lines.at[i], sems.at[i])
+        for i, ref in enumerate(head_refs)
+    ]
+    for c in copies:
+        c.start()
+    count = devices * rows // (2 * width)
+    in_row = 2 * width // rows
+    line = lax.broadcasted_iota(jnp.int32, (lines.shape[1], 2 * width), 0)
+    wanted = (line == own // in_row) | (line == count + own // in_row)
+    picked = []
+    for i, c in enumerate(copies):
+        c.wait()
+        both = jnp.sum(jnp.where(wanted, lines[i].astype(F32), 0.0), axis=0, keepdims=True)
+        picked.append(
+            sum(
+                jnp.where(own % in_row == n, both[:, n * rows : (n + 1) * rows], 0.0)
+                for n in range(in_row)
+            )
+        )
+    picked.append(jnp.zeros((rows - len(copies), rows), F32))
+    scale_ref[...] = jnp.transpose(jnp.concatenate(picked, axis=0))
+
+
+def expert_scales(own, packed, rows, devices):
+    names = piece_names(devices)
+    width = KEY_VALUE_HEADS * HEAD_SIZE
+    return pl.pallas_call(
+        functools.partial(scales_kernel, devices, rows, width),
+        out_shape=jax.ShapeDtypeStruct((rows, rows), F32),
+        in_specs=[SMEM] + [HBM] * len(names),
+        out_specs=VMEM,
+        scratch_shapes=[
+            pltpu.VMEM((len(names), line_rows(devices, rows, width), 2 * width), BF16),
+            pltpu.SemaphoreType.DMA((len(names),)),
+        ],
+        compiler_params=PARAMS,
+        cost_estimate=pl.CostEstimate(flops=10**6, bytes_accessed=2**19, transcendentals=0),
+        name="expert_scales",
+    )(own, *[packed[source_of(name, False, devices)] for name in names])
 
 
 def expert_kernel(parts, scale_ref, gate_ref, up_ref, down_ref, *refs):
@@ -400,19 +414,14 @@
     )
     rows = queries.shape[0]
     cut = rows + line_rows(devices, rows, token_key_heads.shape[1])
-    attention, scales, hidden, normed = attend(
-        own,
-        doc_of_block,
-        queries,
-        residual,
-        norm_gain,
-        ring_gather(packed, cut, devices),
-        out_weight.shape[0],
-        devices,
+    inputs, _ = ring_gather(packed, cut, devices)
+    attention, hidden, normed = attend(
+        own, doc_of_block, queries, residual, norm_gain, inputs, out_weight.shape[0], devices
     )
+    scales = expert_scales(own, inputs, rows, devices)
 
     half, cut = devices // 4, rows // 2
-    tokens = ring_gather(normed, cut, devices)
+    tokens, scales = ring_gather(normed, cut, devices, scales)
     names = piece_names(devices)
     kept, sent = {}, {}
     for j, group in enumerate(piece_groups(devices // 2)):

time: 122 us -> 117 us (0.959)
  waiting for transfers between devices: 62.6 us -> 58.7 us
    ppermute x4, waiting for transfers between devices: 7.82 us -> 3.9 us  [ring_scatter_sum(): second = [lax.ppermute(others, 'seq', across if j == 1 else ring)]]
    pallas_call x0 -> x1, Pallas kernels: none -> 1.96 us  [expert_scales(): pl.pallas_call(functools.partial(scales_kernel, devices, rows, width), ou...]
    ppermute x4, waiting for transfers between devices: 4.43 us -> 5.88 us  [ring_scatter_sum(): first = [lax.ppermute(total, 'seq', ring)]]
    pallas_call x1, Pallas kernels: 9.62 us -> 8.32 us  [attend(): pl.pallas_call(functools.partial(attend_kernel, devices), out_shape=(jax....]
  transfers between devices with their start and end apart: 47 -> 47, of which waited for: 24 -> 24; matrix products, arithmetic and copies ran while one was open for 1% -> 1% of each run, Pallas kernels for 6% -> 8%
where the time goes in v4:
time: 117 us
  waiting for transfers between devices  58.7 us (50%)
  starting transfers between devices  34.2 us (29%)
  Pallas kernels  19.7 us (17%)
  local copies, waits for them, and re-layouts  1.75 us (1%)
  other arithmetic  1.64 us (1%)
    ppermute x8, waiting for transfers between devices, ring_gather(): first = lax.ppermute(first if j < half else first[cut:], 'seq', ring)  26 us
    ppermute x8, waiting for transfers between devices, ring_gather(): lax.ppermute(second if j < half else second[:cut], 'seq', across if j ==...  21.8 us
    ppermute x8, starting transfers between devices, ring_gather(): first = lax.ppermute(first if j < half else first[cut:], 'seq', ring)  9.66 us
    pallas_call x1, Pallas kernels, attend(): pl.pallas_call(functools.partial(attend_kernel, devices), out_shape=(jax....  8.32 us
    pallas_call x5, Pallas kernels, expert(): pl.pallas_call(functools.partial(expert_kernel, parts), out_shape=(shape,...  7.5 us
    ppermute x8, starting transfers between devices, ring_gather(): lax.ppermute(second if j < half else second[:cut], 'seq', across if j ==...  7.45 us
    ppermute x4, starting transfers between devices, ring_scatter_sum(): first = [lax.ppermute(total, 'seq', ring)]  7.08 us
    ppermute x4, waiting for transfers between devices, ring_scatter_sum(): first = [lax.ppermute(total, 'seq', ring)]  5.88 us
  transfers between devices with their start and end apart: 47, of which 24 were waited for; matrix products, arithmetic and copies ran while one was open for 1% of the time, Pallas kernels for 8%

profile of v4, /device:TPU:0, one launch (start us, length us, event | category | flops | bytes accessed | tf_op | source)
XLA Modules:
  0.0 117.0 jit_solution(8732074708005061136)
XLA Ops:
  0.6 1.9 %pack.1.refs_0_.refs_16_ = bf16[400,512]{1,0:T(8,128)(2,1)} custom-call(bf16[128,256]{1,0:T(8,128)(2,1)} %key_ref.1, bf16[128,256]{1,0:T(8,128)(2,1)} %value_ref.1, s32[8,128]{1,0:T(8,128)} %bitcast.21, f32[8,128]{1,0:T(8,128)} %bitcast.22, bf16[128,1024]{1,0:T(8,128)(2,1)} %out_weight_ref.1), custom_call_target="tpu_custom_call" | custom-call | flops 1000000 | bytes 1048576 | tf_op jit(solution)/shard_map/pack/pallas_call | solution.py:148
  2.5 3.0 %collective-permute-start.1 = (bf16[400,512]{1,0:T(8,128)(2,1)}, bf16[400,512]{1,0:T(8,128)(2,1)S(1)}, u32[]{:S(2)}, u32[]{:S(2)}) collective-permute-start(bf16[400,512]{1,0:T(8,128)(2,1)} %pack.1.refs_0_.refs_16_), channel_id=1, source_target_pairs={{0,4},{1,3},{4,8},{5,1},{8,12},{9,5},{12,14},{13,9},{14,10},{15,13... | collective-permute-start | bytes 1228808 | tf_op jit(solution)/shard_map/ppermute | solution.py:77
  6.2 8.5 %collective-permute-done.1.refs_2_.refs_18_ = bf16[400,512]{1,0:T(8,128)(2,1)S(1)} collective-permute-done((bf16[400,512]{1,0:T(8,128)(2,1)}, bf16[400,512]{1,0:T(8,128)(2,1)S(1)}, u32[]{:S(2)}, u32[]{:S(2)}) %collective-permute-start.1) | collective-permute-done | bytes 409632 | tf_op jit(solution)/shard_map/ppermute | solution.py:77
  14.7 2.4 %collective-permute-start.5 = (bf16[400,512]{1,0:T(8,128)(2,1)S(1)}, bf16[400,512]{1,0:T(8,128)(2,1)S(1)}, u32[]{:S(2)}, u32[]{:S(2)}) collective-permute-start(bf16[400,512]{1,0:T(8,128)(2,1)S(1)} %collective-permute-done.1.refs_2_.refs_18_), channel_id=1, source_target_pairs={{0,4},{1,3},{4,8},{5,1},{8,12},{9,5},{12,14},{13,9},{14,10},{15,13... | collective-permute-start | bytes 1228808 | tf_op jit(solution)/shard_map/ppermute | solution.py:77
  17.1 1.6 %collective-permute-start.6 = (bf16[400,512]{1,0:T(8,128)(2,1)S(1)}, bf16[400,512]{1,0:T(8,128)(2,1)S(1)}, u32[]{:S(2)}, u32[]{:S(2)}) collective-permute-start(bf16[400,512]{1,0:T(8,128)(2,1)S(1)} %collective-permute-done.2.refs_3_.refs_19_), channel_id=1, source_target_pairs={{0,4},{1,3},{4,8},{5,1},{8,12},{9,5},{12,14},{13,9},{14,10},{15,13... | collective-permute-start | bytes 1228808 | tf_op jit(solution)/shard_map/ppermute | solution.py:78
  18.7 5.3 %collective-permute-done.5.refs_6_.refs_22_ = bf16[400,512]{1,0:T(8,128)(2,1)S(1)} collective-permute-done((bf16[400,512]{1,0:T(8,128)(2,1)S(1)}, bf16[400,512]{1,0:T(8,128)(2,1)S(1)}, u32[]{:S(2)}, u32[]{:S(2)}) %collective-permute-start.5) | collective-permute-done | bytes 409632 | tf_op jit(solution)/shard_map/ppermute | solution.py:77
  25.5 2.8 %collective-permute-done.6.refs_7_.refs_23_ = bf16[400,512]{1,0:T(8,128)(2,1)S(1)} collective-permute-done((bf16[400,512]{1,0:T(8,128)(2,1)S(1)}, bf16[400,512]{1,0:T(8,128)(2,1)S(1)}, u32[]{:S(2)}, u32[]{:S(2)}) %collective-permute-start.6) | collective-permute-done | bytes 409632 | tf_op jit(solution)/shard_map/ppermute | solution.py:78
  29.4 3.3 %collective-permute-done.9.refs_10_.refs_26_ = bf16[400,512]{1,0:T(8,128)(2,1)S(1)} collective-permute-done((bf16[400,512]{1,0:T(8,128)(2,1)S(1)}, bf16[400,512]{1,0:T(8,128)(2,1)S(1)}, u32[]{:S(2)}, u32[]{:S(2)}) %collective-permute-start.9) | collective-permute-done | bytes 409632 | tf_op jit(solution)/shard_map/ppermute | solution.py:77
  35.1 2.0 %collective-permute-done.10.refs_11_.refs_27_ = bf16[400,512]{1,0:T(8,128)(2,1)S(1)} collective-permute-done((bf16[400,512]{1,0:T(8,128)(2,1)S(1)}, bf16[400,512]{1,0:T(8,128)(2,1)S(1)}, u32[]{:S(2)}, u32[]{:S(2)}) %collective-permute-start.10) | collective-permute-done | bytes 409632 | tf_op jit(solution)/shard_map/ppermute | solution.py:78
  40.1 2.9 %collective-permute-done.13.refs_15_ = bf16[144,512]{1,0:T(8,128)(2,1)S(1)} collective-permute-done((bf16[144,512]{1,0:T(8,128)(2,1)S(1)}, bf16[144,512]{1,0:T(8,128)(2,1)S(1)}, u32[]{:S(2)}, u32[]{:S(2)}) %collective-permute-start.13) | collective-permute-done | bytes 147488 | tf_op jit(solution)/shard_map/ppermute | solution.py:78
  44.6 8.3 %attend.1 = (bf16[128,2048]{1,0:T(8,128)(2,1)}, bf16[128,1024]{1,0:T(8,128)(2,1)}, bf16[128,1024]{1,0:T(8,128)(2,1)}) custom-call(s32[1]{0:T(128)} %bitcast.own_ref, s32[16]{0:T(128)} %doc_ref.1, bf16[128,2048]{1,0:T(8,128)(2,1)} %q_ref.1, bf16[128,1024]{1,0:T(8,128)(2,1)} %res_ref.1, bf16[1,1024]{1,0:T(2,128)(2,1)} %reshape.13.gain_ref, ...), custom_call_target="tpu_custom_call" | custom-call | flops 1744830464 | bytes 8388608 | tf_op jit(solution)/shard_map/attend/pallas_call | solution.py:290
  52.9 2.0 %collective-permute-start.22 = (bf16[128,1024]{1,0:T(8,128)(2,1)}, bf16[128,1024]{1,0:T(8,128)(2,1)S(1)}, u32[]{:S(2)}, u32[]{:S(2)}) collective-permute-start(bf16[128,1024]{1,0:T(8,128)(2,1)} %get-tuple-element.27.refs_0_), channel_id=1, source_target_pairs={{1,4},{0,3},{5,8},{4,1},{9,12},{8,5},{13,14},{12,9},{15,10},{14,13... | collective-permute-start | bytes 786440 | tf_op jit(solution)/shard_map/ppermute | solution.py:78
  54.9 6.5 %collective-permute-done.22.refs_1_ = bf16[128,1024]{1,0:T(8,128)(2,1)S(1)} collective-permute-done((bf16[128,1024]{1,0:T(8,128)(2,1)}, bf16[128,1024]{1,0:T(8,128)(2,1)S(1)}, u32[]{:S(2)}, u32[]{:S(2)}) %collective-permute-start.22) | collective-permute-done | bytes 262176 | tf_op jit(solution)/shard_map/ppermute | solution.py:78
  62.0 1.5 %collective-permute-start.18 = (bf16[128,1024]{1,0:T(8,128)(2,1)S(1)}, bf16[128,1024]{1,0:T(8,128)(2,1)S(1)}, u32[]{:S(2)}, u32[]{:S(2)}) collective-permute-start(bf16[128,1024]{1,0:T(8,128)(2,1)S(1)} %collective-permute-done.17.refs_0_), channel_id=1, source_target_pairs={{0,4},{1,3},{4,8},{5,1},{8,12},{9,5},{12,14},{13,9},{14,10},{15,13... | collective-permute-start | bytes 786440 | tf_op jit(solution)/shard_map/ppermute | solution.py:77
  63.5 4.3 %collective-permute-done.26.refs_1_ = bf16[128,1024]{1,0:T(8,128)(2,1)S(1)} collective-permute-done((bf16[128,1024]{1,0:T(8,128)(2,1)S(1)}, bf16[128,1024]{1,0:T(8,128)(2,1)S(1)}, u32[]{:S(2)}, u32[]{:S(2)}) %collective-permute-start.26) | collective-permute-done | bytes 262176 | tf_op jit(solution)/shard_map/ppermute | solution.py:78
  68.1 2.6 %collective-permute-done.18.refs_0_ = bf16[128,1024]{1,0:T(8,128)(2,1)S(1)} collective-permute-done((bf16[128,1024]{1,0:T(8,128)(2,1)S(1)}, bf16[128,1024]{1,0:T(8,128)(2,1)S(1)}, u32[]{:S(2)}, u32[]{:S(2)}) %collective-permute-start.18) | collective-permute-done | bytes 262176 | tf_op jit(solution)/shard_map/ppermute | solution.py:77
  70.9 2.0 %expert_scales.1.scale_ref = f32[128,128]{1,0:T(8,128)} custom-call(s32[1]{0:T(128)} %bitcast.own_ref, bf16[400,512]{1,0:T(8,128)(2,1)} %pack.1.refs_0_.refs_16_, bf16[400,512]{1,0:T(8,128)(2,1)} %copy-done.11, bf16[400,512]{1,0:T(8,128)(2,1)} %copy-done.7, bf16[400,512]{1,0:T(8,128)(2,1)} %copy-done.8, bf16[400,512]{1,0:T(8,128)(2,1)} %copy-done.13, ...), custom_call_target="tpu_custom_call" | custom-call | flops 1000000 | bytes 524288 | tf_op jit(solution)/shard_map/expert_scales/pallas_call | solution.py:348
  74.7 2.3 %collective-permute-done.19.refs_0_ = bf16[128,1024]{1,0:T(8,128)(2,1)S(1)} collective-permute-done((bf16[128,1024]{1,0:T(8,128)(2,1)S(1)}, bf16[128,1024]{1,0:T(8,128)(2,1)S(1)}, u32[]{:S(2)}, u32[]{:S(2)}) %collective-permute-start.19) | collective-permute-done | bytes 262176 | tf_op jit(solution)/shard_map/ppermute | solution.py:77
  77.3 1.9 %collective-permute-done.35.refs_1_ = bf16[64,1024]{1,0:T(8,128)(2,1)S(1)} collective-permute-done((bf16[64,1024]{1,0:T(8,128)(2,1)S(1)}, bf16[64,1024]{1,0:T(8,128)(2,1)S(1)}, u32[]{:S(2)}, u32[]{:S(2)}) %collective-permute-start.35) | collective-permute-done | bytes 131104 | tf_op jit(solution)/shard_map/ppermute | solution.py:78
  79.2 2.8 %collective-permute-done.34.refs_0_ = bf16[64,1024]{1,0:T(8,128)(2,1)S(1)} collective-permute-done((bf16[64,1024]{1,0:T(8,128)(2,1)S(1)}, bf16[64,1024]{1,0:T(8,128)(2,1)S(1)}, u32[]{:S(2)}, u32[]{:S(2)}) %collective-permute-start.34) | collective-permute-done | bytes 131104 | tf_op jit(solution)/shard_map/ppermute | solution.py:77
  85.2 1.8 %expert.8 = (bf16[256,1024]{1,0:T(8,128)(2,1)S(1)}, bf16[256,1024]{1,0:T(8,128)(2,1)S(1)}) custom-call(f32[128,128]{1,0:T(8,128)S(1)} %copy-done.3, bf16[1024,384]{1,0:T(8,128)(2,1)S(1)} %bitcast.7, bf16[1024,384]{1,0:T(8,128)(2,1)S(1)} %bitcast.12, bf16[384,1024]{1,0:T(8,128)(2,1)S(1)} %bitcast.17, bf16[128,1024]{1,0:T(8,128)(2,1)S(1)} %collective-permute-done.19.refs_0_, ...), custom_call_target="tpu_custom_call" | custom-call | flops 1207959552 | bytes 4194304 | tf_op jit(solution)/shard_map/expert/pallas_call | solution.py:381
  87.5 1.8 %collective-permute-start.43 = (bf16[64,1024]{1,0:T(8,128)(2,1)S(1)}, bf16[64,1024]{1,0:T(8,128)(2,1)S(1)}, u32[]{:S(2)}, u32[]{:S(2)}) collective-permute-start(bf16[64,1024]{1,0:T(8,128)(2,1)S(1)} %add_convert_fusion.7), channel_id=1, source_target_pairs={{4,0},{3,1},{8,4},{1,5},{12,8},{5,9},{14,12},{9,13},{10,14},{13,15... | collective-permute-start | bytes 393224 | tf_op jit(solution)/shard_map/ppermute | solution.py:110
  89.4 1.7 %collective-permute-start.39 = (bf16[64,1024]{1,0:T(8,128)(2,1)S(1)}, bf16[64,1024]{1,0:T(8,128)(2,1)S(1)}, u32[]{:S(2)}, u32[]{:S(2)}) collective-permute-start(bf16[64,1024]{1,0:T(8,128)(2,1)S(1)} %add_convert_fusion.8), channel_id=1, source_target_pairs={{4,0},{3,1},{8,4},{1,5},{12,8},{5,9},{14,12},{9,13},{10,14},{13,15... | collective-permute-start | bytes 393224 | tf_op jit(solution)/shard_map/ppermute | solution.py:109
  91.6 1.8 %expert.7 = (bf16[256,1024]{1,0:T(8,128)(2,1)S(1)}, bf16[256,1024]{1,0:T(8,128)(2,1)S(1)}) custom-call(f32[128,128]{1,0:T(8,128)S(1)} %copy-done.3, bf16[1024,384]{1,0:T(8,128)(2,1)S(1)} %bitcast.8, bf16[1024,384]{1,0:T(8,128)(2,1)S(1)} %bitcast.13, bf16[384,1024]{1,0:T(8,128)(2,1)S(1)} %bitcast.18, bf16[128,1024]{1,0:T(8,128)(2,1)S(1)} %collective-permute-done.18.refs_0_, ...), custom_call_target="tpu_custom_call" | custom-call | flops 1207959552 | bytes 4194304 | tf_op jit(solution)/shard_map/expert/pallas_call | solution.py:381
  94.4 1.8 %collective-permute-start.40 = (bf16[128,1024]{1,0:T(8,128)(2,1)S(1)}, bf16[128,1024]{1,0:T(8,128)(2,1)S(1)}, u32[]{:S(2)}, u32[]{:S(2)}) collective-permute-start(bf16[128,1024]{1,0:T(8,128)(2,1)S(1)} %add_convert_fusion.6), channel_id=1, source_target_pairs={{4,0},{3,1},{8,4},{1,5},{12,8},{5,9},{14,12},{9,13},{10,14},{13,15... | collective-permute-start | bytes 786440 | tf_op jit(solution)/shard_map/ppermute | solution.py:109
  96.4 1.5 %collective-permute-start.44 = (bf16[128,1024]{1,0:T(8,128)(2,1)S(1)}, bf16[128,1024]{1,0:T(8,128)(2,1)S(1)}, u32[]{:S(2)}, u32[]{:S(2)}) collective-permute-start(bf16[128,1024]{1,0:T(8,128)(2,1)S(1)} %add_convert_fusion.3), channel_id=1, source_target_pairs={{4,0},{3,1},{8,4},{1,5},{12,8},{5,9},{14,12},{9,13},{10,14},{13,15... | collective-permute-start | bytes 786440 | tf_op jit(solution)/shard_map/ppermute | solution.py:110
  97.9 1.8 %expert.6 = (bf16[256,1024]{1,0:T(8,128)(2,1)S(1)}, bf16[256,1024]{1,0:T(8,128)(2,1)S(1)}) custom-call(f32[128,128]{1,0:T(8,128)S(1)} %copy-done.3, bf16[1024,384]{1,0:T(8,128)(2,1)S(1)} %bitcast.9, bf16[1024,384]{1,0:T(8,128)(2,1)S(1)} %bitcast.14, bf16[384,1024]{1,0:T(8,128)(2,1)S(1)} %bitcast.19, bf16[128,1024]{1,0:T(8,128)(2,1)S(1)} %collective-permute-done.17.refs_0_, ...), custom_call_target="tpu_custom_call" | custom-call | flops 1207959552 | bytes 4194304 | tf_op jit(solution)/shard_map/expert/pallas_call | solution.py:381
  101.0 1.8 %collective-permute-start.41 = (bf16[128,1024]{1,0:T(8,128)(2,1)S(1)}, bf16[128,1024]{1,0:T(8,128)(2,1)S(1)}, u32[]{:S(2)}, u32[]{:S(2)}) collective-permute-start(bf16[128,1024]{1,0:T(8,128)(2,1)S(1)} %add_convert_fusion.5), channel_id=1, source_target_pairs={{4,0},{3,1},{8,4},{1,5},{12,8},{5,9},{14,12},{9,13},{10,14},{13,15... | collective-permute-start | bytes 786440 | tf_op jit(solution)/shard_map/ppermute | solution.py:109
  103.8 1.8 %collective-permute-start.45 = (bf16[128,1024]{1,0:T(8,128)(2,1)S(1)}, bf16[128,1024]{1,0:T(8,128)(2,1)S(1)}, u32[]{:S(2)}, u32[]{:S(2)}) collective-permute-start(bf16[128,1024]{1,0:T(8,128)(2,1)S(1)} %add_convert_fusion.2), channel_id=1, source_target_pairs={{4,0},{3,1},{8,4},{1,5},{12,8},{5,9},{14,12},{9,13},{10,14},{13,15... | collective-permute-start | bytes 786440 | tf_op jit(solution)/shard_map/ppermute | solution.py:110
  107.6 1.8 %collective-permute-start.42 = (bf16[128,1024]{1,0:T(8,128)(2,1)S(1)}, bf16[128,1024]{1,0:T(8,128)(2,1)S(1)}, u32[]{:S(2)}, u32[]{:S(2)}) collective-permute-start(bf16[128,1024]{1,0:T(8,128)(2,1)S(1)} %add_convert_fusion.4), channel_id=1, source_target_pairs={{4,0},{3,1},{8,4},{1,5},{12,8},{5,9},{14,12},{9,13},{10,14},{13,15... | collective-permute-start | bytes 786440 | tf_op jit(solution)/shard_map/ppermute | solution.py:109
  110.6 3.4 %collective-permute-done.42 = bf16[128,1024]{1,0:T(8,128)(2,1)S(1)} collective-permute-done((bf16[128,1024]{1,0:T(8,128)(2,1)S(1)}, bf16[128,1024]{1,0:T(8,128)(2,1)S(1)}, u32[]{:S(2)}, u32[]{:S(2)}) %collective-permute-start.42) | collective-permute-done | bytes 262176 | tf_op jit(solution)/shard_map/ppermute | solution.py:109
  114.1 2.1 %collective-permute-done.46 = bf16[128,1024]{1,0:T(8,128)(2,1)S(1)} collective-permute-done((bf16[128,1024]{1,0:T(8,128)(2,1)S(1)}, bf16[128,1024]{1,0:T(8,128)(2,1)S(1)}, u32[]{:S(2)}, u32[]{:S(2)}) %collective-permute-start.46) | collective-permute-done | bytes 262176 | tf_op jit(solution)/shard_map/ppermute | solution.py:110
  (124 shorter events, 25.1 us)
Async XLA Ops:
  2.5 12.2 %collective-permute-start.1 = (bf16[400,512]{1,0:T(8,128)(2,1)}, bf16[400,512]{1,0:T(8,128)(2,1)S(1)}, u32[]{:S(2)}, u32[]{:S(2)}) collective-permute-start(bf16[400,512]{1,0:T(8,128)(2,1)} %pack.1.refs_0_.refs_16_), channel_id=1, source_target_pairs={{0,4},{1,3},{4,8},{5,1},{8,12},{9,5},{12,14},{13,9},{14,10},{15,13... | collective-permute-start | bytes 1228808 | tf_op jit(solution)/shard_map/ppermute | solution.py:77
  5.5 11.6 %collective-permute-start.2 = (bf16[400,512]{1,0:T(8,128)(2,1)}, bf16[400,512]{1,0:T(8,128)(2,1)S(1)}, u32[]{:S(2)}, u32[]{:S(2)}) collective-permute-start(bf16[400,512]{1,0:T(8,128)(2,1)} %pack.1.refs_0_.refs_16_), channel_id=1, source_target_pairs={{1,4},{0,3},{5,8},{4,1},{9,12},{8,5},{13,14},{12,9},{15,10},{14,13... | collective-permute-start | bytes 1228808 | tf_op jit(solution)/shard_map/ppermute | solution.py:78
  14.7 9.2 %collective-permute-start.5 = (bf16[400,512]{1,0:T(8,128)(2,1)S(1)}, bf16[400,512]{1,0:T(8,128)(2,1)S(1)}, u32[]{:S(2)}, u32[]{:S(2)}) collective-permute-start(bf16[400,512]{1,0:T(8,128)(2,1)S(1)} %collective-permute-done.1.refs_2_.refs_18_), channel_id=1, source_target_pairs={{0,4},{1,3},{4,8},{5,1},{8,12},{9,5},{12,14},{13,9},{14,10},{15,13... | collective-permute-start | bytes 1228808 | tf_op jit(solution)/shard_map/ppermute | solution.py:77
  17.1 11.2 %collective-permute-start.6 = (bf16[400,512]{1,0:T(8,128)(2,1)S(1)}, bf16[400,512]{1,0:T(8,128)(2,1)S(1)}, u32[]{:S(2)}, u32[]{:S(2)}) collective-permute-start(bf16[400,512]{1,0:T(8,128)(2,1)S(1)} %collective-permute-done.2.refs_3_.refs_19_), channel_id=1, source_target_pairs={{0,4},{1,3},{4,8},{5,1},{8,12},{9,5},{12,14},{13,9},{14,10},{15,13... | collective-permute-start | bytes 1228808 | tf_op jit(solution)/shard_map/ppermute | solution.py:78
  23.9 8.8 %collective-permute-start.9 = (bf16[400,512]{1,0:T(8,128)(2,1)S(1)}, bf16[400,512]{1,0:T(8,128)(2,1)S(1)}, u32[]{:S(2)}, u32[]{:S(2)}) collective-permute-start(bf16[400,512]{1,0:T(8,128)(2,1)S(1)} %collective-permute-done.5.refs_6_.refs_22_), channel_id=1, source_target_pairs={{0,4},{1,3},{4,8},{5,1},{8,12},{9,5},{12,14},{13,9},{14,10},{15,13... | collective-permute-start | bytes 1228808 | tf_op jit(solution)/shard_map/ppermute | solution.py:77
  25.0 7.7 %collective-permute-start = (bf16[400,512]{1,0:T(8,128)(2,1)}, bf16[400,512]{1,0:T(8,128)(2,1)S(1)}, u32[]{:S(2)}, u32[]{:S(2)}) collective-permute-start(bf16[400,512]{1,0:T(8,128)(2,1)} %pack.1.refs_0_.refs_16_), channel_id=1, source_target_pairs={{0,1},{1,0},{2,3},{3,2},{4,5},{5,4},{6,7},{7,6},{8,9},{9,8},{10,11... | collective-permute-start | bytes 1228808 | tf_op jit(solution)/shard_map/ppermute | solution.py:82
  25.0 8.9 %collective-permute-start.4 = (bf16[400,512]{1,0:T(8,128)(2,1)S(1)}, bf16[400,512]{1,0:T(8,128)(2,1)S(1)}, u32[]{:S(2)}, u32[]{:S(2)}) collective-permute-start(bf16[400,512]{1,0:T(8,128)(2,1)S(1)} %collective-permute-done.2.refs_3_.refs_19_), channel_id=1, source_target_pairs={{0,1},{1,0},{2,3},{3,2},{4,5},{5,4},{6,7},{7,6},{8,9},{9,8},{10,11... | collective-permute-start | bytes 1228808 | tf_op jit(solution)/shard_map/ppermute | solution.py:85
  28.3 8.8 %collective-permute-start.10 = (bf16[400,512]{1,0:T(8,128)(2,1)S(1)}, bf16[400,512]{1,0:T(8,128)(2,1)S(1)}, u32[]{:S(2)}, u32[]{:S(2)}) collective-permute-start(bf16[400,512]{1,0:T(8,128)(2,1)S(1)} %collective-permute-done.6.refs_7_.refs_23_), channel_id=1, source_target_pairs={{0,4},{1,3},{4,8},{5,1},{8,12},{9,5},{12,14},{13,9},{14,10},{15,13... | collective-permute-start | bytes 1228808 | tf_op jit(solution)/shard_map/ppermute | solution.py:78
  29.4 7.7 %collective-permute-start.3 = (bf16[400,512]{1,0:T(8,128)(2,1)S(1)}, bf16[400,512]{1,0:T(8,128)(2,1)S(1)}, u32[]{:S(2)}, u32[]{:S(2)}) collective-permute-start(bf16[400,512]{1,0:T(8,128)(2,1)S(1)} %collective-permute-done.1.refs_2_.refs_18_), channel_id=1, source_target_pairs={{0,1},{1,0},{2,3},{3,2},{4,5},{5,4},{6,7},{7,6},{8,9},{9,8},{10,11... | collective-permute-start | bytes 1228808 | tf_op jit(solution)/shard_map/ppermute | solution.py:84
  32.8 7.3 %collective-permute-start.15 = (bf16[256,512]{1,0:T(8,128)(2,1)S(1)}, bf16[256,512]{1,0:T(8,128)(2,1)}, u32[]{:S(2)}, u32[]{:S(2)}) collective-permute-start(bf16[256,512]{1,0:T(8,128)(2,1)S(1)} %slice.81), channel_id=1, source_target_pairs={{0,4},{1,3},{4,8},{5,1},{8,12},{9,5},{12,14},{13,9},{14,10},{15,13... | collective-permute-start | bytes 786440 | tf_op jit(solution)/shard_map/ppermute | solution.py:77
  33.9 10.5 %collective-permute-start.7 = (bf16[400,512]{1,0:T(8,128)(2,1)S(1)}, bf16[400,512]{1,0:T(8,128)(2,1)}, u32[]{:S(2)}, u32[]{:S(2)}) collective-permute-start(bf16[400,512]{1,0:T(8,128)(2,1)S(1)} %collective-permute-done.5.refs_6_.refs_22_), channel_id=1, source_target_pairs={{0,1},{1,0},{2,3},{3,2},{4,5},{5,4},{6,7},{7,6},{8,9},{9,8},{10,11... | collective-permute-start | bytes 1228808 | tf_op jit(solution)/shard_map/ppermute | solution.py:84
  37.1 7.4 %collective-permute-start.12 = (bf16[400,512]{1,0:T(8,128)(2,1)S(1)}, bf16[400,512]{1,0:T(8,128)(2,1)}, u32[]{:S(2)}, u32[]{:S(2)}) collective-permute-start(bf16[400,512]{1,0:T(8,128)(2,1)S(1)} %collective-permute-done.10.refs_11_.refs_27_), channel_id=1, source_target_pairs={{0,1},{1,0},{2,3},{3,2},{4,5},{5,4},{6,7},{7,6},{8,9},{9,8},{10,11... | collective-permute-start | bytes 1228808 | tf_op jit(solution)/shard_map/ppermute | solution.py:85
  37.1 7.4 %collective-permute-start.11 = (bf16[400,512]{1,0:T(8,128)(2,1)S(1)}, bf16[400,512]{1,0:T(8,128)(2,1)}, u32[]{:S(2)}, u32[]{:S(2)}) collective-permute-start(bf16[400,512]{1,0:T(8,128)(2,1)S(1)} %collective-permute-done.9.refs_10_.refs_26_), channel_id=1, source_target_pairs={{0,1},{1,0},{2,3},{3,2},{4,5},{5,4},{6,7},{7,6},{8,9},{9,8},{10,11... | collective-permute-start | bytes 1228808 | tf_op jit(solution)/shard_map/ppermute | solution.py:84
  52.9 8.5 %collective-permute-start.22 = (bf16[128,1024]{1,0:T(8,128)(2,1)}, bf16[128,1024]{1,0:T(8,128)(2,1)S(1)}, u32[]{:S(2)}, u32[]{:S(2)}) collective-permute-start(bf16[128,1024]{1,0:T(8,128)(2,1)} %get-tuple-element.27.refs_0_), channel_id=1, source_target_pairs={{1,4},{0,3},{5,8},{4,1},{9,12},{8,5},{13,14},{12,9},{15,10},{14,13... | collective-permute-start | bytes 786440 | tf_op jit(solution)/shard_map/ppermute | solution.py:78
  54.9 7.1 %collective-permute-start.17 = (bf16[128,1024]{1,0:T(8,128)(2,1)}, bf16[128,1024]{1,0:T(8,128)(2,1)S(1)}, u32[]{:S(2)}, u32[]{:S(2)}) collective-permute-start(bf16[128,1024]{1,0:T(8,128)(2,1)} %get-tuple-element.27.refs_0_), channel_id=1, source_target_pairs={{0,4},{1,3},{4,8},{5,1},{8,12},{9,5},{12,14},{13,9},{14,10},{15,13... | collective-permute-start | bytes 786440 | tf_op jit(solution)/shard_map/ppermute | solution.py:77
  61.4 6.4 %collective-permute-start.26 = (bf16[128,1024]{1,0:T(8,128)(2,1)S(1)}, bf16[128,1024]{1,0:T(8,128)(2,1)S(1)}, u32[]{:S(2)}, u32[]{:S(2)}) collective-permute-start(bf16[128,1024]{1,0:T(8,128)(2,1)S(1)} %collective-permute-done.22.refs_1_), channel_id=1, source_target_pairs={{0,4},{1,3},{4,8},{5,1},{8,12},{9,5},{12,14},{13,9},{14,10},{15,13... | collective-permute-start | bytes 786440 | tf_op jit(solution)/shard_map/ppermute | solution.py:78
  62.0 8.6 %collective-permute-start.18 = (bf16[128,1024]{1,0:T(8,128)(2,1)S(1)}, bf16[128,1024]{1,0:T(8,128)(2,1)S(1)}, u32[]{:S(2)}, u32[]{:S(2)}) collective-permute-start(bf16[128,1024]{1,0:T(8,128)(2,1)S(1)} %collective-permute-done.17.refs_0_), channel_id=1, source_target_pairs={{0,4},{1,3},{4,8},{5,1},{8,12},{9,5},{12,14},{13,9},{14,10},{15,13... | collective-permute-start | bytes 786440 | tf_op jit(solution)/shard_map/ppermute | solution.py:77
  67.8 6.4 %collective-permute-start.30 = (bf16[128,1024]{1,0:T(8,128)(2,1)S(1)}, bf16[128,1024]{1,0:T(8,128)(2,1)S(1)}, u32[]{:S(2)}, u32[]{:S(2)}) collective-permute-start(bf16[128,1024]{1,0:T(8,128)(2,1)S(1)} %collective-permute-done.26.refs_1_), channel_id=1, source_target_pairs={{0,4},{1,3},{4,8},{5,1},{8,12},{9,5},{12,14},{13,9},{14,10},{15,13... | collective-permute-start | bytes 786440 | tf_op jit(solution)/shard_map/ppermute | solution.py:78
  70.6 6.4 %collective-permute-start.19 = (bf16[128,1024]{1,0:T(8,128)(2,1)S(1)}, bf16[128,1024]{1,0:T(8,128)(2,1)S(1)}, u32[]{:S(2)}, u32[]{:S(2)}) collective-permute-start(bf16[128,1024]{1,0:T(8,128)(2,1)S(1)} %collective-permute-done.18.refs_0_), channel_id=1, source_target_pairs={{0,4},{1,3},{4,8},{5,1},{8,12},{9,5},{12,14},{13,9},{14,10},{15,13... | collective-permute-start | bytes 786440 | tf_op jit(solution)/shard_map/ppermute | solution.py:77
  84.7 6.4 %collective-permute-start.28 = (bf16[128,1024]{1,0:T(8,128)(2,1)S(1)}, bf16[128,1024]{1,0:T(8,128)(2,1)S(1)}, u32[]{:S(2)}, u32[]{:S(2)}) collective-permute-start(bf16[128,1024]{1,0:T(8,128)(2,1)S(1)} %collective-permute-done.26.refs_1_), channel_id=1, source_target_pairs={{0,1},{1,0},{2,3},{3,2},{4,5},{5,4},{6,7},{7,6},{8,9},{9,8},{10,11... | collective-permute-start | bytes 786440 | tf_op jit(solution)/shard_map/ppermute | solution.py:85
  85.0 6.1 %collective-permute-start.27 = (bf16[128,1024]{1,0:T(8,128)(2,1)S(1)}, bf16[128,1024]{1,0:T(8,128)(2,1)S(1)}, u32[]{:S(2)}, u32[]{:S(2)}) collective-permute-start(bf16[128,1024]{1,0:T(8,128)(2,1)S(1)} %collective-permute-done.18.refs_0_), channel_id=1, source_target_pairs={{0,1},{1,0},{2,3},{3,2},{4,5},{5,4},{6,7},{7,6},{8,9},{9,8},{10,11... | collective-permute-start | bytes 786440 | tf_op jit(solution)/shard_map/ppermute | solution.py:84
  87.0 7.4 %collective-permute-start.33 = (bf16[256,1024]{1,0:T(8,128)(2,1)S(1)}, bf16[256,1024]{1,0:T(8,128)(2,1)S(1)}, u32[]{:S(2)}, u32[]{:S(2)}) collective-permute-start(bf16[256,1024]{1,0:T(8,128)(2,1)S(1)} %get-tuple-element.36), channel_id=1, source_target_pairs={{0,1},{1,0},{2,3},{3,2},{4,5},{5,4},{6,7},{7,6},{8,9},{9,8},{10,11... | collective-permute-start | bytes 1572872 | tf_op jit(solution)/shard_map/ppermute | solution.py:98
  87.5 5.9 %collective-permute-start.43 = (bf16[64,1024]{1,0:T(8,128)(2,1)S(1)}, bf16[64,1024]{1,0:T(8,128)(2,1)S(1)}, u32[]{:S(2)}, u32[]{:S(2)}) collective-permute-start(bf16[64,1024]{1,0:T(8,128)(2,1)S(1)} %add_convert_fusion.7), channel_id=1, source_target_pairs={{4,0},{3,1},{8,4},{1,5},{12,8},{5,9},{14,12},{9,13},{10,14},{13,15... | collective-permute-start | bytes 393224 | tf_op jit(solution)/shard_map/ppermute | solution.py:110
  91.1 14.5 %collective-permute-start.20 = (bf16[128,1024]{1,0:T(8,128)(2,1)S(1)}, bf16[128,1024]{1,0:T(8,128)(2,1)S(1)}, u32[]{:S(2)}, u32[]{:S(2)}) collective-permute-start(bf16[128,1024]{1,0:T(8,128)(2,1)S(1)} %copy-done.4), channel_id=1, source_target_pairs={{0,1},{1,0},{2,3},{3,2},{4,5},{5,4},{6,7},{7,6},{8,9},{9,8},{10,11... | collective-permute-start | bytes 786440 | tf_op jit(solution)/shard_map/ppermute | solution.py:82
  94.3 5.4 %collective-permute-start.29 = (bf16[256,1024]{1,0:T(8,128)(2,1)S(1)}, bf16[256,1024]{1,0:T(8,128)(2,1)S(1)}, u32[]{:S(2)}, u32[]{:S(2)}) collective-permute-start(bf16[256,1024]{1,0:T(8,128)(2,1)S(1)} %get-tuple-element.34), channel_id=1, source_target_pairs={{0,1},{1,0},{2,3},{3,2},{4,5},{5,4},{6,7},{7,6},{8,9},{9,8},{10,11... | collective-permute-start | bytes 1572872 | tf_op jit(solution)/shard_map/ppermute | solution.py:98
  94.4 6.4 %collective-permute-start.40 = (bf16[128,1024]{1,0:T(8,128)(2,1)S(1)}, bf16[128,1024]{1,0:T(8,128)(2,1)S(1)}, u32[]{:S(2)}, u32[]{:S(2)}) collective-permute-start(bf16[128,1024]{1,0:T(8,128)(2,1)S(1)} %add_convert_fusion.6), channel_id=1, source_target_pairs={{4,0},{3,1},{8,4},{1,5},{12,8},{5,9},{14,12},{9,13},{10,14},{13,15... | collective-permute-start | bytes 786440 | tf_op jit(solution)/shard_map/ppermute | solution.py:109
  96.4 7.3 %collective-permute-start.44 = (bf16[128,1024]{1,0:T(8,128)(2,1)S(1)}, bf16[128,1024]{1,0:T(8,128)(2,1)S(1)}, u32[]{:S(2)}, u32[]{:S(2)}) collective-permute-start(bf16[128,1024]{1,0:T(8,128)(2,1)S(1)} %add_convert_fusion.3), channel_id=1, source_target_pairs={{4,0},{3,1},{8,4},{1,5},{12,8},{5,9},{14,12},{9,13},{10,14},{13,15... | collective-permute-start | bytes 786440 | tf_op jit(solution)/shard_map/ppermute | solution.py:110
  99.7 7.0 %collective-permute-start.25 = (bf16[256,1024]{1,0:T(8,128)(2,1)S(1)}, bf16[256,1024]{1,0:T(8,128)(2,1)S(1)}, u32[]{:S(2)}, u32[]{:S(2)}) collective-permute-start(bf16[256,1024]{1,0:T(8,128)(2,1)S(1)} %get-tuple-element.32), channel_id=1, source_target_pairs={{0,1},{1,0},{2,3},{3,2},{4,5},{5,4},{6,7},{7,6},{8,9},{9,8},{10,11... | collective-permute-start | bytes 1572872 | tf_op jit(solution)/shard_map/ppermute | solution.py:98
  101.0 6.4 %collective-permute-start.41 = (bf16[128,1024]{1,0:T(8,128)(2,1)S(1)}, bf16[128,1024]{1,0:T(8,128)(2,1)S(1)}, u32[]{:S(2)}, u32[]{:S(2)}) collective-permute-start(bf16[128,1024]{1,0:T(8,128)(2,1)S(1)} %add_convert_fusion.5), channel_id=1, source_target_pairs={{4,0},{3,1},{8,4},{1,5},{12,8},{5,9},{14,12},{9,13},{10,14},{13,15... | collective-permute-start | bytes 786440 | tf_op jit(solution)/shard_map/ppermute | solution.py:109
  103.8 6.4 %collective-permute-start.45 = (bf16[128,1024]{1,0:T(8,128)(2,1)S(1)}, bf16[128,1024]{1,0:T(8,128)(2,1)S(1)}, u32[]{:S(2)}, u32[]{:S(2)}) collective-permute-start(bf16[128,1024]{1,0:T(8,128)(2,1)S(1)} %add_convert_fusion.2), channel_id=1, source_target_pairs={{4,0},{3,1},{8,4},{1,5},{12,8},{5,9},{14,12},{9,13},{10,14},{13,15... | collective-permute-start | bytes 786440 | tf_op jit(solution)/shard_map/ppermute | solution.py:110
  107.6 6.4 %collective-permute-start.42 = (bf16[128,1024]{1,0:T(8,128)(2,1)S(1)}, bf16[128,1024]{1,0:T(8,128)(2,1)S(1)}, u32[]{:S(2)}, u32[]{:S(2)}) collective-permute-start(bf16[128,1024]{1,0:T(8,128)(2,1)S(1)} %add_convert_fusion.4), channel_id=1, source_target_pairs={{4,0},{3,1},{8,4},{1,5},{12,8},{5,9},{14,12},{9,13},{10,14},{13,15... | collective-permute-start | bytes 786440 | tf_op jit(solution)/shard_map/ppermute | solution.py:109
  110.4 5.9 %collective-permute-start.46 = (bf16[128,1024]{1,0:T(8,128)(2,1)S(1)}, bf16[128,1024]{1,0:T(8,128)(2,1)S(1)}, u32[]{:S(2)}, u32[]{:S(2)}) collective-permute-start(bf16[128,1024]{1,0:T(8,128)(2,1)S(1)} %add_convert_fusion.1), channel_id=1, source_target_pairs={{4,1},{3,0},{8,5},{1,4},{12,9},{5,8},{14,13},{9,12},{10,15},{13,14... | collective-permute-start | bytes 786440 | tf_op jit(solution)/shard_map/ppermute | solution.py:110
  (32 other events, 245.8 us)

commit v5 on v4

--- a/solution.py
+++ b/solution.py
@@ -48,15 +48,6 @@
     return names + [(-(devices // 4), 0), (-(devices // 4), 1)]
 
 
-def source_of(name, tail, devices):
-    half = devices // 4
-    if name == (-half, 0):
-        return name if tail else (half, 0)
-    if name == (-half, 1):
-        return (half, 1) if tail else name
-    return name
-
-
 def block_of(own, name, devices):
     chips = devices // 2
     chip, core = own // 2, own % 2
@@ -66,7 +57,7 @@
     return 2 * chip + (core if name[1] == 0 else 1 - core)
 
 
-def ring_gather(piece, cut, devices, aside=None):
+def ring_gather(piece, cut, devices, aside=None, before=None):
     half = devices // 4
     (ring, across), swap = ring_steps(devices // 2), swap_steps(devices)
     pieces = {(0, 0): piece}
@@ -74,6 +65,8 @@
     for j in range(1, half + 1):
         if j == half and aside is not None:
             first, aside = lax.optimization_barrier((first, aside))
+        if before is not None:
+            first, second = before(j, first, second)
         first = lax.ppermute(first if j < half else first[cut:], "seq", ring)
         second = lax.ppermute(
             second if j < half else second[:cut], "seq", across if j == 1 else ring
@@ -84,6 +77,25 @@
         pieces[j, 1] = lax.ppermute(pieces[-j, 0], "seq", swap)
         pieces[j, 0] = lax.ppermute(pieces[-j, 1], "seq", swap)
     return pieces, aside
+
+
+def gather_keys(piece, devices):
+    half = devices // 4
+    (ring, across), swap = ring_steps(devices // 2), swap_steps(devices)
+    pieces = {(0, 0): piece}
+    first = second = piece
+    for j in range(1, half + 1):
+        first = lax.ppermute(first, "seq", ring)
+        pieces[-j, 0] = first
+        if j < half:
+            second = lax.ppermute(second, "seq", across if j == 1 else ring)
+            pieces[-j, 1] = second
+    pieces[0, 1] = lax.ppermute(piece, "seq", swap)
+    for j in range(1, half + 1):
+        pieces[-j if j == half else j, 1] = lax.ppermute(pieces[-j, 0], "seq", swap)
+        if j < half:
+            pieces[j, 0] = lax.ppermute(pieces[-j, 1], "seq", swap)
+    return pieces
 
 
 def added(*terms):
@@ -112,7 +124,7 @@
     return added(mix, *second).astype(BF16)
 
 
-def pack_kernel(devices, key_ref, value_ref, id_ref, weight_ref, out_weight_ref, out_ref):
+def pack_kernel(devices, key_ref, value_ref, id_ref, weight_ref, out_ref):
     rows, width = key_ref.shape
     out_ref[:rows, :width] = key_ref[...]
     out_ref[:rows, width:] = value_ref[...]
@@ -130,10 +142,6 @@
     if extra > 2 * len(lines):
         low.append(jnp.zeros((extra - 2 * len(lines), 2 * width), F32))
     out_ref[rows : rows + extra, :] = jnp.concatenate(high + low, axis=0).astype(BF16)
-    depth = out_weight_ref.shape[0]
-    for n in range(out_weight_ref.shape[1] // (2 * width)):
-        start = rows + extra + n * depth
-        out_ref[start : start + depth, :] = out_weight_ref[:, 2 * width * n : 2 * width * (n + 1)]
 
 
 def line_rows(devices, rows, width):
@@ -141,30 +149,27 @@
     return -(-lines // 16) * 16
 
 
-def pack(keys, values, ids, weights, out_weight, devices):
+def pack(keys, values, ids, weights, devices):
     rows, width = keys.shape
     total = rows + line_rows(devices, rows, width)
-    total += out_weight.shape[0] * out_weight.shape[1] // (2 * width)
     return pl.pallas_call(
         functools.partial(pack_kernel, devices),
         out_shape=jax.ShapeDtypeStruct((total, 2 * width), BF16),
-        in_specs=[VMEM] * 5,
+        in_specs=[VMEM] * 4,
         out_specs=VMEM,
         compiler_params=PARAMS,
         cost_estimate=pl.CostEstimate(flops=10**6, bytes_accessed=2**20, transcendentals=0),
         name="pack",
-    )(keys, values, jnp.transpose(ids), jnp.transpose(weights), out_weight)
-
-
-def attend_kernel(devices, own_ref, doc_ref, q_ref, res_ref, gain_ref, *refs):
+    )(keys, values, jnp.transpose(ids), jnp.transpose(weights))
+
+
+def attend_kernel(devices, own_ref, doc_ref, q_ref, *refs):
     names = piece_names(devices)
-    head_refs, tail_refs = refs[: len(names)], refs[len(names) : 2 * len(names)]
-    out_ref, hidden_ref, normed_ref, both, weight, sems = refs[2 * len(names) :]
-    rows, model = res_ref.shape
+    head_refs = refs[: len(names)]
+    out_ref, scale_ref, both, lines, sems = refs[len(names) :]
+    rows = q_ref.shape[0]
     width = KEY_VALUE_HEADS * HEAD_SIZE
     window = both.shape[0]
-    parts = model // (2 * width)
-    depth = weight.shape[1] // parts
     own = own_ref[0]
     own_doc = doc_ref[own]
 
@@ -174,12 +179,9 @@
             head_refs[i].at[pl.ds(0, rows), :], both.at[pl.ds(start, rows), :], sems.at[i, 0]
         )
 
-    def weight_copy(i):
-        behind = tail_refs[i].shape[0] - parts * depth
+    def line_copy(i):
         return pltpu.make_async_copy(
-            tail_refs[i].at[pl.ds(behind, parts * depth), :],
-            weight.at[block_of(own, names[i], devices)],
-            sems.at[i, 1],
+            head_refs[i].at[pl.ds(rows, lines.shape[1]), :], lines.at[i], sems.at[i, 1]
         )
 
     kv_copy(0, 0).start()
@@ -197,7 +199,7 @@
 
         filled = filled + shown.astype(jnp.int32)
     for i in range(len(names)):
-        weight_copy(i).start()
+        line_copy(i).start()
 
     kv_copy(0, 0).wait()
     for s in range(1, window // rows):
@@ -257,22 +259,74 @@
                 h * rows : (h + 1) * rows
             ]
 
+    count = devices * rows // (2 * width)
+    in_row = 2 * width // rows
+    line = lax.broadcasted_iota(jnp.int32, (lines.shape[1], 2 * width), 0)
+    wanted = (line == own // in_row) | (line == count + own // in_row)
+    picked = []
     for i in range(len(names)):
-        weight_copy(i).wait()
-    total = []
-    for n in range(parts):
-        here = res_ref[:, 2 * width * n : 2 * width * (n + 1)].astype(F32)
-        for chip in range(devices // 2):
-            pair = jnp.concatenate(
-                [weight[2 * chip + k, n * depth : (n + 1) * depth, :] for k in range(2)], axis=0
+        line_copy(i).wait()
+        line = jnp.sum(jnp.where(wanted, lines[i].astype(F32), 0.0), axis=0, keepdims=True)
+        picked.append(
+            sum(
+                jnp.where(own % in_row == n, line[:, n * rows : (n + 1) * rows], 0.0)
+                for n in range(in_row)
             )
-            here += jnp.dot(
-                out_ref[:, 2 * depth * chip : 2 * depth * (chip + 1)],
-                pair,
-                preferred_element_type=F32,
-            )
-        total.append(here)
-    hidden = jnp.concatenate(total, axis=1)
+        )
+    picked.append(jnp.zeros((rows - len(names), rows), F32))
+    scale_ref[...] = jnp.transpose(jnp.concatenate(picked, axis=0))
+
+
+def attend(own, docs, queries, heads, devices):
+    rows = queries.shape[0]
+    window = (min(MOST_BLK, devices) + 1) * rows
+    names = piece_names(devices)
+    width = KEY_VALUE_HEADS * HEAD_SIZE
+    return pl.pallas_call(
+        functools.partial(attend_kernel, devices),
+        out_shape=(
+            jax.ShapeDtypeStruct(queries.shape, BF16),
+            jax.ShapeDtypeStruct((rows, rows), F32),
+        ),
+        in_specs=[SMEM, SMEM, VMEM] + [HBM] * len(names),
+        out_specs=(VMEM, VMEM),
+        scratch_shapes=[
+            pltpu.VMEM((window, 2 * width), BF16),
+            pltpu.VMEM((len(names), line_rows(devices, rows, width), 2 * width), BF16),
+            pltpu.SemaphoreType.DMA((len(names), 2)),
+        ],
+        compiler_params=PARAMS,
+        cost_estimate=pl.CostEstimate(
+            flops=4 * QUERY_HEADS * rows * window * HEAD_SIZE,
+            bytes_accessed=8 * 2**20,
+            transcendentals=QUERY_HEADS * rows * window,
+        ),
+        name="attend",
+    )(own, docs, queries, *[heads[name] for name in names])
+
+
+def project_kernel(devices, own_ref, att_ref, res_ref, gain_ref, *refs):
+    names = piece_names(devices)
+    w_refs, (hidden_ref, normed_ref, weight, sems) = refs[:-4], refs[-4:]
+    own = own_ref[0]
+    depth = weight.shape[0] // devices
+    copies = []
+    for i, ref in enumerate(w_refs):
+        if i < len(names) - 2:
+            name, start = names[i], 0
+        else:
+            far = i - (len(names) - 2)
+            name, start = names[len(names) - 2 + far // 2], far % 2 * (depth - ref.shape[0])
+        at = pl.multiple_of(block_of(own, name, devices) * depth + start, 16)
+        copies.append(
+            pltpu.make_async_copy(ref, weight.at[pl.ds(at, ref.shape[0]), :], sems.at[i])
+        )
+        copies[-1].start()
+    for c in copies:
+        c.wait()
+    hidden = res_ref[...].astype(F32) + jnp.dot(
+        att_ref[...], weight[...], preferred_element_type=F32
+    )
     hidden_ref[...] = hidden.astype(BF16)
     mean_square = jnp.mean(hidden * hidden, axis=-1, keepdims=True)
     normed_ref[...] = (
@@ -280,84 +334,29 @@
     ).astype(BF16)
 
 
-def attend(own, docs, queries, residual, gain, packed, depth, devices):
-    rows, model = residual.shape
-    window = (min(MOST_BLK, devices) + 1) * rows
+def project(own, attention, residual, gain, pieces, depth, devices):
     names = piece_names(devices)
-    width = KEY_VALUE_HEADS * HEAD_SIZE
-    parts = model // (2 * width)
+    half = devices // 4
+    refs = [pieces[name] for name in names[:-2]]
+    refs += [pieces[name] for name in ((half, 0), (-half, 0), (-half, 1), (half, 1))]
     shape = jax.ShapeDtypeStruct(residual.shape, BF16)
     return pl.pallas_call(
-        functools.partial(attend_kernel, devices),
-        out_shape=(jax.ShapeDtypeStruct(queries.shape, BF16), shape, shape),
-        in_specs=[SMEM, SMEM, VMEM, VMEM, VMEM] + [HBM] * (2 * len(names)),
-        out_specs=(VMEM,) * 3,
+        functools.partial(project_kernel, devices),
+        out_shape=(shape, shape),
+        in_specs=[SMEM, VMEM, VMEM, VMEM] + [HBM] * len(refs),
+        out_specs=(VMEM, VMEM),
         scratch_shapes=[
-            pltpu.VMEM((window, 2 * width), BF16),
-            pltpu.VMEM((devices, parts * depth, 2 * width), BF16),
-            pltpu.SemaphoreType.DMA((len(names), 2)),
+            pltpu.VMEM((depth * devices, residual.shape[1]), BF16),
+            pltpu.SemaphoreType.DMA((len(refs),)),
         ],
-        compiler_params=PARAMS,
+        compiler_params=pltpu.CompilerParams(vmem_limit_bytes=24 * 2**20),
         cost_estimate=pl.CostEstimate(
-            flops=4 * QUERY_HEADS * rows * window * HEAD_SIZE + 2 * rows * depth * devices * model,
-            bytes_accessed=8 * 2**20,
-            transcendentals=QUERY_HEADS * rows * window,
+            flops=2 * residual.shape[0] * depth * devices * residual.shape[1],
+            bytes_accessed=6 * 2**20,
+            transcendentals=0,
         ),
-        name="attend",
-    )(
-        own,
-        docs,
-        queries,
-        residual,
-        gain.reshape(1, -1),
-        *[packed[source_of(name, False, devices)] for name in names],
-        *[packed[source_of(name, True, devices)] for name in names],
-    )
-
-
-def scales_kernel(devices, rows, width, own_ref, *refs):
-    head_refs, (scale_ref, lines, sems) = refs[:-3], refs[-3:]
-    own = own_ref[0]
-    copies = [
-        pltpu.make_async_copy(ref.at[pl.ds(rows, lines.shape[1]), :], lines.at[i], sems.at[i])
-        for i, ref in enumerate(head_refs)
-    ]
-    for c in copies:
-        c.start()
-    count = devices * rows // (2 * width)
-    in_row = 2 * width // rows
-    line = lax.broadcasted_iota(jnp.int32, (lines.shape[1], 2 * width), 0)
-    wanted = (line == own // in_row) | (line == count + own // in_row)
-    picked = []
-    for i, c in enumerate(copies):
-        c.wait()
-        both = jnp.sum(jnp.where(wanted, lines[i].astype(F32), 0.0), axis=0, keepdims=True)
-        picked.append(
-            sum(
-                jnp.where(own % in_row == n, both[:, n * rows : (n + 1) * rows], 0.0)
-                for n in range(in_row)
-            )
-        )
-    picked.append(jnp.zeros((rows - len(copies), rows), F32))
-    scale_ref[...] = jnp.transpose(jnp.concatenate(picked, axis=0))
-
-
-def expert_scales(own, packed, rows, devices):
-    names = piece_names(devices)
-    width = KEY_VALUE_HEADS * HEAD_SIZE
-    return pl.pallas_call(
-        functools.partial(scales_kernel, devices, rows, width),
-        out_shape=jax.ShapeDtypeStruct((rows, rows), F32),
-        in_specs=[SMEM] + [HBM] * len(names),
-        out_specs=VMEM,
-        scratch_shapes=[
-            pltpu.VMEM((len(names), line_rows(devices, rows, width), 2 * width), BF16),
-            pltpu.SemaphoreType.DMA((len(names),)),
-        ],
-        compiler_params=PARAMS,
-        cost_estimate=pl.CostEstimate(flops=10**6, bytes_accessed=2**19, transcendentals=0),
-        name="expert_scales",
-    )(own, *[packed[source_of(name, False, devices)] for name in names])
+        name="project",
+    )(own, attention, residual, gain.reshape(1, -1), *refs)
 
 
 def expert_kernel(parts, scale_ref, gate_ref, up_ref, down_ref, *refs):
@@ -409,19 +408,30 @@
 ):
     devices = lax.axis_size("seq")
     own = lax.axis_index("seq").astype(jnp.int32).reshape(1)
-    packed = pack(
-        token_key_heads, token_value_heads, expert_ids, gate_weights, out_weight, devices
-    )
     rows = queries.shape[0]
-    cut = rows + line_rows(devices, rows, token_key_heads.shape[1])
-    inputs, _ = ring_gather(packed, cut, devices)
-    attention, hidden, normed = attend(
-        own, doc_of_block, queries, residual, norm_gain, inputs, out_weight.shape[0], devices
-    )
-    scales = expert_scales(own, inputs, rows, devices)
+    packed = pack(token_key_heads, token_value_heads, expert_ids, gate_weights, devices)
+    keys = gather_keys(packed, devices)
+    half, depth = devices // 4, out_weight.shape[0]
+    made = {}
+
+    def before(j, first, second):
+        if j == 1:
+            pass
+        if j == half - 1:
+            first, keys[-half, 0] = lax.optimization_barrier((first, keys[-half, 0]))
+        if j == half:
+            made["attention"], made["scales"] = attend(own, doc_of_block, queries, keys, devices)
+            first, second, made["attention"] = lax.optimization_barrier(
+                (first, second, made["attention"])
+            )
+        return first, second
+
+    weights, _ = ring_gather(out_weight, depth // 2, devices, before=before)
+    attention, scales = made["attention"], made["scales"]
+    hidden, normed = project(own, attention, residual, norm_gain, weights, depth, devices)
 
     half, cut = devices // 4, rows // 2
-    tokens, scales = ring_gather(normed, cut, devices, scales)
+    tokens, _ = ring_gather(normed, cut, devices)
     names = piece_names(devices)
     kept, sent = {}, {}
     for j, group in enumerate(piece_groups(devices // 2)):

time: 117 us -> 114 us (0.974)
  waiting for transfers between devices: 58.7 us -> 41.5 us
  starting transfers between devices: 34.2 us -> 50.6 us
  local copies, waits for them, and re-layouts: 1.75 us -> 0.24 us
  Pallas kernels: 19.7 us -> 18.5 us
    ppermute x8, waiting for transfers between devices: 21.8 us -> 7.7 us  [ring_gather(): lax.ppermute(second if j < half else second[:cut], 'seq', across if j ==...]
    ppermute x8, waiting for transfers between devices: 26 us -> 14 us  [ring_gather(): first = lax.ppermute(first if j < half else first[cut:], 'seq', ring)]
    ppermute x0 -> x15, starting transfers between devices: none -> 10.8 us  [the longest x4 4.93 us: gather_keys(): first = lax.ppermute(first, 'seq', ring)]
    ppermute x0 -> x15, waiting for transfers between devices: none -> 7.09 us  [the longest x4 3.71 us: gather_keys(): first = lax.ppermute(first, 'seq', ring)]
    ppermute x8, starting transfers between devices: 7.45 us -> 12.3 us  [ring_gather(): lax.ppermute(second if j < half else second[:cut], 'seq', across if j ==...]
    ppermute x8, starting transfers between devices: 9.66 us -> 12.3 us  [ring_gather(): first = lax.ppermute(first if j < half else first[cut:], 'seq', ring)]
    pallas_call x1, Pallas kernels: 8.32 us -> 6.58 us  [attend(): pl.pallas_call(functools.partial(attend_kernel, devices), out_shape=(jax....]
  transfers between devices with their start and end apart: 47 -> 62, of which waited for: 24 -> 25; matrix products, arithmetic and copies ran while one was open for 1% -> 1% of each run, Pallas kernels for 8% -> 14%
where the time goes in v5:
time: 114 us
  starting transfers between devices  50.6 us (44%)
  waiting for transfers between devices  41.5 us (36%)
  Pallas kernels  18.5 us (16%)
  other arithmetic  1.63 us (1%)
  between operations  1.16 us (1%)
    ppermute x8, waiting for transfers between devices, ring_gather(): first = lax.ppermute(first if j < half else first[cut:], 'seq', ring)  14 us
    ppermute x8, starting transfers between devices, ring_gather(): first = lax.ppermute(first if j < half else first[cut:], 'seq', ring)  12.3 us
    ppermute x8, starting transfers between devices, ring_gather(): lax.ppermute(second if j < half else second[:cut], 'seq', across if j ==...  12.3 us
    ppermute x8, waiting for transfers between devices, ring_gather(): lax.ppermute(second if j < half else second[:cut], 'seq', across if j ==...  7.7 us
    pallas_call x5, Pallas kernels, expert(): pl.pallas_call(functools.partial(expert_kernel, parts), out_shape=(shape,...  7.5 us
    ppermute x4, starting transfers between devices, ring_scatter_sum(): first = [lax.ppermute(total, 'seq', ring)]  6.79 us
    pallas_call x1, Pallas kernels, attend(): pl.pallas_call(functools.partial(attend_kernel, devices), out_shape=(jax....  6.58 us
    ppermute x4, waiting for transfers between devices, ring_scatter_sum(): first = [lax.ppermute(total, 'seq', ring)]  6.29 us
  transfers between devices with their start and end apart: 62, of which 25 were waited for; matrix products, arithmetic and copies ran while one was open for 1% of the time, Pallas kernels for 14%

profile of v5, /device:TPU:0, one launch (start us, length us, event | category | flops | bytes accessed | tf_op | source)
XLA Modules:
  0.0 113.7 jit_solution(10824988856003426765)
XLA Ops:
  0.6 2.5 %collective-permute-start.7 = (bf16[128,1024]{1,0:T(8,128)(2,1)}, bf16[128,1024]{1,0:T(8,128)(2,1)S(1)}, u32[]{:S(2)}, u32[]{:S(2)}) collective-permute-start(bf16[128,1024]{1,0:T(8,128)(2,1)} %refs_0_.1), channel_id=1, source_target_pairs={{1,4},{0,3},{5,8},{4,1},{9,12},{8,5},{13,14},{12,9},{15,10},{14,13... | collective-permute-start | bytes 786440 | tf_op jit(solution)/shard_map/ppermute | solution.py:71
  3.1 1.6 %pack.1.refs_0_ = bf16[144,512]{1,0:T(8,128)(2,1)} custom-call(bf16[128,256]{1,0:T(8,128)(2,1)} %key_ref.1, bf16[128,256]{1,0:T(8,128)(2,1)} %value_ref.1, s32[8,128]{1,0:T(8,128)} %bitcast.21, f32[8,128]{1,0:T(8,128)} %bitcast.22), custom_call_target="tpu_custom_call" | custom-call | flops 1000000 | bytes 1048576 | tf_op jit(solution)/shard_map/pack/pallas_call | solution.py:155
  5.3 1.6 %collective-permute-start = (bf16[128,1024]{1,0:T(8,128)(2,1)S(1)}, bf16[128,1024]{1,0:T(8,128)(2,1)S(1)}, u32[]{:S(2)}, u32[]{:S(2)}) collective-permute-start(bf16[128,1024]{1,0:T(8,128)(2,1)S(1)} %copy-done.5), channel_id=1, source_target_pairs={{0,4},{1,3},{4,8},{5,1},{8,12},{9,5},{12,14},{13,9},{14,10},{15,13... | collective-permute-start | bytes 786440 | tf_op jit(solution)/shard_map/ppermute | solution.py:70
  11.3 2.0 %collective-permute-done.11.refs_3_ = bf16[144,512]{1,0:T(8,128)(2,1)S(1)} collective-permute-done((bf16[144,512]{1,0:T(8,128)(2,1)}, bf16[144,512]{1,0:T(8,128)(2,1)S(1)}, u32[]{:S(2)}, u32[]{:S(2)}) %collective-permute-start.11) | collective-permute-done | bytes 147488 | tf_op jit(solution)/shard_map/ppermute | solution.py:91
  13.3 1.6 %collective-permute-start.14 = (bf16[144,512]{1,0:T(8,128)(2,1)S(1)}, bf16[144,512]{1,0:T(8,128)(2,1)S(1)}, u32[]{:S(2)}, u32[]{:S(2)}) collective-permute-start(bf16[144,512]{1,0:T(8,128)(2,1)S(1)} %collective-permute-done.11.refs_3_), channel_id=1, source_target_pairs={{0,4},{1,3},{4,8},{5,1},{8,12},{9,5},{12,14},{13,9},{14,10},{15,13... | collective-permute-start | bytes 442376 | tf_op jit(solution)/shard_map/ppermute | solution.py:91
  18.5 1.6 %collective-permute-start.1 = (bf16[128,1024]{1,0:T(8,128)(2,1)S(1)}, bf16[128,1024]{1,0:T(8,128)(2,1)S(1)}, u32[]{:S(2)}, u32[]{:S(2)}) collective-permute-start(bf16[128,1024]{1,0:T(8,128)(2,1)S(1)} %collective-permute-done.refs_2_), channel_id=1, source_target_pairs={{0,4},{1,3},{4,8},{5,1},{8,12},{9,5},{12,14},{13,9},{14,10},{15,13... | collective-permute-start | bytes 786440 | tf_op jit(solution)/shard_map/ppermute | solution.py:70
  22.9 1.6 %collective-permute-start.5 = (bf16[144,512]{1,0:T(8,128)(2,1)S(1)}, bf16[144,512]{1,0:T(8,128)(2,1)S(1)}, u32[]{:S(2)}, u32[]{:S(2)}) collective-permute-start(bf16[144,512]{1,0:T(8,128)(2,1)S(1)} %collective-permute-done.4.refs_10_), channel_id=1, source_target_pairs={{0,4},{1,3},{4,8},{5,1},{8,12},{9,5},{12,14},{13,9},{14,10},{15,13... | collective-permute-start | bytes 442376 | tf_op jit(solution)/shard_map/ppermute | solution.py:88
  28.9 1.6 %collective-permute-start.6 = (bf16[128,1024]{1,0:T(8,128)(2,1)S(1)}, bf16[128,1024]{1,0:T(8,128)(2,1)S(1)}, u32[]{:S(2)}, u32[]{:S(2)}) collective-permute-start(bf16[128,1024]{1,0:T(8,128)(2,1)S(1)} %collective-permute-done.1.refs_6_), channel_id=1, source_target_pairs={{0,4},{1,3},{4,8},{5,1},{8,12},{9,5},{12,14},{13,9},{14,10},{15,13... | collective-permute-start | bytes 786440 | tf_op jit(solution)/shard_map/ppermute | solution.py:70
  31.9 6.6 %attend.1 = (bf16[128,2048]{1,0:T(8,128)(2,1)}, f32[128,128]{1,0:T(8,128)}) custom-call(s32[1]{0:T(128)} %bitcast.2.own_ref, s32[16]{0:T(128)} %doc_ref.1, bf16[128,2048]{1,0:T(8,128)(2,1)} %q_ref.1, bf16[144,512]{1,0:T(8,128)(2,1)} %pack.1.refs_0_, bf16[144,512]{1,0:T(8,128)(2,1)} %copy-done.10, bf16[144,512]{1,0:T(8,128)(2,1)} %copy-done.8, ...), custom_call_target="tpu_custom_call" | custom-call | flops 1207959552 | bytes 8388608 | tf_op jit(solution)/shard_map/attend/pallas_call | solution.py:285
  39.2 1.7 %collective-permute-start.28 = (bf16[64,1024]{1,0:T(8,128)(2,1)S(1)}, bf16[64,1024]{1,0:T(8,128)(2,1)S(1)}, u32[]{:S(2)}, u32[]{:S(2)}) collective-permute-start(bf16[64,1024]{1,0:T(8,128)(2,1)S(1)} %slice.60), channel_id=1, source_target_pairs={{0,4},{1,3},{4,8},{5,1},{8,12},{9,5},{12,14},{13,9},{14,10},{15,13... | collective-permute-start | bytes 393224 | tf_op jit(solution)/shard_map/ppermute | solution.py:71
  42.4 1.8 %collective-permute-done.28.refs_16_ = bf16[64,1024]{1,0:T(8,128)(2,1)S(1)} collective-permute-done((bf16[64,1024]{1,0:T(8,128)(2,1)S(1)}, bf16[64,1024]{1,0:T(8,128)(2,1)S(1)}, u32[]{:S(2)}, u32[]{:S(2)}) %collective-permute-start.28) | collective-permute-done | bytes 131104 | tf_op jit(solution)/shard_map/ppermute | solution.py:71
  44.2 1.7 %collective-permute-done.30.refs_15_ = bf16[64,1024]{1,0:T(8,128)(2,1)S(1)} collective-permute-done((bf16[64,1024]{1,0:T(8,128)(2,1)S(1)}, bf16[64,1024]{1,0:T(8,128)(2,1)S(1)}, u32[]{:S(2)}, u32[]{:S(2)}) %collective-permute-start.30) | collective-permute-done | bytes 131104 | tf_op jit(solution)/shard_map/ppermute | solution.py:70
  47.2 2.8 %project.1 = (bf16[128,1024]{1,0:T(8,128)(2,1)}, bf16[128,1024]{1,0:T(8,128)(2,1)S(1)}) custom-call(s32[1]{0:T(128)} %bitcast.2.own_ref, bf16[128,2048]{1,0:T(8,128)(2,1)S(1)} %copy-done.3, bf16[128,1024]{1,0:T(8,128)(2,1)S(1)} %copy-done.4, bf16[1,1024]{1,0:T(2,128)(2,1)S(1)} %reshape.13.gain_ref, bf16[128,1024]{1,0:T(8,128)(2,1)S(1)} %copy-done.5, ...), custom_call_target="tpu_custom_call" | custom-call | flops 536870912 | bytes 6291456 | tf_op jit(solution)/shard_map/project/pallas_call | solution.py:343
  50.0 1.6 %collective-permute-start.34 = (bf16[128,1024]{1,0:T(8,128)(2,1)S(1)}, bf16[128,1024]{1,0:T(8,128)(2,1)S(1)}, u32[]{:S(2)}, u32[]{:S(2)}) collective-permute-start(bf16[128,1024]{1,0:T(8,128)(2,1)S(1)} %get-tuple-element.37.refs_0_), channel_id=1, source_target_pairs={{0,4},{1,3},{4,8},{5,1},{8,12},{9,5},{12,14},{13,9},{14,10},{15,13... | collective-permute-start | bytes 786440 | tf_op jit(solution)/shard_map/ppermute | solution.py:70
  51.8 6.5 %collective-permute-done.34.refs_0_ = bf16[128,1024]{1,0:T(8,128)(2,1)S(1)} collective-permute-done((bf16[128,1024]{1,0:T(8,128)(2,1)S(1)}, bf16[128,1024]{1,0:T(8,128)(2,1)S(1)}, u32[]{:S(2)}, u32[]{:S(2)}) %collective-permute-start.34) | collective-permute-done | bytes 262176 | tf_op jit(solution)/shard_map/ppermute | solution.py:70
  59.8 1.7 %collective-permute-start.40 = (bf16[128,1024]{1,0:T(8,128)(2,1)S(1)}, bf16[128,1024]{1,0:T(8,128)(2,1)S(1)}, u32[]{:S(2)}, u32[]{:S(2)}) collective-permute-start(bf16[128,1024]{1,0:T(8,128)(2,1)S(1)} %collective-permute-done.35.refs_1_), channel_id=1, source_target_pairs={{0,4},{1,3},{4,8},{5,1},{8,12},{9,5},{12,14},{13,9},{14,10},{15,13... | collective-permute-start | bytes 786440 | tf_op jit(solution)/shard_map/ppermute | solution.py:71
  61.5 3.2 %collective-permute-done.39.refs_0_ = bf16[128,1024]{1,0:T(8,128)(2,1)S(1)} collective-permute-done((bf16[128,1024]{1,0:T(8,128)(2,1)S(1)}, bf16[128,1024]{1,0:T(8,128)(2,1)S(1)}, u32[]{:S(2)}, u32[]{:S(2)}) %collective-permute-start.39) | collective-permute-done | bytes 262176 | tf_op jit(solution)/shard_map/ppermute | solution.py:70
  69.0 2.1 %collective-permute-done.44.refs_0_ = bf16[128,1024]{1,0:T(8,128)(2,1)S(1)} collective-permute-done((bf16[128,1024]{1,0:T(8,128)(2,1)S(1)}, bf16[128,1024]{1,0:T(8,128)(2,1)S(1)}, u32[]{:S(2)}, u32[]{:S(2)}) %collective-permute-start.44) | collective-permute-done | bytes 262176 | tf_op jit(solution)/shard_map/ppermute | solution.py:70
  71.1 1.5 %collective-permute-start.49 = (bf16[64,1024]{1,0:T(8,128)(2,1)S(1)}, bf16[64,1024]{1,0:T(8,128)(2,1)S(1)}, u32[]{:S(2)}, u32[]{:S(2)}) collective-permute-start(bf16[64,1024]{1,0:T(8,128)(2,1)S(1)} %slice.83), channel_id=1, source_target_pairs={{0,4},{1,3},{4,8},{5,1},{8,12},{9,5},{12,14},{13,9},{14,10},{15,13... | collective-permute-start | bytes 393224 | tf_op jit(solution)/shard_map/ppermute | solution.py:70
  73.9 1.7 %collective-permute-start.50 = (bf16[64,1024]{1,0:T(8,128)(2,1)S(1)}, bf16[64,1024]{1,0:T(8,128)(2,1)S(1)}, u32[]{:S(2)}, u32[]{:S(2)}) collective-permute-start(bf16[64,1024]{1,0:T(8,128)(2,1)S(1)} %slice.84), channel_id=1, source_target_pairs={{0,4},{1,3},{4,8},{5,1},{8,12},{9,5},{12,14},{13,9},{14,10},{15,13... | collective-permute-start | bytes 393224 | tf_op jit(solution)/shard_map/ppermute | solution.py:71
  76.1 3.0 %collective-permute-done.50.refs_1_ = bf16[64,1024]{1,0:T(8,128)(2,1)S(1)} collective-permute-done((bf16[64,1024]{1,0:T(8,128)(2,1)S(1)}, bf16[64,1024]{1,0:T(8,128)(2,1)S(1)}, u32[]{:S(2)}, u32[]{:S(2)}) %collective-permute-start.50) | collective-permute-done | bytes 131104 | tf_op jit(solution)/shard_map/ppermute | solution.py:71
  82.3 1.8 %expert.8 = (bf16[256,1024]{1,0:T(8,128)(2,1)S(1)}, bf16[256,1024]{1,0:T(8,128)(2,1)S(1)}) custom-call(f32[128,128]{1,0:T(8,128)S(1)} %copy-done.6, bf16[1024,384]{1,0:T(8,128)(2,1)S(1)} %bitcast.7, bf16[1024,384]{1,0:T(8,128)(2,1)S(1)} %bitcast.12, bf16[384,1024]{1,0:T(8,128)(2,1)S(1)} %bitcast.17, bf16[128,1024]{1,0:T(8,128)(2,1)S(1)} %collective-permute-done.44.refs_0_, ...), custom_call_target="tpu_custom_call" | custom-call | flops 1207959552 | bytes 4194304 | tf_op jit(solution)/shard_map/expert/pallas_call | solution.py:380
  85.6 2.0 %collective-permute-start.54 = (bf16[64,1024]{1,0:T(8,128)(2,1)S(1)}, bf16[64,1024]{1,0:T(8,128)(2,1)S(1)}, u32[]{:S(2)}, u32[]{:S(2)}) collective-permute-start(bf16[64,1024]{1,0:T(8,128)(2,1)S(1)} %add_convert_fusion.8), channel_id=1, source_target_pairs={{4,0},{3,1},{8,4},{1,5},{12,8},{5,9},{14,12},{9,13},{10,14},{13,15... | collective-permute-start | bytes 393224 | tf_op jit(solution)/shard_map/ppermute | solution.py:121
  88.1 1.8 %expert.7 = (bf16[256,1024]{1,0:T(8,128)(2,1)S(1)}, bf16[256,1024]{1,0:T(8,128)(2,1)S(1)}) custom-call(f32[128,128]{1,0:T(8,128)S(1)} %copy-done.6, bf16[1024,384]{1,0:T(8,128)(2,1)S(1)} %bitcast.8, bf16[1024,384]{1,0:T(8,128)(2,1)S(1)} %bitcast.13, bf16[384,1024]{1,0:T(8,128)(2,1)S(1)} %bitcast.18, bf16[128,1024]{1,0:T(8,128)(2,1)S(1)} %collective-permute-done.39.refs_0_, ...), custom_call_target="tpu_custom_call" | custom-call | flops 1207959552 | bytes 4194304 | tf_op jit(solution)/shard_map/expert/pallas_call | solution.py:380
  91.1 1.6 %collective-permute-start.55 = (bf16[128,1024]{1,0:T(8,128)(2,1)S(1)}, bf16[128,1024]{1,0:T(8,128)(2,1)S(1)}, u32[]{:S(2)}, u32[]{:S(2)}) collective-permute-start(bf16[128,1024]{1,0:T(8,128)(2,1)S(1)} %add_convert_fusion.6), channel_id=1, source_target_pairs={{4,0},{3,1},{8,4},{1,5},{12,8},{5,9},{14,12},{9,13},{10,14},{13,15... | collective-permute-start | bytes 786440 | tf_op jit(solution)/shard_map/ppermute | solution.py:121
  92.9 1.8 %collective-permute-start.59 = (bf16[128,1024]{1,0:T(8,128)(2,1)S(1)}, bf16[128,1024]{1,0:T(8,128)(2,1)S(1)}, u32[]{:S(2)}, u32[]{:S(2)}) collective-permute-start(bf16[128,1024]{1,0:T(8,128)(2,1)S(1)} %add_convert_fusion.3), channel_id=1, source_target_pairs={{4,0},{3,1},{8,4},{1,5},{12,8},{5,9},{14,12},{9,13},{10,14},{13,15... | collective-permute-start | bytes 786440 | tf_op jit(solution)/shard_map/ppermute | solution.py:122
  94.7 1.8 %expert.6 = (bf16[256,1024]{1,0:T(8,128)(2,1)S(1)}, bf16[256,1024]{1,0:T(8,128)(2,1)S(1)}) custom-call(f32[128,128]{1,0:T(8,128)S(1)} %copy-done.6, bf16[1024,384]{1,0:T(8,128)(2,1)S(1)} %bitcast.9, bf16[1024,384]{1,0:T(8,128)(2,1)S(1)} %bitcast.14, bf16[384,1024]{1,0:T(8,128)(2,1)S(1)} %bitcast.19, bf16[128,1024]{1,0:T(8,128)(2,1)S(1)} %collective-permute-done.34.refs_0_, ...), custom_call_target="tpu_custom_call" | custom-call | flops 1207959552 | bytes 4194304 | tf_op jit(solution)/shard_map/expert/pallas_call | solution.py:380
  97.7 1.6 %collective-permute-start.56 = (bf16[128,1024]{1,0:T(8,128)(2,1)S(1)}, bf16[128,1024]{1,0:T(8,128)(2,1)S(1)}, u32[]{:S(2)}, u32[]{:S(2)}) collective-permute-start(bf16[128,1024]{1,0:T(8,128)(2,1)S(1)} %add_convert_fusion.5), channel_id=1, source_target_pairs={{4,0},{3,1},{8,4},{1,5},{12,8},{5,9},{14,12},{9,13},{10,14},{13,15... | collective-permute-start | bytes 786440 | tf_op jit(solution)/shard_map/ppermute | solution.py:121
  100.5 1.6 %collective-permute-start.60 = (bf16[128,1024]{1,0:T(8,128)(2,1)S(1)}, bf16[128,1024]{1,0:T(8,128)(2,1)S(1)}, u32[]{:S(2)}, u32[]{:S(2)}) collective-permute-start(bf16[128,1024]{1,0:T(8,128)(2,1)S(1)} %add_convert_fusion.2), channel_id=1, source_target_pairs={{4,0},{3,1},{8,4},{1,5},{12,8},{5,9},{14,12},{9,13},{10,14},{13,15... | collective-permute-start | bytes 786440 | tf_op jit(solution)/shard_map/ppermute | solution.py:122
  104.2 1.6 %collective-permute-start.57 = (bf16[128,1024]{1,0:T(8,128)(2,1)S(1)}, bf16[128,1024]{1,0:T(8,128)(2,1)S(1)}, u32[]{:S(2)}, u32[]{:S(2)}) collective-permute-start(bf16[128,1024]{1,0:T(8,128)(2,1)S(1)} %add_convert_fusion.4), channel_id=1, source_target_pairs={{4,0},{3,1},{8,4},{1,5},{12,8},{5,9},{14,12},{9,13},{10,14},{13,15... | collective-permute-start | bytes 786440 | tf_op jit(solution)/shard_map/ppermute | solution.py:121
  107.1 3.5 %collective-permute-done.57 = bf16[128,1024]{1,0:T(8,128)(2,1)S(1)} collective-permute-done((bf16[128,1024]{1,0:T(8,128)(2,1)S(1)}, bf16[128,1024]{1,0:T(8,128)(2,1)S(1)}, u32[]{:S(2)}, u32[]{:S(2)}) %collective-permute-start.57) | collective-permute-done | bytes 262176 | tf_op jit(solution)/shard_map/ppermute | solution.py:121
  110.8 2.1 %collective-permute-done.61 = bf16[128,1024]{1,0:T(8,128)(2,1)S(1)} collective-permute-done((bf16[128,1024]{1,0:T(8,128)(2,1)S(1)}, bf16[128,1024]{1,0:T(8,128)(2,1)S(1)}, u32[]{:S(2)}, u32[]{:S(2)}) %collective-permute-start.61) | collective-permute-done | bytes 262176 | tf_op jit(solution)/shard_map/ppermute | solution.py:122
  (166 shorter events, 41.6 us)
Async XLA Ops:
  0.6 14.3 %collective-permute-start.7 = (bf16[128,1024]{1,0:T(8,128)(2,1)}, bf16[128,1024]{1,0:T(8,128)(2,1)S(1)}, u32[]{:S(2)}, u32[]{:S(2)}) collective-permute-start(bf16[128,1024]{1,0:T(8,128)(2,1)} %refs_0_.1), channel_id=1, source_target_pairs={{1,4},{0,3},{5,8},{4,1},{9,12},{8,5},{13,14},{12,9},{15,10},{14,13... | collective-permute-start | bytes 786440 | tf_op jit(solution)/shard_map/ppermute | solution.py:71
  5.3 11.1 %collective-permute-start = (bf16[128,1024]{1,0:T(8,128)(2,1)S(1)}, bf16[128,1024]{1,0:T(8,128)(2,1)S(1)}, u32[]{:S(2)}, u32[]{:S(2)}) collective-permute-start(bf16[128,1024]{1,0:T(8,128)(2,1)S(1)} %copy-done.5), channel_id=1, source_target_pairs={{0,4},{1,3},{4,8},{5,1},{8,12},{9,5},{12,14},{13,9},{14,10},{15,13... | collective-permute-start | bytes 786440 | tf_op jit(solution)/shard_map/ppermute | solution.py:70
  6.9 6.4 %collective-permute-start.11 = (bf16[144,512]{1,0:T(8,128)(2,1)}, bf16[144,512]{1,0:T(8,128)(2,1)S(1)}, u32[]{:S(2)}, u32[]{:S(2)}) collective-permute-start(bf16[144,512]{1,0:T(8,128)(2,1)} %pack.1.refs_0_), channel_id=1, source_target_pairs={{1,4},{0,3},{5,8},{4,1},{9,12},{8,5},{13,14},{12,9},{15,10},{14,13... | collective-permute-start | bytes 442376 | tf_op jit(solution)/shard_map/ppermute | solution.py:91
  8.0 8.4 %collective-permute-start.10 = (bf16[144,512]{1,0:T(8,128)(2,1)}, bf16[144,512]{1,0:T(8,128)(2,1)S(1)}, u32[]{:S(2)}, u32[]{:S(2)}) collective-permute-start(bf16[144,512]{1,0:T(8,128)(2,1)} %pack.1.refs_0_), channel_id=1, source_target_pairs={{0,1},{1,0},{2,3},{3,2},{4,5},{5,4},{6,7},{7,6},{8,9},{9,8},{10,11... | collective-permute-start | bytes 442376 | tf_op jit(solution)/shard_map/ppermute | solution.py:93
  10.0 6.9 %collective-permute-start.3 = (bf16[144,512]{1,0:T(8,128)(2,1)S(1)}, bf16[144,512]{1,0:T(8,128)(2,1)S(1)}, u32[]{:S(2)}, u32[]{:S(2)}) collective-permute-start(bf16[144,512]{1,0:T(8,128)(2,1)S(1)} %collective-permute-done.2.refs_2_), channel_id=1, source_target_pairs={{0,4},{1,3},{4,8},{5,1},{8,12},{9,5},{12,14},{13,9},{14,10},{15,13... | collective-permute-start | bytes 442376 | tf_op jit(solution)/shard_map/ppermute | solution.py:88
  14.9 9.5 %collective-permute-start.8 = (bf16[128,1024]{1,0:T(8,128)(2,1)S(1)}, bf16[128,1024]{1,0:T(8,128)(2,1)S(1)}, u32[]{:S(2)}, u32[]{:S(2)}) collective-permute-start(bf16[128,1024]{1,0:T(8,128)(2,1)S(1)} %collective-permute-done.7.refs_3_), channel_id=1, source_target_pairs={{0,4},{1,3},{4,8},{5,1},{8,12},{9,5},{12,14},{13,9},{14,10},{15,13... | collective-permute-start | bytes 786440 | tf_op jit(solution)/shard_map/ppermute | solution.py:71
  17.0 5.9 %collective-permute-start.4 = (bf16[144,512]{1,0:T(8,128)(2,1)S(1)}, bf16[144,512]{1,0:T(8,128)(2,1)S(1)}, u32[]{:S(2)}, u32[]{:S(2)}) collective-permute-start(bf16[144,512]{1,0:T(8,128)(2,1)S(1)} %collective-permute-done.3.refs_6_), channel_id=1, source_target_pairs={{0,4},{1,3},{4,8},{5,1},{8,12},{9,5},{12,14},{13,9},{14,10},{15,13... | collective-permute-start | bytes 442376 | tf_op jit(solution)/shard_map/ppermute | solution.py:88
  18.5 9.3 %collective-permute-start.1 = (bf16[128,1024]{1,0:T(8,128)(2,1)S(1)}, bf16[128,1024]{1,0:T(8,128)(2,1)S(1)}, u32[]{:S(2)}, u32[]{:S(2)}) collective-permute-start(bf16[128,1024]{1,0:T(8,128)(2,1)S(1)} %collective-permute-done.refs_2_), channel_id=1, source_target_pairs={{0,4},{1,3},{4,8},{5,1},{8,12},{9,5},{12,14},{13,9},{14,10},{15,13... | collective-permute-start | bytes 786440 | tf_op jit(solution)/shard_map/ppermute | solution.py:70
  20.1 7.2 %collective-permute-start.17 = (bf16[144,512]{1,0:T(8,128)(2,1)S(1)}, bf16[144,512]{1,0:T(8,128)(2,1)S(1)}, u32[]{:S(2)}, u32[]{:S(2)}) collective-permute-start(bf16[144,512]{1,0:T(8,128)(2,1)S(1)} %collective-permute-done.14.refs_7_), channel_id=1, source_target_pairs={{0,4},{1,3},{4,8},{5,1},{8,12},{9,5},{12,14},{13,9},{14,10},{15,13... | collective-permute-start | bytes 442376 | tf_op jit(solution)/shard_map/ppermute | solution.py:91
  22.9 6.0 %collective-permute-start.5 = (bf16[144,512]{1,0:T(8,128)(2,1)S(1)}, bf16[144,512]{1,0:T(8,128)(2,1)S(1)}, u32[]{:S(2)}, u32[]{:S(2)}) collective-permute-start(bf16[144,512]{1,0:T(8,128)(2,1)S(1)} %collective-permute-done.4.refs_10_), channel_id=1, source_target_pairs={{0,4},{1,3},{4,8},{5,1},{8,12},{9,5},{12,14},{13,9},{14,10},{15,13... | collective-permute-start | bytes 442376 | tf_op jit(solution)/shard_map/ppermute | solution.py:88
  24.4 7.2 %collective-permute-start.9 = (bf16[128,1024]{1,0:T(8,128)(2,1)S(1)}, bf16[128,1024]{1,0:T(8,128)(2,1)S(1)}, u32[]{:S(2)}, u32[]{:S(2)}) collective-permute-start(bf16[128,1024]{1,0:T(8,128)(2,1)S(1)} %collective-permute-done.8.refs_7_), channel_id=1, source_target_pairs={{0,4},{1,3},{4,8},{5,1},{8,12},{9,5},{12,14},{13,9},{14,10},{15,13... | collective-permute-start | bytes 786440 | tf_op jit(solution)/shard_map/ppermute | solution.py:71
  28.9 9.6 %collective-permute-start.6 = (bf16[128,1024]{1,0:T(8,128)(2,1)S(1)}, bf16[128,1024]{1,0:T(8,128)(2,1)S(1)}, u32[]{:S(2)}, u32[]{:S(2)}) collective-permute-start(bf16[128,1024]{1,0:T(8,128)(2,1)S(1)} %collective-permute-done.1.refs_6_), channel_id=1, source_target_pairs={{0,4},{1,3},{4,8},{5,1},{8,12},{9,5},{12,14},{13,9},{14,10},{15,13... | collective-permute-start | bytes 786440 | tf_op jit(solution)/shard_map/ppermute | solution.py:70
  30.5 8.4 %collective-permute-start.21 = (bf16[128,1024]{1,0:T(8,128)(2,1)S(1)}, bf16[128,1024]{1,0:T(8,128)(2,1)S(1)}, u32[]{:S(2)}, u32[]{:S(2)}) collective-permute-start(bf16[128,1024]{1,0:T(8,128)(2,1)S(1)} %copy-done.5), channel_id=1, source_target_pairs={{0,1},{1,0},{2,3},{3,2},{4,5},{5,4},{6,7},{7,6},{8,9},{9,8},{10,11... | collective-permute-start | bytes 786440 | tf_op jit(solution)/shard_map/ppermute | solution.py:75
  30.6 8.6 %collective-permute-start.22 = (bf16[128,1024]{1,0:T(8,128)(2,1)S(1)}, bf16[128,1024]{1,0:T(8,128)(2,1)S(1)}, u32[]{:S(2)}, u32[]{:S(2)}) collective-permute-start(bf16[128,1024]{1,0:T(8,128)(2,1)S(1)} %collective-permute-done.refs_2_), channel_id=1, source_target_pairs={{0,1},{1,0},{2,3},{3,2},{4,5},{5,4},{6,7},{7,6},{8,9},{9,8},{10,11... | collective-permute-start | bytes 786440 | tf_op jit(solution)/shard_map/ppermute | solution.py:77
  31.2 9.7 %collective-permute-start.23 = (bf16[128,1024]{1,0:T(8,128)(2,1)S(1)}, bf16[128,1024]{1,0:T(8,128)(2,1)S(1)}, u32[]{:S(2)}, u32[]{:S(2)}) collective-permute-start(bf16[128,1024]{1,0:T(8,128)(2,1)S(1)} %collective-permute-done.7.refs_3_), channel_id=1, source_target_pairs={{0,1},{1,0},{2,3},{3,2},{4,5},{5,4},{6,7},{7,6},{8,9},{9,8},{10,11... | collective-permute-start | bytes 786440 | tf_op jit(solution)/shard_map/ppermute | solution.py:78
  31.6 10.7 %collective-permute-start.24 = (bf16[128,1024]{1,0:T(8,128)(2,1)S(1)}, bf16[128,1024]{1,0:T(8,128)(2,1)S(1)}, u32[]{:S(2)}, u32[]{:S(2)}) collective-permute-start(bf16[128,1024]{1,0:T(8,128)(2,1)S(1)} %collective-permute-done.1.refs_6_), channel_id=1, source_target_pairs={{0,1},{1,0},{2,3},{3,2},{4,5},{5,4},{6,7},{7,6},{8,9},{9,8},{10,11... | collective-permute-start | bytes 786440 | tf_op jit(solution)/shard_map/ppermute | solution.py:77
  38.5 7.3 %collective-permute-start.25 = (bf16[128,1024]{1,0:T(8,128)(2,1)S(1)}, bf16[128,1024]{1,0:T(8,128)(2,1)S(1)}, u32[]{:S(2)}, u32[]{:S(2)}) collective-permute-start(bf16[128,1024]{1,0:T(8,128)(2,1)S(1)} %collective-permute-done.8.refs_7_), channel_id=1, source_target_pairs={{0,1},{1,0},{2,3},{3,2},{4,5},{5,4},{6,7},{7,6},{8,9},{9,8},{10,11... | collective-permute-start | bytes 786440 | tf_op jit(solution)/shard_map/ppermute | solution.py:78
  38.9 6.9 %collective-permute-start.27 = (bf16[128,1024]{1,0:T(8,128)(2,1)S(1)}, bf16[128,1024]{1,0:T(8,128)(2,1)S(1)}, u32[]{:S(2)}, u32[]{:S(2)}) collective-permute-start(bf16[128,1024]{1,0:T(8,128)(2,1)S(1)} %collective-permute-done.9.refs_11_), channel_id=1, source_target_pairs={{0,1},{1,0},{2,3},{3,2},{4,5},{5,4},{6,7},{7,6},{8,9},{9,8},{10,11... | collective-permute-start | bytes 786440 | tf_op jit(solution)/shard_map/ppermute | solution.py:78
  50.0 8.3 %collective-permute-start.34 = (bf16[128,1024]{1,0:T(8,128)(2,1)S(1)}, bf16[128,1024]{1,0:T(8,128)(2,1)S(1)}, u32[]{:S(2)}, u32[]{:S(2)}) collective-permute-start(bf16[128,1024]{1,0:T(8,128)(2,1)S(1)} %get-tuple-element.37.refs_0_), channel_id=1, source_target_pairs={{0,4},{1,3},{4,8},{5,1},{8,12},{9,5},{12,14},{13,9},{14,10},{15,13... | collective-permute-start | bytes 786440 | tf_op jit(solution)/shard_map/ppermute | solution.py:70
  51.6 8.2 %collective-permute-start.35 = (bf16[128,1024]{1,0:T(8,128)(2,1)S(1)}, bf16[128,1024]{1,0:T(8,128)(2,1)S(1)}, u32[]{:S(2)}, u32[]{:S(2)}) collective-permute-start(bf16[128,1024]{1,0:T(8,128)(2,1)S(1)} %get-tuple-element.37.refs_0_), channel_id=1, source_target_pairs={{1,4},{0,3},{5,8},{4,1},{9,12},{8,5},{13,14},{12,9},{15,10},{14,13... | collective-permute-start | bytes 786440 | tf_op jit(solution)/shard_map/ppermute | solution.py:71
  58.3 6.4 %collective-permute-start.39 = (bf16[128,1024]{1,0:T(8,128)(2,1)S(1)}, bf16[128,1024]{1,0:T(8,128)(2,1)S(1)}, u32[]{:S(2)}, u32[]{:S(2)}) collective-permute-start(bf16[128,1024]{1,0:T(8,128)(2,1)S(1)} %collective-permute-done.34.refs_0_), channel_id=1, source_target_pairs={{0,4},{1,3},{4,8},{5,1},{8,12},{9,5},{12,14},{13,9},{14,10},{15,13... | collective-permute-start | bytes 786440 | tf_op jit(solution)/shard_map/ppermute | solution.py:70
  59.8 7.7 %collective-permute-start.40 = (bf16[128,1024]{1,0:T(8,128)(2,1)S(1)}, bf16[128,1024]{1,0:T(8,128)(2,1)S(1)}, u32[]{:S(2)}, u32[]{:S(2)}) collective-permute-start(bf16[128,1024]{1,0:T(8,128)(2,1)S(1)} %collective-permute-done.35.refs_1_), channel_id=1, source_target_pairs={{0,4},{1,3},{4,8},{5,1},{8,12},{9,5},{12,14},{13,9},{14,10},{15,13... | collective-permute-start | bytes 786440 | tf_op jit(solution)/shard_map/ppermute | solution.py:71
  64.7 6.4 %collective-permute-start.44 = (bf16[128,1024]{1,0:T(8,128)(2,1)S(1)}, bf16[128,1024]{1,0:T(8,128)(2,1)S(1)}, u32[]{:S(2)}, u32[]{:S(2)}) collective-permute-start(bf16[128,1024]{1,0:T(8,128)(2,1)S(1)} %collective-permute-done.39.refs_0_), channel_id=1, source_target_pairs={{0,4},{1,3},{4,8},{5,1},{8,12},{9,5},{12,14},{13,9},{14,10},{15,13... | collective-permute-start | bytes 786440 | tf_op jit(solution)/shard_map/ppermute | solution.py:70
  67.5 6.4 %collective-permute-start.45 = (bf16[128,1024]{1,0:T(8,128)(2,1)S(1)}, bf16[128,1024]{1,0:T(8,128)(2,1)S(1)}, u32[]{:S(2)}, u32[]{:S(2)}) collective-permute-start(bf16[128,1024]{1,0:T(8,128)(2,1)S(1)} %collective-permute-done.40.refs_1_), channel_id=1, source_target_pairs={{0,4},{1,3},{4,8},{5,1},{8,12},{9,5},{12,14},{13,9},{14,10},{15,13... | collective-permute-start | bytes 786440 | tf_op jit(solution)/shard_map/ppermute | solution.py:71
  84.1 7.0 %collective-permute-start.48 = (bf16[256,1024]{1,0:T(8,128)(2,1)S(1)}, bf16[256,1024]{1,0:T(8,128)(2,1)S(1)}, u32[]{:S(2)}, u32[]{:S(2)}) collective-permute-start(bf16[256,1024]{1,0:T(8,128)(2,1)S(1)} %get-tuple-element.45), channel_id=1, source_target_pairs={{0,1},{1,0},{2,3},{3,2},{4,5},{5,4},{6,7},{7,6},{8,9},{9,8},{10,11... | collective-permute-start | bytes 1572872 | tf_op jit(solution)/shard_map/ppermute | solution.py:110
  87.6 14.5 %collective-permute-start.32 = (bf16[128,1024]{1,0:T(8,128)(2,1)S(1)}, bf16[128,1024]{1,0:T(8,128)(2,1)S(1)}, u32[]{:S(2)}, u32[]{:S(2)}) collective-permute-start(bf16[128,1024]{1,0:T(8,128)(2,1)S(1)} %get-tuple-element.37.refs_0_), channel_id=1, source_target_pairs={{0,1},{1,0},{2,3},{3,2},{4,5},{5,4},{6,7},{7,6},{8,9},{9,8},{10,11... | collective-permute-start | bytes 786440 | tf_op jit(solution)/shard_map/ppermute | solution.py:75
  91.1 6.4 %collective-permute-start.55 = (bf16[128,1024]{1,0:T(8,128)(2,1)S(1)}, bf16[128,1024]{1,0:T(8,128)(2,1)S(1)}, u32[]{:S(2)}, u32[]{:S(2)}) collective-permute-start(bf16[128,1024]{1,0:T(8,128)(2,1)S(1)} %add_convert_fusion.6), channel_id=1, source_target_pairs={{4,0},{3,1},{8,4},{1,5},{12,8},{5,9},{14,12},{9,13},{10,14},{13,15... | collective-permute-start | bytes 786440 | tf_op jit(solution)/shard_map/ppermute | solution.py:121
  92.9 7.5 %collective-permute-start.59 = (bf16[128,1024]{1,0:T(8,128)(2,1)S(1)}, bf16[128,1024]{1,0:T(8,128)(2,1)S(1)}, u32[]{:S(2)}, u32[]{:S(2)}) collective-permute-start(bf16[128,1024]{1,0:T(8,128)(2,1)S(1)} %add_convert_fusion.3), channel_id=1, source_target_pairs={{4,0},{3,1},{8,4},{1,5},{12,8},{5,9},{14,12},{9,13},{10,14},{13,15... | collective-permute-start | bytes 786440 | tf_op jit(solution)/shard_map/ppermute | solution.py:122
  96.5 6.8 %collective-permute-start.38 = (bf16[256,1024]{1,0:T(8,128)(2,1)S(1)}, bf16[256,1024]{1,0:T(8,128)(2,1)S(1)}, u32[]{:S(2)}, u32[]{:S(2)}) collective-permute-start(bf16[256,1024]{1,0:T(8,128)(2,1)S(1)} %get-tuple-element.41), channel_id=1, source_target_pairs={{0,1},{1,0},{2,3},{3,2},{4,5},{5,4},{6,7},{7,6},{8,9},{9,8},{10,11... | collective-permute-start | bytes 1572872 | tf_op jit(solution)/shard_map/ppermute | solution.py:110
  97.7 6.4 %collective-permute-start.56 = (bf16[128,1024]{1,0:T(8,128)(2,1)S(1)}, bf16[128,1024]{1,0:T(8,128)(2,1)S(1)}, u32[]{:S(2)}, u32[]{:S(2)}) collective-permute-start(bf16[128,1024]{1,0:T(8,128)(2,1)S(1)} %add_convert_fusion.5), channel_id=1, source_target_pairs={{4,0},{3,1},{8,4},{1,5},{12,8},{5,9},{14,12},{9,13},{10,14},{13,15... | collective-permute-start | bytes 786440 | tf_op jit(solution)/shard_map/ppermute | solution.py:121
  100.5 6.4 %collective-permute-start.60 = (bf16[128,1024]{1,0:T(8,128)(2,1)S(1)}, bf16[128,1024]{1,0:T(8,128)(2,1)S(1)}, u32[]{:S(2)}, u32[]{:S(2)}) collective-permute-start(bf16[128,1024]{1,0:T(8,128)(2,1)S(1)} %add_convert_fusion.2), channel_id=1, source_target_pairs={{4,0},{3,1},{8,4},{1,5},{12,8},{5,9},{14,12},{9,13},{10,14},{13,15... | collective-permute-start | bytes 786440 | tf_op jit(solution)/shard_map/ppermute | solution.py:122
  104.2 6.4 %collective-permute-start.57 = (bf16[128,1024]{1,0:T(8,128)(2,1)S(1)}, bf16[128,1024]{1,0:T(8,128)(2,1)S(1)}, u32[]{:S(2)}, u32[]{:S(2)}) collective-permute-start(bf16[128,1024]{1,0:T(8,128)(2,1)S(1)} %add_convert_fusion.4), channel_id=1, source_target_pairs={{4,0},{3,1},{8,4},{1,5},{12,8},{5,9},{14,12},{9,13},{10,14},{13,15... | collective-permute-start | bytes 786440 | tf_op jit(solution)/shard_map/ppermute | solution.py:121
  (53 other events, 390.0 us)

commit v6 on v5

--- a/solution.py
+++ b/solution.py
@@ -349,7 +349,7 @@
             pltpu.VMEM((depth * devices, residual.shape[1]), BF16),
             pltpu.SemaphoreType.DMA((len(refs),)),
         ],
-        compiler_params=pltpu.CompilerParams(vmem_limit_bytes=24 * 2**20),
+        compiler_params=pltpu.CompilerParams(vmem_limit_bytes=14 * 2**20),
         cost_estimate=pl.CostEstimate(
             flops=2 * residual.shape[0] * depth * devices * residual.shape[1],
             bytes_accessed=6 * 2**20,
@@ -430,7 +430,7 @@
     attention, scales = made["attention"], made["scales"]
     hidden, normed = project(own, attention, residual, norm_gain, weights, depth, devices)
 
-    half, cut = devices // 4, rows // 2
+    half, cut = devices // 4, rows // 8 * 5
     tokens, _ = ring_gather(normed, cut, devices)
     names = piece_names(devices)
     kept, sent = {}, {}

time: 114 us -> 113 us (level)
  starting transfers between devices: 50.6 us -> 48.4 us
  waiting for transfers between devices: 41.5 us -> 42.9 us
    ppermute x8, waiting for transfers between devices: 7.7 us -> 14.9 us  [ring_gather(): lax.ppermute(second if j < half else second[:cut], 'seq', across if j ==...]
    ppermute x8, waiting for transfers between devices: 14 us -> 6.82 us  [ring_gather(): first = lax.ppermute(first if j < half else first[cut:], 'seq', ring)]
  transfers between devices with their start and end apart: 62 -> 62, of which waited for: 25 -> 26; matrix products, arithmetic and copies ran while one was open for 1% -> 1% of each run, Pallas kernels for 14% -> 14%
where the time goes in v6:
time: 113 us
  starting transfers between devices  48.4 us (43%)
  waiting for transfers between devices  42.9 us (38%)
  Pallas kernels  18.5 us (16%)
  other arithmetic  1.63 us (1%)
  between operations  1.14 us (1%)
    ppermute x8, waiting for transfers between devices, ring_gather(): lax.ppermute(second if j < half else second[:cut], 'seq', across if j ==...  14.9 us
    ppermute x8, starting transfers between devices, ring_gather(): first = lax.ppermute(first if j < half else first[cut:], 'seq', ring)  12.1 us
    ppermute x8, starting transfers between devices, ring_gather(): lax.ppermute(second if j < half else second[:cut], 'seq', across if j ==...  11.6 us
    pallas_call x5, Pallas kernels, expert(): pl.pallas_call(functools.partial(expert_kernel, parts), out_shape=(shape,...  7.5 us
    ppermute x4, waiting for transfers between devices, ring_scatter_sum(): first = [lax.ppermute(total, 'seq', ring)]  6.92 us
    ppermute x8, waiting for transfers between devices, ring_gather(): first = lax.ppermute(first if j < half else first[cut:], 'seq', ring)  6.82 us
    pallas_call x1, Pallas kernels, attend(): pl.pallas_call(functools.partial(attend_kernel, devices), out_shape=(jax....  6.58 us
    ppermute x4, starting transfers between devices, ring_scatter_sum(): first = [lax.ppermute(total, 'seq', ring)]  6.21 us
  transfers between devices with their start and end apart: 62, of which 26 were waited for; matrix products, arithmetic and copies ran while one was open for 1% of the time, Pallas kernels for 14%

profile of v6, /device:TPU:0, one launch (start us, length us, event | category | flops | bytes accessed | tf_op | source)
XLA Modules:
  0.0 112.8 jit_solution(8048876735712708500)
XLA Ops:
  0.6 2.5 %collective-permute-start.7 = (bf16[128,1024]{1,0:T(8,128)(2,1)}, bf16[128,1024]{1,0:T(8,128)(2,1)S(1)}, u32[]{:S(2)}, u32[]{:S(2)}) collective-permute-start(bf16[128,1024]{1,0:T(8,128)(2,1)} %refs_0_.1), channel_id=1, source_target_pairs={{1,4},{0,3},{5,8},{4,1},{9,12},{8,5},{13,14},{12,9},{15,10},{14,13... | collective-permute-start | bytes 786440 | tf_op jit(solution)/shard_map/ppermute | solution.py:71
  3.1 1.6 %pack.1.refs_0_ = bf16[144,512]{1,0:T(8,128)(2,1)} custom-call(bf16[128,256]{1,0:T(8,128)(2,1)} %key_ref.1, bf16[128,256]{1,0:T(8,128)(2,1)} %value_ref.1, s32[8,128]{1,0:T(8,128)} %bitcast.21, f32[8,128]{1,0:T(8,128)} %bitcast.22), custom_call_target="tpu_custom_call" | custom-call | flops 1000000 | bytes 1048576 | tf_op jit(solution)/shard_map/pack/pallas_call | solution.py:155
  5.3 1.6 %collective-permute-start = (bf16[128,1024]{1,0:T(8,128)(2,1)S(1)}, bf16[128,1024]{1,0:T(8,128)(2,1)S(1)}, u32[]{:S(2)}, u32[]{:S(2)}) collective-permute-start(bf16[128,1024]{1,0:T(8,128)(2,1)S(1)} %copy-done.5), channel_id=1, source_target_pairs={{0,4},{1,3},{4,8},{5,1},{8,12},{9,5},{12,14},{13,9},{14,10},{15,13... | collective-permute-start | bytes 786440 | tf_op jit(solution)/shard_map/ppermute | solution.py:70
  8.6 1.4 %collective-permute-done.2.refs_2_ = bf16[144,512]{1,0:T(8,128)(2,1)S(1)} collective-permute-done((bf16[144,512]{1,0:T(8,128)(2,1)}, bf16[144,512]{1,0:T(8,128)(2,1)S(1)}, u32[]{:S(2)}, u32[]{:S(2)}) %collective-permute-start.2) | collective-permute-done | bytes 147488 | tf_op jit(solution)/shard_map/ppermute | solution.py:88
  11.3 2.0 %collective-permute-done.11.refs_3_ = bf16[144,512]{1,0:T(8,128)(2,1)S(1)} collective-permute-done((bf16[144,512]{1,0:T(8,128)(2,1)}, bf16[144,512]{1,0:T(8,128)(2,1)S(1)}, u32[]{:S(2)}, u32[]{:S(2)}) %collective-permute-start.11) | collective-permute-done | bytes 147488 | tf_op jit(solution)/shard_map/ppermute | solution.py:91
  13.3 1.6 %collective-permute-start.14 = (bf16[144,512]{1,0:T(8,128)(2,1)S(1)}, bf16[144,512]{1,0:T(8,128)(2,1)S(1)}, u32[]{:S(2)}, u32[]{:S(2)}) collective-permute-start(bf16[144,512]{1,0:T(8,128)(2,1)S(1)} %collective-permute-done.11.refs_3_), channel_id=1, source_target_pairs={{0,4},{1,3},{4,8},{5,1},{8,12},{9,5},{12,14},{13,9},{14,10},{15,13... | collective-permute-start | bytes 442376 | tf_op jit(solution)/shard_map/ppermute | solution.py:91
  14.9 1.5 %collective-permute-start.8 = (bf16[128,1024]{1,0:T(8,128)(2,1)S(1)}, bf16[128,1024]{1,0:T(8,128)(2,1)S(1)}, u32[]{:S(2)}, u32[]{:S(2)}) collective-permute-start(bf16[128,1024]{1,0:T(8,128)(2,1)S(1)} %collective-permute-done.7.refs_3_), channel_id=1, source_target_pairs={{0,4},{1,3},{4,8},{5,1},{8,12},{9,5},{12,14},{13,9},{14,10},{15,13... | collective-permute-start | bytes 786440 | tf_op jit(solution)/shard_map/ppermute | solution.py:71
  17.0 1.5 %collective-permute-start.4 = (bf16[144,512]{1,0:T(8,128)(2,1)S(1)}, bf16[144,512]{1,0:T(8,128)(2,1)S(1)}, u32[]{:S(2)}, u32[]{:S(2)}) collective-permute-start(bf16[144,512]{1,0:T(8,128)(2,1)S(1)} %collective-permute-done.3.refs_6_), channel_id=1, source_target_pairs={{0,4},{1,3},{4,8},{5,1},{8,12},{9,5},{12,14},{13,9},{14,10},{15,13... | collective-permute-start | bytes 442376 | tf_op jit(solution)/shard_map/ppermute | solution.py:88
  18.5 1.6 %collective-permute-start.1 = (bf16[128,1024]{1,0:T(8,128)(2,1)S(1)}, bf16[128,1024]{1,0:T(8,128)(2,1)S(1)}, u32[]{:S(2)}, u32[]{:S(2)}) collective-permute-start(bf16[128,1024]{1,0:T(8,128)(2,1)S(1)} %collective-permute-done.refs_2_), channel_id=1, source_target_pairs={{0,4},{1,3},{4,8},{5,1},{8,12},{9,5},{12,14},{13,9},{14,10},{15,13... | collective-permute-start | bytes 786440 | tf_op jit(solution)/shard_map/ppermute | solution.py:70
  20.1 1.5 %collective-permute-start.17 = (bf16[144,512]{1,0:T(8,128)(2,1)S(1)}, bf16[144,512]{1,0:T(8,128)(2,1)S(1)}, u32[]{:S(2)}, u32[]{:S(2)}) collective-permute-start(bf16[144,512]{1,0:T(8,128)(2,1)S(1)} %collective-permute-done.14.refs_7_), channel_id=1, source_target_pairs={{0,4},{1,3},{4,8},{5,1},{8,12},{9,5},{12,14},{13,9},{14,10},{15,13... | collective-permute-start | bytes 442376 | tf_op jit(solution)/shard_map/ppermute | solution.py:91
  22.9 1.6 %collective-permute-start.5 = (bf16[144,512]{1,0:T(8,128)(2,1)S(1)}, bf16[144,512]{1,0:T(8,128)(2,1)S(1)}, u32[]{:S(2)}, u32[]{:S(2)}) collective-permute-start(bf16[144,512]{1,0:T(8,128)(2,1)S(1)} %collective-permute-done.4.refs_10_), channel_id=1, source_target_pairs={{0,4},{1,3},{4,8},{5,1},{8,12},{9,5},{12,14},{13,9},{14,10},{15,13... | collective-permute-start | bytes 442376 | tf_op jit(solution)/shard_map/ppermute | solution.py:88
  24.4 1.5 %collective-permute-start.9 = (bf16[128,1024]{1,0:T(8,128)(2,1)S(1)}, bf16[128,1024]{1,0:T(8,128)(2,1)S(1)}, u32[]{:S(2)}, u32[]{:S(2)}) collective-permute-start(bf16[128,1024]{1,0:T(8,128)(2,1)S(1)} %collective-permute-done.8.refs_7_), channel_id=1, source_target_pairs={{0,4},{1,3},{4,8},{5,1},{8,12},{9,5},{12,14},{13,9},{14,10},{15,13... | collective-permute-start | bytes 786440 | tf_op jit(solution)/shard_map/ppermute | solution.py:71
  28.9 1.6 %collective-permute-start.6 = (bf16[128,1024]{1,0:T(8,128)(2,1)S(1)}, bf16[128,1024]{1,0:T(8,128)(2,1)S(1)}, u32[]{:S(2)}, u32[]{:S(2)}) collective-permute-start(bf16[128,1024]{1,0:T(8,128)(2,1)S(1)} %collective-permute-done.1.refs_6_), channel_id=1, source_target_pairs={{0,4},{1,3},{4,8},{5,1},{8,12},{9,5},{12,14},{13,9},{14,10},{15,13... | collective-permute-start | bytes 786440 | tf_op jit(solution)/shard_map/ppermute | solution.py:70
  31.9 6.6 %attend.1 = (bf16[128,2048]{1,0:T(8,128)(2,1)}, f32[128,128]{1,0:T(8,128)}) custom-call(s32[1]{0:T(128)} %bitcast.2.own_ref, s32[16]{0:T(128)} %doc_ref.1, bf16[128,2048]{1,0:T(8,128)(2,1)} %q_ref.1, bf16[144,512]{1,0:T(8,128)(2,1)} %pack.1.refs_0_, bf16[144,512]{1,0:T(8,128)(2,1)} %copy-done.10, bf16[144,512]{1,0:T(8,128)(2,1)} %copy-done.8, ...), custom_call_target="tpu_custom_call" | custom-call | flops 1207959552 | bytes 8388608 | tf_op jit(solution)/shard_map/attend/pallas_call | solution.py:285
  39.2 1.7 %collective-permute-start.28 = (bf16[64,1024]{1,0:T(8,128)(2,1)S(1)}, bf16[64,1024]{1,0:T(8,128)(2,1)S(1)}, u32[]{:S(2)}, u32[]{:S(2)}) collective-permute-start(bf16[64,1024]{1,0:T(8,128)(2,1)S(1)} %slice.60), channel_id=1, source_target_pairs={{0,4},{1,3},{4,8},{5,1},{8,12},{9,5},{12,14},{13,9},{14,10},{15,13... | collective-permute-start | bytes 393224 | tf_op jit(solution)/shard_map/ppermute | solution.py:71
  42.2 2.0 %collective-permute-done.28.refs_16_ = bf16[64,1024]{1,0:T(8,128)(2,1)S(1)} collective-permute-done((bf16[64,1024]{1,0:T(8,128)(2,1)S(1)}, bf16[64,1024]{1,0:T(8,128)(2,1)S(1)}, u32[]{:S(2)}, u32[]{:S(2)}) %collective-permute-start.28) | collective-permute-done | bytes 131104 | tf_op jit(solution)/shard_map/ppermute | solution.py:71
  44.2 1.7 %collective-permute-done.30.refs_15_ = bf16[64,1024]{1,0:T(8,128)(2,1)S(1)} collective-permute-done((bf16[64,1024]{1,0:T(8,128)(2,1)S(1)}, bf16[64,1024]{1,0:T(8,128)(2,1)S(1)}, u32[]{:S(2)}, u32[]{:S(2)}) %collective-permute-start.30) | collective-permute-done | bytes 131104 | tf_op jit(solution)/shard_map/ppermute | solution.py:70
  47.2 2.8 %project.1 = (bf16[128,1024]{1,0:T(8,128)(2,1)}, bf16[128,1024]{1,0:T(8,128)(2,1)S(1)}) custom-call(s32[1]{0:T(128)} %bitcast.2.own_ref, bf16[128,2048]{1,0:T(8,128)(2,1)S(1)} %copy-done.3, bf16[128,1024]{1,0:T(8,128)(2,1)S(1)} %copy-done.4, bf16[1,1024]{1,0:T(2,128)(2,1)S(1)} %reshape.13.gain_ref, bf16[128,1024]{1,0:T(8,128)(2,1)S(1)} %copy-done.5, ...), custom_call_target="tpu_custom_call" | custom-call | flops 536870912 | bytes 6291456 | tf_op jit(solution)/shard_map/project/pallas_call | solution.py:343
  50.4 1.5 %collective-permute-start.34 = (bf16[128,1024]{1,0:T(8,128)(2,1)S(1)}, bf16[128,1024]{1,0:T(8,128)(2,1)S(1)}, u32[]{:S(2)}, u32[]{:S(2)}) collective-permute-start(bf16[128,1024]{1,0:T(8,128)(2,1)S(1)} %get-tuple-element.37.refs_0_), channel_id=1, source_target_pairs={{0,4},{1,3},{4,8},{5,1},{8,12},{9,5},{12,14},{13,9},{14,10},{15,13... | collective-permute-start | bytes 786440 | tf_op jit(solution)/shard_map/ppermute | solution.py:70
  51.9 6.0 %collective-permute-done.35.refs_1_ = bf16[128,1024]{1,0:T(8,128)(2,1)S(1)} collective-permute-done((bf16[128,1024]{1,0:T(8,128)(2,1)S(1)}, bf16[128,1024]{1,0:T(8,128)(2,1)S(1)}, u32[]{:S(2)}, u32[]{:S(2)}) %collective-permute-start.35) | collective-permute-done | bytes 262176 | tf_op jit(solution)/shard_map/ppermute | solution.py:71
  59.2 1.6 %collective-permute-start.39 = (bf16[128,1024]{1,0:T(8,128)(2,1)S(1)}, bf16[128,1024]{1,0:T(8,128)(2,1)S(1)}, u32[]{:S(2)}, u32[]{:S(2)}) collective-permute-start(bf16[128,1024]{1,0:T(8,128)(2,1)S(1)} %collective-permute-done.34.refs_0_), channel_id=1, source_target_pairs={{0,4},{1,3},{4,8},{5,1},{8,12},{9,5},{12,14},{13,9},{14,10},{15,13... | collective-permute-start | bytes 786440 | tf_op jit(solution)/shard_map/ppermute | solution.py:70
  60.8 3.4 %collective-permute-done.40.refs_1_ = bf16[128,1024]{1,0:T(8,128)(2,1)S(1)} collective-permute-done((bf16[128,1024]{1,0:T(8,128)(2,1)S(1)}, bf16[128,1024]{1,0:T(8,128)(2,1)S(1)}, u32[]{:S(2)}, u32[]{:S(2)}) %collective-permute-start.40) | collective-permute-done | bytes 262176 | tf_op jit(solution)/shard_map/ppermute | solution.py:71
  65.5 1.5 %collective-permute-done.39.refs_0_ = bf16[128,1024]{1,0:T(8,128)(2,1)S(1)} collective-permute-done((bf16[128,1024]{1,0:T(8,128)(2,1)S(1)}, bf16[128,1024]{1,0:T(8,128)(2,1)S(1)}, u32[]{:S(2)}, u32[]{:S(2)}) %collective-permute-start.39) | collective-permute-done | bytes 262176 | tf_op jit(solution)/shard_map/ppermute | solution.py:70
  68.3 2.2 %collective-permute-done.45.refs_1_ = bf16[128,1024]{1,0:T(8,128)(2,1)S(1)} collective-permute-done((bf16[128,1024]{1,0:T(8,128)(2,1)S(1)}, bf16[128,1024]{1,0:T(8,128)(2,1)S(1)}, u32[]{:S(2)}, u32[]{:S(2)}) %collective-permute-start.45) | collective-permute-done | bytes 262176 | tf_op jit(solution)/shard_map/ppermute | solution.py:71
  73.4 1.6 %collective-permute-start.49 = (bf16[48,1024]{1,0:T(8,128)(2,1)S(1)}, bf16[48,1024]{1,0:T(8,128)(2,1)S(1)}, u32[]{:S(2)}, u32[]{:S(2)}) collective-permute-start(bf16[48,1024]{1,0:T(8,128)(2,1)S(1)} %slice.83), channel_id=1, source_target_pairs={{0,4},{1,3},{4,8},{5,1},{8,12},{9,5},{12,14},{13,9},{14,10},{15,13... | collective-permute-start | bytes 294920 | tf_op jit(solution)/shard_map/ppermute | solution.py:70
  76.0 2.3 %collective-permute-done.49.refs_0_ = bf16[48,1024]{1,0:T(8,128)(2,1)S(1)} collective-permute-done((bf16[48,1024]{1,0:T(8,128)(2,1)S(1)}, bf16[48,1024]{1,0:T(8,128)(2,1)S(1)}, u32[]{:S(2)}, u32[]{:S(2)}) %collective-permute-start.49) | collective-permute-done | bytes 98336 | tf_op jit(solution)/shard_map/ppermute | solution.py:70
  81.4 1.8 %expert.8 = (bf16[256,1024]{1,0:T(8,128)(2,1)S(1)}, bf16[256,1024]{1,0:T(8,128)(2,1)S(1)}) custom-call(f32[128,128]{1,0:T(8,128)S(1)} %copy-done.6, bf16[1024,384]{1,0:T(8,128)(2,1)S(1)} %bitcast.7, bf16[1024,384]{1,0:T(8,128)(2,1)S(1)} %bitcast.12, bf16[384,1024]{1,0:T(8,128)(2,1)S(1)} %bitcast.17, bf16[128,1024]{1,0:T(8,128)(2,1)S(1)} %collective-permute-done.44.refs_0_, ...), custom_call_target="tpu_custom_call" | custom-call | flops 1207959552 | bytes 4194304 | tf_op jit(solution)/shard_map/expert/pallas_call | solution.py:380
  85.0 1.9 %collective-permute-start.54 = (bf16[48,1024]{1,0:T(8,128)(2,1)S(1)}, bf16[48,1024]{1,0:T(8,128)(2,1)S(1)}, u32[]{:S(2)}, u32[]{:S(2)}) collective-permute-start(bf16[48,1024]{1,0:T(8,128)(2,1)S(1)} %add_convert_fusion.8), channel_id=1, source_target_pairs={{4,0},{3,1},{8,4},{1,5},{12,8},{5,9},{14,12},{9,13},{10,14},{13,15... | collective-permute-start | bytes 294920 | tf_op jit(solution)/shard_map/ppermute | solution.py:121
  86.9 1.8 %expert.7 = (bf16[256,1024]{1,0:T(8,128)(2,1)S(1)}, bf16[256,1024]{1,0:T(8,128)(2,1)S(1)}) custom-call(f32[128,128]{1,0:T(8,128)S(1)} %copy-done.6, bf16[1024,384]{1,0:T(8,128)(2,1)S(1)} %bitcast.8, bf16[1024,384]{1,0:T(8,128)(2,1)S(1)} %bitcast.13, bf16[384,1024]{1,0:T(8,128)(2,1)S(1)} %bitcast.18, bf16[128,1024]{1,0:T(8,128)(2,1)S(1)} %collective-permute-done.39.refs_0_, ...), custom_call_target="tpu_custom_call" | custom-call | flops 1207959552 | bytes 4194304 | tf_op jit(solution)/shard_map/expert/pallas_call | solution.py:380
  93.1 1.8 %expert.6 = (bf16[256,1024]{1,0:T(8,128)(2,1)S(1)}, bf16[256,1024]{1,0:T(8,128)(2,1)S(1)}) custom-call(f32[128,128]{1,0:T(8,128)S(1)} %copy-done.6, bf16[1024,384]{1,0:T(8,128)(2,1)S(1)} %bitcast.9, bf16[1024,384]{1,0:T(8,128)(2,1)S(1)} %bitcast.14, bf16[384,1024]{1,0:T(8,128)(2,1)S(1)} %bitcast.19, bf16[128,1024]{1,0:T(8,128)(2,1)S(1)} %collective-permute-done.34.refs_0_, ...), custom_call_target="tpu_custom_call" | custom-call | flops 1207959552 | bytes 4194304 | tf_op jit(solution)/shard_map/expert/pallas_call | solution.py:380
  106.2 3.5 %collective-permute-done.57 = bf16[128,1024]{1,0:T(8,128)(2,1)S(1)} collective-permute-done((bf16[128,1024]{1,0:T(8,128)(2,1)S(1)}, bf16[128,1024]{1,0:T(8,128)(2,1)S(1)}, u32[]{:S(2)}, u32[]{:S(2)}) %collective-permute-start.57) | collective-permute-done | bytes 262176 | tf_op jit(solution)/shard_map/ppermute | solution.py:121
  109.9 2.1 %collective-permute-done.61 = bf16[128,1024]{1,0:T(8,128)(2,1)S(1)} collective-permute-done((bf16[128,1024]{1,0:T(8,128)(2,1)S(1)}, bf16[128,1024]{1,0:T(8,128)(2,1)S(1)}, u32[]{:S(2)}, u32[]{:S(2)}) %collective-permute-start.61) | collective-permute-done | bytes 262176 | tf_op jit(solution)/shard_map/ppermute | solution.py:122
  (166 shorter events, 42.5 us)
Async XLA Ops:
  0.6 14.3 %collective-permute-start.7 = (bf16[128,1024]{1,0:T(8,128)(2,1)}, bf16[128,1024]{1,0:T(8,128)(2,1)S(1)}, u32[]{:S(2)}, u32[]{:S(2)}) collective-permute-start(bf16[128,1024]{1,0:T(8,128)(2,1)} %refs_0_.1), channel_id=1, source_target_pairs={{1,4},{0,3},{5,8},{4,1},{9,12},{8,5},{13,14},{12,9},{15,10},{14,13... | collective-permute-start | bytes 786440 | tf_op jit(solution)/shard_map/ppermute | solution.py:71
  5.3 11.1 %collective-permute-start = (bf16[128,1024]{1,0:T(8,128)(2,1)S(1)}, bf16[128,1024]{1,0:T(8,128)(2,1)S(1)}, u32[]{:S(2)}, u32[]{:S(2)}) collective-permute-start(bf16[128,1024]{1,0:T(8,128)(2,1)S(1)} %copy-done.5), channel_id=1, source_target_pairs={{0,4},{1,3},{4,8},{5,1},{8,12},{9,5},{12,14},{13,9},{14,10},{15,13... | collective-permute-start | bytes 786440 | tf_op jit(solution)/shard_map/ppermute | solution.py:70
  6.9 6.4 %collective-permute-start.11 = (bf16[144,512]{1,0:T(8,128)(2,1)}, bf16[144,512]{1,0:T(8,128)(2,1)S(1)}, u32[]{:S(2)}, u32[]{:S(2)}) collective-permute-start(bf16[144,512]{1,0:T(8,128)(2,1)} %pack.1.refs_0_), channel_id=1, source_target_pairs={{1,4},{0,3},{5,8},{4,1},{9,12},{8,5},{13,14},{12,9},{15,10},{14,13... | collective-permute-start | bytes 442376 | tf_op jit(solution)/shard_map/ppermute | solution.py:91
  8.0 8.4 %collective-permute-start.10 = (bf16[144,512]{1,0:T(8,128)(2,1)}, bf16[144,512]{1,0:T(8,128)(2,1)S(1)}, u32[]{:S(2)}, u32[]{:S(2)}) collective-permute-start(bf16[144,512]{1,0:T(8,128)(2,1)} %pack.1.refs_0_), channel_id=1, source_target_pairs={{0,1},{1,0},{2,3},{3,2},{4,5},{5,4},{6,7},{7,6},{8,9},{9,8},{10,11... | collective-permute-start | bytes 442376 | tf_op jit(solution)/shard_map/ppermute | solution.py:93
  10.0 6.9 %collective-permute-start.3 = (bf16[144,512]{1,0:T(8,128)(2,1)S(1)}, bf16[144,512]{1,0:T(8,128)(2,1)S(1)}, u32[]{:S(2)}, u32[]{:S(2)}) collective-permute-start(bf16[144,512]{1,0:T(8,128)(2,1)S(1)} %collective-permute-done.2.refs_2_), channel_id=1, source_target_pairs={{0,4},{1,3},{4,8},{5,1},{8,12},{9,5},{12,14},{13,9},{14,10},{15,13... | collective-permute-start | bytes 442376 | tf_op jit(solution)/shard_map/ppermute | solution.py:88
  14.9 9.5 %collective-permute-start.8 = (bf16[128,1024]{1,0:T(8,128)(2,1)S(1)}, bf16[128,1024]{1,0:T(8,128)(2,1)S(1)}, u32[]{:S(2)}, u32[]{:S(2)}) collective-permute-start(bf16[128,1024]{1,0:T(8,128)(2,1)S(1)} %collective-permute-done.7.refs_3_), channel_id=1, source_target_pairs={{0,4},{1,3},{4,8},{5,1},{8,12},{9,5},{12,14},{13,9},{14,10},{15,13... | collective-permute-start | bytes 786440 | tf_op jit(solution)/shard_map/ppermute | solution.py:71
  18.5 9.3 %collective-permute-start.1 = (bf16[128,1024]{1,0:T(8,128)(2,1)S(1)}, bf16[128,1024]{1,0:T(8,128)(2,1)S(1)}, u32[]{:S(2)}, u32[]{:S(2)}) collective-permute-start(bf16[128,1024]{1,0:T(8,128)(2,1)S(1)} %collective-permute-done.refs_2_), channel_id=1, source_target_pairs={{0,4},{1,3},{4,8},{5,1},{8,12},{9,5},{12,14},{13,9},{14,10},{15,13... | collective-permute-start | bytes 786440 | tf_op jit(solution)/shard_map/ppermute | solution.py:70
  20.1 7.2 %collective-permute-start.17 = (bf16[144,512]{1,0:T(8,128)(2,1)S(1)}, bf16[144,512]{1,0:T(8,128)(2,1)S(1)}, u32[]{:S(2)}, u32[]{:S(2)}) collective-permute-start(bf16[144,512]{1,0:T(8,128)(2,1)S(1)} %collective-permute-done.14.refs_7_), channel_id=1, source_target_pairs={{0,4},{1,3},{4,8},{5,1},{8,12},{9,5},{12,14},{13,9},{14,10},{15,13... | collective-permute-start | bytes 442376 | tf_op jit(solution)/shard_map/ppermute | solution.py:91
  22.9 6.0 %collective-permute-start.5 = (bf16[144,512]{1,0:T(8,128)(2,1)S(1)}, bf16[144,512]{1,0:T(8,128)(2,1)S(1)}, u32[]{:S(2)}, u32[]{:S(2)}) collective-permute-start(bf16[144,512]{1,0:T(8,128)(2,1)S(1)} %collective-permute-done.4.refs_10_), channel_id=1, source_target_pairs={{0,4},{1,3},{4,8},{5,1},{8,12},{9,5},{12,14},{13,9},{14,10},{15,13... | collective-permute-start | bytes 442376 | tf_op jit(solution)/shard_map/ppermute | solution.py:88
  24.4 7.2 %collective-permute-start.9 = (bf16[128,1024]{1,0:T(8,128)(2,1)S(1)}, bf16[128,1024]{1,0:T(8,128)(2,1)S(1)}, u32[]{:S(2)}, u32[]{:S(2)}) collective-permute-start(bf16[128,1024]{1,0:T(8,128)(2,1)S(1)} %collective-permute-done.8.refs_7_), channel_id=1, source_target_pairs={{0,4},{1,3},{4,8},{5,1},{8,12},{9,5},{12,14},{13,9},{14,10},{15,13... | collective-permute-start | bytes 786440 | tf_op jit(solution)/shard_map/ppermute | solution.py:71
  28.9 9.6 %collective-permute-start.6 = (bf16[128,1024]{1,0:T(8,128)(2,1)S(1)}, bf16[128,1024]{1,0:T(8,128)(2,1)S(1)}, u32[]{:S(2)}, u32[]{:S(2)}) collective-permute-start(bf16[128,1024]{1,0:T(8,128)(2,1)S(1)} %collective-permute-done.1.refs_6_), channel_id=1, source_target_pairs={{0,4},{1,3},{4,8},{5,1},{8,12},{9,5},{12,14},{13,9},{14,10},{15,13... | collective-permute-start | bytes 786440 | tf_op jit(solution)/shard_map/ppermute | solution.py:70
  30.5 8.4 %collective-permute-start.21 = (bf16[128,1024]{1,0:T(8,128)(2,1)S(1)}, bf16[128,1024]{1,0:T(8,128)(2,1)S(1)}, u32[]{:S(2)}, u32[]{:S(2)}) collective-permute-start(bf16[128,1024]{1,0:T(8,128)(2,1)S(1)} %copy-done.5), channel_id=1, source_target_pairs={{0,1},{1,0},{2,3},{3,2},{4,5},{5,4},{6,7},{7,6},{8,9},{9,8},{10,11... | collective-permute-start | bytes 786440 | tf_op jit(solution)/shard_map/ppermute | solution.py:75
  30.6 8.6 %collective-permute-start.22 = (bf16[128,1024]{1,0:T(8,128)(2,1)S(1)}, bf16[128,1024]{1,0:T(8,128)(2,1)S(1)}, u32[]{:S(2)}, u32[]{:S(2)}) collective-permute-start(bf16[128,1024]{1,0:T(8,128)(2,1)S(1)} %collective-permute-done.refs_2_), channel_id=1, source_target_pairs={{0,1},{1,0},{2,3},{3,2},{4,5},{5,4},{6,7},{7,6},{8,9},{9,8},{10,11... | collective-permute-start | bytes 786440 | tf_op jit(solution)/shard_map/ppermute | solution.py:77
  31.2 9.7 %collective-permute-start.23 = (bf16[128,1024]{1,0:T(8,128)(2,1)S(1)}, bf16[128,1024]{1,0:T(8,128)(2,1)S(1)}, u32[]{:S(2)}, u32[]{:S(2)}) collective-permute-start(bf16[128,1024]{1,0:T(8,128)(2,1)S(1)} %collective-permute-done.7.refs_3_), channel_id=1, source_target_pairs={{0,1},{1,0},{2,3},{3,2},{4,5},{5,4},{6,7},{7,6},{8,9},{9,8},{10,11... | collective-permute-start | bytes 786440 | tf_op jit(solution)/shard_map/ppermute | solution.py:78
  31.6 10.5 %collective-permute-start.24 = (bf16[128,1024]{1,0:T(8,128)(2,1)S(1)}, bf16[128,1024]{1,0:T(8,128)(2,1)S(1)}, u32[]{:S(2)}, u32[]{:S(2)}) collective-permute-start(bf16[128,1024]{1,0:T(8,128)(2,1)S(1)} %collective-permute-done.1.refs_6_), channel_id=1, source_target_pairs={{0,1},{1,0},{2,3},{3,2},{4,5},{5,4},{6,7},{7,6},{8,9},{9,8},{10,11... | collective-permute-start | bytes 786440 | tf_op jit(solution)/shard_map/ppermute | solution.py:77
  38.5 7.3 %collective-permute-start.25 = (bf16[128,1024]{1,0:T(8,128)(2,1)S(1)}, bf16[128,1024]{1,0:T(8,128)(2,1)S(1)}, u32[]{:S(2)}, u32[]{:S(2)}) collective-permute-start(bf16[128,1024]{1,0:T(8,128)(2,1)S(1)} %collective-permute-done.8.refs_7_), channel_id=1, source_target_pairs={{0,1},{1,0},{2,3},{3,2},{4,5},{5,4},{6,7},{7,6},{8,9},{9,8},{10,11... | collective-permute-start | bytes 786440 | tf_op jit(solution)/shard_map/ppermute | solution.py:78
  38.9 6.9 %collective-permute-start.27 = (bf16[128,1024]{1,0:T(8,128)(2,1)S(1)}, bf16[128,1024]{1,0:T(8,128)(2,1)S(1)}, u32[]{:S(2)}, u32[]{:S(2)}) collective-permute-start(bf16[128,1024]{1,0:T(8,128)(2,1)S(1)} %collective-permute-done.9.refs_11_), channel_id=1, source_target_pairs={{0,1},{1,0},{2,3},{3,2},{4,5},{5,4},{6,7},{7,6},{8,9},{9,8},{10,11... | collective-permute-start | bytes 786440 | tf_op jit(solution)/shard_map/ppermute | solution.py:78
  50.0 7.8 %collective-permute-start.35 = (bf16[128,1024]{1,0:T(8,128)(2,1)S(1)}, bf16[128,1024]{1,0:T(8,128)(2,1)S(1)}, u32[]{:S(2)}, u32[]{:S(2)}) collective-permute-start(bf16[128,1024]{1,0:T(8,128)(2,1)S(1)} %get-tuple-element.37.refs_0_), channel_id=1, source_target_pairs={{1,4},{0,3},{5,8},{4,1},{9,12},{8,5},{13,14},{12,9},{15,10},{14,13... | collective-permute-start | bytes 786440 | tf_op jit(solution)/shard_map/ppermute | solution.py:71
  50.4 8.8 %collective-permute-start.34 = (bf16[128,1024]{1,0:T(8,128)(2,1)S(1)}, bf16[128,1024]{1,0:T(8,128)(2,1)S(1)}, u32[]{:S(2)}, u32[]{:S(2)}) collective-permute-start(bf16[128,1024]{1,0:T(8,128)(2,1)S(1)} %get-tuple-element.37.refs_0_), channel_id=1, source_target_pairs={{0,4},{1,3},{4,8},{5,1},{8,12},{9,5},{12,14},{13,9},{14,10},{15,13... | collective-permute-start | bytes 786440 | tf_op jit(solution)/shard_map/ppermute | solution.py:70
  57.8 6.4 %collective-permute-start.40 = (bf16[128,1024]{1,0:T(8,128)(2,1)S(1)}, bf16[128,1024]{1,0:T(8,128)(2,1)S(1)}, u32[]{:S(2)}, u32[]{:S(2)}) collective-permute-start(bf16[128,1024]{1,0:T(8,128)(2,1)S(1)} %collective-permute-done.35.refs_1_), channel_id=1, source_target_pairs={{0,4},{1,3},{4,8},{5,1},{8,12},{9,5},{12,14},{13,9},{14,10},{15,13... | collective-permute-start | bytes 786440 | tf_op jit(solution)/shard_map/ppermute | solution.py:71
  59.2 7.8 %collective-permute-start.39 = (bf16[128,1024]{1,0:T(8,128)(2,1)S(1)}, bf16[128,1024]{1,0:T(8,128)(2,1)S(1)}, u32[]{:S(2)}, u32[]{:S(2)}) collective-permute-start(bf16[128,1024]{1,0:T(8,128)(2,1)S(1)} %collective-permute-done.34.refs_0_), channel_id=1, source_target_pairs={{0,4},{1,3},{4,8},{5,1},{8,12},{9,5},{12,14},{13,9},{14,10},{15,13... | collective-permute-start | bytes 786440 | tf_op jit(solution)/shard_map/ppermute | solution.py:70
  64.2 6.4 %collective-permute-start.45 = (bf16[128,1024]{1,0:T(8,128)(2,1)S(1)}, bf16[128,1024]{1,0:T(8,128)(2,1)S(1)}, u32[]{:S(2)}, u32[]{:S(2)}) collective-permute-start(bf16[128,1024]{1,0:T(8,128)(2,1)S(1)} %collective-permute-done.40.refs_1_), channel_id=1, source_target_pairs={{0,4},{1,3},{4,8},{5,1},{8,12},{9,5},{12,14},{13,9},{14,10},{15,13... | collective-permute-start | bytes 786440 | tf_op jit(solution)/shard_map/ppermute | solution.py:71
  67.0 6.4 %collective-permute-start.44 = (bf16[128,1024]{1,0:T(8,128)(2,1)S(1)}, bf16[128,1024]{1,0:T(8,128)(2,1)S(1)}, u32[]{:S(2)}, u32[]{:S(2)}) collective-permute-start(bf16[128,1024]{1,0:T(8,128)(2,1)S(1)} %collective-permute-done.39.refs_0_), channel_id=1, source_target_pairs={{0,4},{1,3},{4,8},{5,1},{8,12},{9,5},{12,14},{13,9},{14,10},{15,13... | collective-permute-start | bytes 786440 | tf_op jit(solution)/shard_map/ppermute | solution.py:70
  83.2 7.0 %collective-permute-start.48 = (bf16[256,1024]{1,0:T(8,128)(2,1)S(1)}, bf16[256,1024]{1,0:T(8,128)(2,1)S(1)}, u32[]{:S(2)}, u32[]{:S(2)}) collective-permute-start(bf16[256,1024]{1,0:T(8,128)(2,1)S(1)} %get-tuple-element.45), channel_id=1, source_target_pairs={{0,1},{1,0},{2,3},{3,2},{4,5},{5,4},{6,7},{7,6},{8,9},{9,8},{10,11... | collective-permute-start | bytes 1572872 | tf_op jit(solution)/shard_map/ppermute | solution.py:110
  84.5 16.6 %collective-permute-start.32 = (bf16[128,1024]{1,0:T(8,128)(2,1)S(1)}, bf16[128,1024]{1,0:T(8,128)(2,1)S(1)}, u32[]{:S(2)}, u32[]{:S(2)}) collective-permute-start(bf16[128,1024]{1,0:T(8,128)(2,1)S(1)} %get-tuple-element.37.refs_0_), channel_id=1, source_target_pairs={{0,1},{1,0},{2,3},{3,2},{4,5},{5,4},{6,7},{7,6},{8,9},{9,8},{10,11... | collective-permute-start | bytes 786440 | tf_op jit(solution)/shard_map/ppermute | solution.py:75
  85.0 6.9 %collective-permute-start.36 = (bf16[128,1024]{1,0:T(8,128)(2,1)S(1)}, bf16[128,1024]{1,0:T(8,128)(2,1)S(1)}, u32[]{:S(2)}, u32[]{:S(2)}) collective-permute-start(bf16[128,1024]{1,0:T(8,128)(2,1)S(1)} %collective-permute-done.34.refs_0_), channel_id=1, source_target_pairs={{0,1},{1,0},{2,3},{3,2},{4,5},{5,4},{6,7},{7,6},{8,9},{9,8},{10,11... | collective-permute-start | bytes 786440 | tf_op jit(solution)/shard_map/ppermute | solution.py:77
  90.2 6.4 %collective-permute-start.55 = (bf16[128,1024]{1,0:T(8,128)(2,1)S(1)}, bf16[128,1024]{1,0:T(8,128)(2,1)S(1)}, u32[]{:S(2)}, u32[]{:S(2)}) collective-permute-start(bf16[128,1024]{1,0:T(8,128)(2,1)S(1)} %add_convert_fusion.6), channel_id=1, source_target_pairs={{4,0},{3,1},{8,4},{1,5},{12,8},{5,9},{14,12},{9,13},{10,14},{13,15... | collective-permute-start | bytes 786440 | tf_op jit(solution)/shard_map/ppermute | solution.py:121
  91.8 7.6 %collective-permute-start.59 = (bf16[128,1024]{1,0:T(8,128)(2,1)S(1)}, bf16[128,1024]{1,0:T(8,128)(2,1)S(1)}, u32[]{:S(2)}, u32[]{:S(2)}) collective-permute-start(bf16[128,1024]{1,0:T(8,128)(2,1)S(1)} %add_convert_fusion.3), channel_id=1, source_target_pairs={{4,0},{3,1},{8,4},{1,5},{12,8},{5,9},{14,12},{9,13},{10,14},{13,15... | collective-permute-start | bytes 786440 | tf_op jit(solution)/shard_map/ppermute | solution.py:122
  94.9 7.3 %collective-permute-start.38 = (bf16[256,1024]{1,0:T(8,128)(2,1)S(1)}, bf16[256,1024]{1,0:T(8,128)(2,1)S(1)}, u32[]{:S(2)}, u32[]{:S(2)}) collective-permute-start(bf16[256,1024]{1,0:T(8,128)(2,1)S(1)} %get-tuple-element.41), channel_id=1, source_target_pairs={{0,1},{1,0},{2,3},{3,2},{4,5},{5,4},{6,7},{7,6},{8,9},{9,8},{10,11... | collective-permute-start | bytes 1572872 | tf_op jit(solution)/shard_map/ppermute | solution.py:110
  96.8 6.4 %collective-permute-start.56 = (bf16[128,1024]{1,0:T(8,128)(2,1)S(1)}, bf16[128,1024]{1,0:T(8,128)(2,1)S(1)}, u32[]{:S(2)}, u32[]{:S(2)}) collective-permute-start(bf16[128,1024]{1,0:T(8,128)(2,1)S(1)} %add_convert_fusion.5), channel_id=1, source_target_pairs={{4,0},{3,1},{8,4},{1,5},{12,8},{5,9},{14,12},{9,13},{10,14},{13,15... | collective-permute-start | bytes 786440 | tf_op jit(solution)/shard_map/ppermute | solution.py:121
  99.6 6.4 %collective-permute-start.60 = (bf16[128,1024]{1,0:T(8,128)(2,1)S(1)}, bf16[128,1024]{1,0:T(8,128)(2,1)S(1)}, u32[]{:S(2)}, u32[]{:S(2)}) collective-permute-start(bf16[128,1024]{1,0:T(8,128)(2,1)S(1)} %add_convert_fusion.2), channel_id=1, source_target_pairs={{4,0},{3,1},{8,4},{1,5},{12,8},{5,9},{14,12},{9,13},{10,14},{13,15... | collective-permute-start | bytes 786440 | tf_op jit(solution)/shard_map/ppermute | solution.py:122
  103.3 6.4 %collective-permute-start.57 = (bf16[128,1024]{1,0:T(8,128)(2,1)S(1)}, bf16[128,1024]{1,0:T(8,128)(2,1)S(1)}, u32[]{:S(2)}, u32[]{:S(2)}) collective-permute-start(bf16[128,1024]{1,0:T(8,128)(2,1)S(1)} %add_convert_fusion.4), channel_id=1, source_target_pairs={{4,0},{3,1},{8,4},{1,5},{12,8},{5,9},{14,12},{9,13},{10,14},{13,15... | collective-permute-start | bytes 786440 | tf_op jit(solution)/shard_map/ppermute | solution.py:121
  (53 other events, 383.1 us)
